TPU v7x, 32 devices: a whole 2x2x4 slice. The times are simulated.
32 devices in a mesh: team: 8 (over y, x, core), rep: 4 (over z).
Axes of the slice: x: 2, y: 2, z: 4, core: 2. Of those that a mesh axis runs over, the one named last changes fastest.
Arguments:
- points: bfloat16 [8192, 128], P('team'), may hold values from -3 to 3
Outputs:
- potential: float32 [8192], P('team')
- displacement: float32 [8192, 128], P('team')
All inputs are finite; a program needn't handle non-finite values.
Results may differ from a plain program's by a relative error of at most 0.0097.
The roundings to bfloat16 on the way count: a program that leaves them out, or rounds other values in their place, can miss the bound.
Values may be sent and summed in bfloat16 or wider, within the bound.
No kernel may reach another device: no remote copies, remote signals or barrier semaphores. Data moves between devices by JAX's collectives and lax.ppermute only.
A program may use at most 64 MiB of HBM per device.

v0:
```python
import jax
import jax.numpy as jnp
from jax import lax
from jax.sharding import PartitionSpec as P


def shifted(block, axis, distance):
    devices = range(lax.axis_size(axis))
    route = [((i - distance) % len(devices), i) for i in devices]
    return lax.ppermute(block, axis, route)


def square_norms(block_points):
    return jnp.sum(jnp.square(block_points.astype(jnp.float32)), axis=1)


def digit_set(offset, bit_index):
    return jnp.right_shift(offset, bit_index) % 2 == 1


def deliver_partner(block_points, offset):
    digits = lax.axis_size("rep").bit_length()
    current = block_points
    for bit_index in range(digits):
        arrived = shifted(current, "team", -(1 << bit_index))
        current = jnp.where(digit_set(offset, bit_index), arrived, current)
    return current


def deliver_mirror(block_points, offset):
    digits = lax.axis_size("rep").bit_length()
    current = block_points
    for bit_index in range(digits):
        arrived = shifted(current, "team", 1 << bit_index)
        current = jnp.where(digit_set(offset, bit_index), arrived, current)
    return current


def potential_partner(pot_one, offset):
    digits = lax.axis_size("rep").bit_length()
    current = pot_one
    for bit_index in range(digits):
        arrived = shifted(current, "team", -(1 << bit_index))
        current = jnp.where(digit_set(offset, bit_index), arrived, current)
    return current


def potential_mirror(pot_one, offset):
    digits = lax.axis_size("rep").bit_length()
    current = pot_one
    for bit_index in range(digits):
        arrived = shifted(current, "team", 1 << bit_index)
        current = jnp.where(digit_set(offset, bit_index), arrived, current)
    return current


def tile_sums(row_side, col_side, inv_eps, with_num):
    rows_x, rows_sq, rows_pot = row_side
    cols_x, cols_sq, cols_pot = col_side
    block_rows = rows_x.shape[0]
    numer_width = rows_x.shape[1] if with_num else 0
    col_count = 0
    row_block = min(block_rows, 512)
    col_block = min(block_rows, 256)
    cols_scale = jnp.exp(cols_pot * inv_eps)
    initial = (
        jnp.zeros((block_rows,), jnp.float32),
        jnp.zeros((block_rows, numer_width), jnp.float32),
        jnp.zeros((col_count,), jnp.float32),
        jnp.zeros((col_count, numer_width), jnp.float32),
    )

    def row_step(row_index, carried):
        row_total, row_numer, col_total, col_numer = carried
        row_start = row_index * row_block
        part_x = lax.dynamic_slice_in_dim(rows_x, row_start, row_block, 0)
        part_sq = lax.dynamic_slice_in_dim(rows_sq, row_start, row_block, 0)

        def col_step(col_index, inner_carried):
            block_total, block_numer, col_acc, col_num_acc = inner_carried
            col_start = col_index * col_block
            other_x = lax.dynamic_slice_in_dim(cols_x, col_start, col_block, 0)
            other_sq = lax.dynamic_slice_in_dim(cols_sq, col_start, col_block, 0)
            other_scale = lax.dynamic_slice_in_dim(cols_scale, col_start, col_block, 0)
            products = lax.dot_general(
                part_x, other_x, (((1,), (1,)), ((), ())), preferred_element_type=jnp.float32
            )
            kernel = jnp.exp(
                (products - 0.5 * part_sq[:, None] - 0.5 * other_sq[None, :]) * inv_eps
            )
            row_weight = kernel * other_scale[None, :]
            block_total = block_total + jnp.sum(row_weight, axis=1)
            if with_num:
                block_numer = block_numer + jnp.dot(
                    row_weight.astype(jnp.bfloat16), other_x, preferred_element_type=jnp.float32
                )
            return (block_total, block_numer, col_acc, col_num_acc)

        start_inner = (
            jnp.zeros((row_block,), jnp.float32),
            jnp.zeros((row_block, numer_width), jnp.float32),
            col_total,
            col_numer,
        )
        block_total, block_numer, col_total, col_numer = lax.fori_loop(
            0, block_rows // col_block, col_step, start_inner
        )
        row_total = lax.dynamic_update_slice_in_dim(row_total, block_total, row_start, 0)
        row_numer = lax.dynamic_update_slice_in_dim(row_numer, block_numer, row_start, 0)
        return (row_total, row_numer, col_total, col_numer)

    return lax.fori_loop(0, block_rows // row_block, row_step, initial)


def crossed_sums(own_side, partner_side, mirror_side, inv_eps, with_num):
    forward_part = tile_sums(own_side, partner_side, inv_eps, with_num)
    backward_part = tile_sums(own_side, mirror_side, inv_eps, with_num)
    return (forward_part[0] + backward_part[0], forward_part[1] + backward_part[1])


def neighbour_potentials(pot_one, offset, replica):
    partner_pot = potential_partner(pot_one, offset)
    mirror_pot = potential_mirror(pot_one, offset)
    mirror_pot = jnp.where(replica == 0, pot_one, mirror_pot)
    return (partner_pot, mirror_pot)


def shards(points):
    block_rows = points.shape[0]
    replicas = lax.axis_size("rep")
    team_count = lax.axis_size("team")
    replica = lax.axis_index("rep")
    offset = jnp.where(replica == 0, replicas, replica)
    own_sq = square_norms(points)
    log_count = jnp.log(jnp.float32(block_rows * team_count))
    zero_pot = jnp.zeros((block_rows,), jnp.float32)
    partner_x = deliver_partner(points, offset)
    partner_sq = square_norms(partner_x)
    mirror_far = deliver_mirror(points, offset)
    mirror_x = jnp.where(replica == 0, points, mirror_far)
    mirror_sq = square_norms(mirror_x)
    first_local, unused_numer = crossed_sums(
        (points, own_sq, zero_pot),
        (partner_x, partner_sq, zero_pot),
        (mirror_x, mirror_sq, zero_pot),
        0.25,
        False,
    )
    first_sum = lax.psum(first_local, "rep")
    pot_one = 0.5 * (zero_pot - 4.0 * (jnp.log(first_sum) - log_count))
    partner_pot, mirror_pot = neighbour_potentials(pot_one, offset, replica)
    second_local, numer_local = crossed_sums(
        (points, own_sq, pot_one),
        (partner_x, partner_sq, partner_pot),
        (mirror_x, mirror_sq, mirror_pot),
        0.5,
        True,
    )
    second, numerator = lax.psum((second_local, numer_local), "rep")
    potential = 0.5 * (pot_one - 2.0 * (jnp.log(second) - log_count))
    displacement = points.astype(jnp.float32) - numerator / second[:, None]
    return (potential, displacement)


def solution(mesh):
    return jax.shard_map(
        shards,
        mesh=mesh,
        in_specs=(P("team", None),),
        out_specs=(P("team"), P("team", None)),
        check_vma=False,
    )
```

profile of v0, /device:TPU:0, one launch (start us, length us, event | category | flops | bytes accessed | tf_op | source)
XLA Modules:
  0.0 137.2 jit_solution(6187384436440241568)
XLA Ops:
  7.2 0.5 collective-permute-start.3
  7.7 2.9 %collective-permute-start = (bf16[1024,128]{1,0:T(8,128)(2,1)}, bf16[1024,128]{1,0:T(8,128)(2,1)S(1)}, u32[]{:S(2)}, u32[]{:S(2)}) collective-permute-start(bf16[1024,128]{1,0:T(8,128)(2,1)} %param.17), channel_id=1, source_target_pairs={{4,0},{8,4},{12,8},{16,12},{20,16},{24,20},{28,24},{0,28},{5,1},{9... | collective-permute-start | bytes 786440 | tf_op jit(solution)/shard_map/ppermute | solution.py:10
  10.7 4.3 %collective-permute-done.3 = bf16[1024,128]{1,0:T(8,128)(2,1)S(1)} collective-permute-done((bf16[1024,128]{1,0:T(8,128)(2,1)}, bf16[1024,128]{1,0:T(8,128)(2,1)S(1)}, u32[]{:S(2)}, u32[]{:S(2)}) %collective-permute-start.3) | collective-permute-done | bytes 262176 | tf_op jit(solution)/shard_map/ppermute | solution.py:10
  15.0 1.6 %collective-permute-done = bf16[1024,128]{1,0:T(8,128)(2,1)S(1)} collective-permute-done((bf16[1024,128]{1,0:T(8,128)(2,1)}, bf16[1024,128]{1,0:T(8,128)(2,1)S(1)}, u32[]{:S(2)}, u32[]{:S(2)}) %collective-permute-start) | collective-permute-done | bytes 262176 | tf_op jit(solution)/shard_map/ppermute | solution.py:10
  16.6 1.0 broadcast_select_fusion
  17.6 1.5 %collective-permute-start.4 = (bf16[1024,128]{1,0:T(8,128)(2,1)S(1)}, bf16[1024,128]{1,0:T(8,128)(2,1)S(1)}, u32[]{:S(2)}, u32[]{:S(2)}) collective-permute-start(bf16[1024,128]{1,0:T(8,128)(2,1)S(1)} %get-tuple-element.1293), channel_id=1, source_target_pairs={{24,0},{28,4},{0,8},{4,12},{8,16},{12,20},{16,24},{20,28},{25,1},{... | collective-permute-start | bytes 786440 | tf_op jit(solution)/shard_map/ppermute | solution.py:10
  19.2 1.4 %collective-permute-start.1 = (bf16[1024,128]{1,0:T(8,128)(2,1)S(1)}, bf16[1024,128]{1,0:T(8,128)(2,1)S(1)}, u32[]{:S(2)}, u32[]{:S(2)}) collective-permute-start(bf16[1024,128]{1,0:T(8,128)(2,1)S(1)} %get-tuple-element.1294), channel_id=1, source_target_pairs={{8,0},{12,4},{16,8},{20,12},{24,16},{28,20},{0,24},{4,28},{9,1},{1... | collective-permute-start | bytes 786440 | tf_op jit(solution)/shard_map/ppermute | solution.py:10
  20.6 6.5 %collective-permute-done.4 = bf16[1024,128]{1,0:T(8,128)(2,1)S(1)} collective-permute-done((bf16[1024,128]{1,0:T(8,128)(2,1)S(1)}, bf16[1024,128]{1,0:T(8,128)(2,1)S(1)}, u32[]{:S(2)}, u32[]{:S(2)}) %collective-permute-start.4) | collective-permute-done | bytes 262176 | tf_op jit(solution)/shard_map/ppermute | solution.py:10
  27.1 3.3 %collective-permute-start.5 = (bf16[1024,128]{1,0:T(8,128)(2,1)S(1)}, bf16[1024,128]{1,0:T(8,128)(2,1)S(1)}, u32[]{:S(2)}, u32[]{:S(2)}) collective-permute-start(bf16[1024,128]{1,0:T(8,128)(2,1)S(1)} %broadcast_select_fusion.2), channel_id=1, source_target_pairs={{16,0},{20,4},{24,8},{28,12},{0,16},{4,20},{8,24},{12,28},{17,1},{... | collective-permute-start | bytes 786440 | tf_op jit(solution)/shard_map/ppermute | solution.py:10
  30.4 2.5 %collective-permute-done.1 = bf16[1024,128]{1,0:T(8,128)(2,1)S(1)} collective-permute-done((bf16[1024,128]{1,0:T(8,128)(2,1)S(1)}, bf16[1024,128]{1,0:T(8,128)(2,1)S(1)}, u32[]{:S(2)}, u32[]{:S(2)}) %collective-permute-start.1) | collective-permute-done | bytes 262176 | tf_op jit(solution)/shard_map/ppermute | solution.py:10
  33.0 0.4 collective-permute-start.2
  33.4 4.2 %collective-permute-done.5 = bf16[1024,128]{1,0:T(8,128)(2,1)S(1)} collective-permute-done((bf16[1024,128]{1,0:T(8,128)(2,1)S(1)}, bf16[1024,128]{1,0:T(8,128)(2,1)S(1)}, u32[]{:S(2)}, u32[]{:S(2)}) %collective-permute-start.5) | collective-permute-done | bytes 262176 | tf_op jit(solution)/shard_map/ppermute | solution.py:10
  37.6 0.3 multiply_reduce_fusion
  38.0 3.9 %while.175 = (s32[]{:T(128)}, f32[1024]{0:T(1024)S(1)}, bf16[1024,128]{1,0:T(8,128)(2,1)S(1)}, f32[1024]{0:T(1024)S(1)}, bf16[1024,128]{1,0:T(8,128)(2,1)S(1)}, ...) while((s32[]{:T(128)}, f32[1024]{0:T(1024)S(1)}, ...), condition=%wide.region_12.13_spmd, body=%wide.region_8.12_spmd.sunk | while | flops 34080008 | bytes 484804 | solution.py:112
  38.1 1.6 %while.181 = (s32[]{:T(128)}, f32[512]{0:T(512)S(1)}, bf16[1024,128]{1,0:T(8,128)(2,1)S(1)}, bf16[512,128]{1,0:T(8,128)(2,1)S(1)}, f32[512]{0:T(512)S(1)}, /*ind...) while((s32[]{:T(128)}, f32[512]{0:T(512)S(1)}, ...), condition=%wide.region_11.11_spmd.clone, body=%wide.region_9.10_spmd.clone.sunk | while | flops 34080004 | bytes 214189 | solution.py:105
  40.0 1.6 %while.181 = (s32[]{:T(128)}, f32[512]{0:T(512)S(1)}, bf16[1024,128]{1,0:T(8,128)(2,1)S(1)}, bf16[512,128]{1,0:T(8,128)(2,1)S(1)}, f32[512]{0:T(512)S(1)}, /*ind...) while((s32[]{:T(128)}, f32[512]{0:T(512)S(1)}, ...), condition=%wide.region_11.11_spmd.clone, body=%wide.region_9.10_spmd.clone.sunk | while | flops 34080004 | bytes 214189 | solution.py:105
  42.4 3.9 %while.173 = (s32[]{:T(128)}, f32[1024]{0:T(1024)S(1)}, bf16[1024,128]{1,0:T(8,128)(2,1)S(1)}, f32[1024]{0:T(1024)S(1)}, bf16[1024,128]{1,0:T(8,128)(2,1)S(1)}, ...) while((s32[]{:T(128)}, f32[1024]{0:T(1024)S(1)}, ...), condition=%wide.region_6.7_spmd, body=%wide.region_2.6_spmd.sunk | while | flops 34080008 | bytes 484804 | solution.py:112
  42.5 1.6 %while.180 = (s32[]{:T(128)}, f32[512]{0:T(512)S(1)}, bf16[1024,128]{1,0:T(8,128)(2,1)S(1)}, bf16[512,128]{1,0:T(8,128)(2,1)S(1)}, f32[512]{0:T(512)S(1)}, /*ind...) while((s32[]{:T(128)}, f32[512]{0:T(512)S(1)}, ...), condition=%wide.region_5.5_spmd.clone, body=%wide.region_3.4_spmd.clone.sunk | while | flops 34080004 | bytes 214189 | solution.py:105
  44.5 1.6 %while.180 = (s32[]{:T(128)}, f32[512]{0:T(512)S(1)}, bf16[1024,128]{1,0:T(8,128)(2,1)S(1)}, bf16[512,128]{1,0:T(8,128)(2,1)S(1)}, f32[512]{0:T(512)S(1)}, /*ind...) while((s32[]{:T(128)}, f32[512]{0:T(512)S(1)}, ...), condition=%wide.region_5.5_spmd.clone, body=%wide.region_3.4_spmd.clone.sunk | while | flops 34080004 | bytes 214189 | solution.py:105
  46.3 12.0 %psum.21 = f32[1024]{0:T(1024)S(1)} all-reduce(f32[1024]{0:T(1024)S(1)} %add.285), channel_id=1, replica_groups=mesh['team'=8,'rep'=4] {'rep'}, use_global_device_ids=true, to_apply=%region_13.14 | all-reduce | flops 1024 | bytes 8192 | tf_op jit(solution)/shard_map/psum | solution.py:149
  58.4 3.9 %collective-permute-done.9 = f32[1024]{0:T(1024)S(1)} collective-permute-done((f32[1024]{0:T(1024)S(1)}, f32[1024]{0:T(1024)S(1)}, u32[]{:S(2)}, u32[]{:S(2)}) %collective-permute-start.9) | collective-permute-done | bytes 4128 | tf_op jit(solution)/shard_map/ppermute | solution.py:10
  62.3 2.6 %collective-permute-start.10 = (f32[1024]{0:T(1024)S(1)}, f32[1024]{0:T(1024)S(1)}, u32[]{:S(2)}, u32[]{:S(2)}) collective-permute-start(f32[1024]{0:T(1024)S(1)} %broadcast_select_fusion.5), channel_id=1, source_target_pairs={{24,0},{28,4},{0,8},{4,12},{8,16},{12,20},{16,24},{20,28},{25,1},{... | collective-permute-start | bytes 12296 | tf_op jit(solution)/shard_map/ppermute | solution.py:10
  65.0 1.9 %collective-permute-done.10 = f32[1024]{0:T(1024)S(1)} collective-permute-done((f32[1024]{0:T(1024)S(1)}, f32[1024]{0:T(1024)S(1)}, u32[]{:S(2)}, u32[]{:S(2)}) %collective-permute-start.10) | collective-permute-done | bytes 4128 | tf_op jit(solution)/shard_map/ppermute | solution.py:10
  66.9 1.0 collective-permute-start.11
  68.0 2.6 %collective-permute-done.11 = f32[1024]{0:T(1024)S(1)} collective-permute-done((f32[1024]{0:T(1024)S(1)}, f32[1024]{0:T(1024)S(1)}, u32[]{:S(2)}, u32[]{:S(2)}) %collective-permute-start.11) | collective-permute-done | bytes 4128 | tf_op jit(solution)/shard_map/ppermute | solution.py:10
  70.5 2.1 %collective-permute-start.7 = (f32[1024]{0:T(1024)S(1)}, f32[1024]{0:T(1024)S(1)}, u32[]{:S(2)}, u32[]{:S(2)}) collective-permute-start(f32[1024]{0:T(1024)S(1)} %get-tuple-element.1296), channel_id=1, source_target_pairs={{8,0},{12,4},{16,8},{20,12},{24,16},{28,20},{0,24},{4,28},{9,1},{1... | collective-permute-start | bytes 12296 | tf_op jit(solution)/shard_map/ppermute | solution.py:10
  72.6 1.6 %collective-permute-done.7 = f32[1024]{0:T(1024)S(1)} collective-permute-done((f32[1024]{0:T(1024)S(1)}, f32[1024]{0:T(1024)S(1)}, u32[]{:S(2)}, u32[]{:S(2)}) %collective-permute-start.7) | collective-permute-done | bytes 4128 | tf_op jit(solution)/shard_map/ppermute | solution.py:10
  74.2 1.0 collective-permute-start.8
  75.3 7.4 %while.179 = (s32[]{:T(128)}, f32[1024]{0:T(1024)S(1)}, f32[1024,128]{1,0:T(8,128)S(1)}, bf16[1024,128]{1,0:T(8,128)(2,1)S(1)}, f32[1024]{0:T(1024)S(1)}, /*inde...) while((s32[]{:T(128)}, f32[1024]{0:T(1024)S(1)}, ...), condition=%wide.region_23.24_spmd, body=%wide.region_19.23_spmd.sunk | while | flops 68027656 | bytes 2126337 | solution.py:112
  75.4 3.3 %while.183 = (s32[]{:T(128)}, f32[512]{0:T(512)S(1)}, f32[512,128]{1,0:T(8,128)S(1)}, bf16[1024,128]{1,0:T(8,128)(2,1)S(1)}, bf16[512,128]{1,0:T(8,128)(2,1)S(1)...) while((s32[]{:T(128)}, f32[512]{0:T(512)S(1)}, ...), condition=%wide.region_22.22_spmd.clone, body=%wide.region_20.21_spmd.clone.sunk | while | flops 68027648 | bytes 1331398 | solution.py:105
  75.6 0.3 fusion.56
  75.9 0.3 convolution_add_fusion.4
  76.7 0.3 convolution_add_fusion.4
  77.2 0.3 fusion.56
  77.6 0.3 convolution_add_fusion.4
  78.1 0.3 fusion.56
  78.4 0.3 convolution_add_fusion.4
  79.1 3.3 %while.183 = (s32[]{:T(128)}, f32[512]{0:T(512)S(1)}, f32[512,128]{1,0:T(8,128)S(1)}, bf16[1024,128]{1,0:T(8,128)(2,1)S(1)}, bf16[512,128]{1,0:T(8,128)(2,1)S(1)...) while((s32[]{:T(128)}, f32[512]{0:T(512)S(1)}, ...), condition=%wide.region_22.22_spmd.clone, body=%wide.region_20.21_spmd.clone.sunk | while | flops 68027648 | bytes 1331398 | solution.py:105
  79.3 0.3 fusion.56
  79.6 0.3 convolution_add_fusion.4
  80.1 0.3 fusion.56
  80.4 0.3 convolution_add_fusion.4
  80.9 0.3 fusion.56
  81.3 0.3 convolution_add_fusion.4
  82.1 0.3 convolution_add_fusion.4
  82.8 7.5 %while.177 = (s32[]{:T(128)}, f32[1024]{0:T(1024)S(1)}, f32[1024,128]{1,0:T(8,128)S(1)}, bf16[1024,128]{1,0:T(8,128)(2,1)S(1)}, f32[1024]{0:T(1024)S(1)}, /*inde...) while((s32[]{:T(128)}, f32[1024]{0:T(1024)S(1)}, ...), condition=%wide.region_18.19_spmd, body=%wide.region_14.18_spmd.sunk | while | flops 68027656 | bytes 2126337 | solution.py:112
  82.9 3.3 %while.182 = (s32[]{:T(128)}, f32[512]{0:T(512)S(1)}, f32[512,128]{1,0:T(8,128)S(1)}, bf16[1024,128]{1,0:T(8,128)(2,1)S(1)}, bf16[512,128]{1,0:T(8,128)(2,1)S(1)...) while((s32[]{:T(128)}, f32[512]{0:T(512)S(1)}, ...), condition=%wide.region_17.17_spmd.clone, body=%wide.region_15.16_spmd.clone.sunk | while | flops 68027648 | bytes 1331398 | solution.py:105
  83.4 0.3 convolution_add_fusion.5
  84.2 0.3 convolution_add_fusion.5
  85.1 0.3 convolution_add_fusion.5
  85.9 0.3 convolution_add_fusion.5
  86.6 3.3 %while.182 = (s32[]{:T(128)}, f32[512]{0:T(512)S(1)}, f32[512,128]{1,0:T(8,128)S(1)}, bf16[1024,128]{1,0:T(8,128)(2,1)S(1)}, bf16[512,128]{1,0:T(8,128)(2,1)S(1)...) while((s32[]{:T(128)}, f32[512]{0:T(512)S(1)}, ...), condition=%wide.region_17.17_spmd.clone, body=%wide.region_15.16_spmd.clone.sunk | while | flops 68027648 | bytes 1331398 | solution.py:105
  86.8 0.3 fusion.60
  87.1 0.3 convolution_add_fusion.5
  87.6 0.3 fusion.60
  88.0 0.3 convolution_add_fusion.5
  88.5 0.3 fusion.60
  88.8 0.3 convolution_add_fusion.5
  89.6 0.3 convolution_add_fusion.5
  90.3 0.8 add.287
  91.1 8.4 %psum.22 = f32[1024]{0:T(1024)S(1)} all-reduce(f32[1024]{0:T(1024)S(1)} %add.286), channel_id=1, replica_groups=mesh['team'=8,'rep'=4] {'rep'}, use_global_device_ids=true, to_apply=%region_24.25 | all-reduce | flops 1024 | bytes 8192 | tf_op jit(solution)/shard_map/psum | solution.py:159
  99.5 0.6 subtract_multiply_fusion
  100.2 28.1 %all-reduce.2.cloned.1.call-done = f32[1024,128]{1,0:T(8,128)} async-done(((f32[1024,128]{1,0:T(8,128)}), f32[1024,128]{1,0:T(8,128)}) %all-reduce.2.cloned.1.call-update) | async-done | bytes 524304 | tf_op jit(solution)/shard_map/psum | solution.py:159
  128.3 2.0 %convert_subtract_fusion = f32[1024,128]{1,0:T(8,128)} fusion(bf16[1024,128]{1,0:T(8,128)(2,1)S(1)} %get-tuple-element.2043, f32[1024,128]{1,0:T(8,128)} %all-reduce.2.cloned.1.call-done, f32[1024]{0:T(1024)S(1)} %psum.22), kind=kLoop, calls=%fused_computation.54 | loop fusion | flops 393216 | bytes 1314816 | tf_op jit(solution)/shard_map/sub | solution.py:161
  (201 shorter events, 14.5 us)
Async XLA Ops:
  7.2 121.1 %all-reduce.2.cloned.1.call-start = ((), (), s32[]{:S(2)}) async-start(), calls=%async_computation | async-start | bytes 1048576 | tf_op jit(solution)/shard_map/psum | solution.py:159
  7.2 7.8 %collective-permute-start.3 = (bf16[1024,128]{1,0:T(8,128)(2,1)}, bf16[1024,128]{1,0:T(8,128)(2,1)S(1)}, u32[]{:S(2)}, u32[]{:S(2)}) collective-permute-start(bf16[1024,128]{1,0:T(8,128)(2,1)} %param.17), channel_id=1, source_target_pairs={{28,0},{0,4},{4,8},{8,12},{12,16},{16,20},{20,24},{24,28},{29,1},{... | collective-permute-start | bytes 786440 | tf_op jit(solution)/shard_map/ppermute | solution.py:10
  7.7 8.9 %collective-permute-start = (bf16[1024,128]{1,0:T(8,128)(2,1)}, bf16[1024,128]{1,0:T(8,128)(2,1)S(1)}, u32[]{:S(2)}, u32[]{:S(2)}) collective-permute-start(bf16[1024,128]{1,0:T(8,128)(2,1)} %param.17), channel_id=1, source_target_pairs={{4,0},{8,4},{12,8},{16,12},{20,16},{24,20},{28,24},{0,28},{5,1},{9... | collective-permute-start | bytes 786440 | tf_op jit(solution)/shard_map/ppermute | solution.py:10
  17.6 9.5 %collective-permute-start.4 = (bf16[1024,128]{1,0:T(8,128)(2,1)S(1)}, bf16[1024,128]{1,0:T(8,128)(2,1)S(1)}, u32[]{:S(2)}, u32[]{:S(2)}) collective-permute-start(bf16[1024,128]{1,0:T(8,128)(2,1)S(1)} %get-tuple-element.1293), channel_id=1, source_target_pairs={{24,0},{28,4},{0,8},{4,12},{8,16},{12,20},{16,24},{20,28},{25,1},{... | collective-permute-start | bytes 786440 | tf_op jit(solution)/shard_map/ppermute | solution.py:10
  19.2 13.8 %collective-permute-start.1 = (bf16[1024,128]{1,0:T(8,128)(2,1)S(1)}, bf16[1024,128]{1,0:T(8,128)(2,1)S(1)}, u32[]{:S(2)}, u32[]{:S(2)}) collective-permute-start(bf16[1024,128]{1,0:T(8,128)(2,1)S(1)} %get-tuple-element.1294), channel_id=1, source_target_pairs={{8,0},{12,4},{16,8},{20,12},{24,16},{28,20},{0,24},{4,28},{9,1},{1... | collective-permute-start | bytes 786440 | tf_op jit(solution)/shard_map/ppermute | solution.py:10
  27.1 10.4 %collective-permute-start.5 = (bf16[1024,128]{1,0:T(8,128)(2,1)S(1)}, bf16[1024,128]{1,0:T(8,128)(2,1)S(1)}, u32[]{:S(2)}, u32[]{:S(2)}) collective-permute-start(bf16[1024,128]{1,0:T(8,128)(2,1)S(1)} %broadcast_select_fusion.2), channel_id=1, source_target_pairs={{16,0},{20,4},{24,8},{28,12},{0,16},{4,20},{8,24},{12,28},{17,1},{... | collective-permute-start | bytes 786440 | tf_op jit(solution)/shard_map/ppermute | solution.py:10
  30.4 7.2 %copy-start = (bf16[1024,128]{1,0:T(8,128)(2,1)S(1)}, bf16[1024,128]{1,0:T(8,128)(2,1)}, u32[]{:S(2)}) copy-start(bf16[1024,128]{1,0:T(8,128)(2,1)} %param.17) | copy-start | bytes 786436
  33.0 9.2 %collective-permute-start.2 = (bf16[1024,128]{1,0:T(8,128)(2,1)S(1)}, bf16[1024,128]{1,0:T(8,128)(2,1)S(1)}, u32[]{:S(2)}, u32[]{:S(2)}) collective-permute-start(bf16[1024,128]{1,0:T(8,128)(2,1)S(1)} %broadcast_select_fusion.3), channel_id=1, source_target_pairs={{16,0},{20,4},{24,8},{28,12},{0,16},{4,20},{8,24},{12,28},{17,1},{... | collective-permute-start | bytes 786440 | tf_op jit(solution)/shard_map/ppermute | solution.py:10
  58.3 4.0 %collective-permute-start.9 = (f32[1024]{0:T(1024)S(1)}, f32[1024]{0:T(1024)S(1)}, u32[]{:S(2)}, u32[]{:S(2)}) collective-permute-start(f32[1024]{0:T(1024)S(1)} %subtract_multiply_fusion.1), channel_id=1, source_target_pairs={{28,0},{0,4},{4,8},{8,12},{12,16},{16,20},{20,24},{24,28},{29,1},{... | collective-permute-start | bytes 12296 | tf_op jit(solution)/shard_map/ppermute | solution.py:10
  62.3 4.6 %collective-permute-start.10 = (f32[1024]{0:T(1024)S(1)}, f32[1024]{0:T(1024)S(1)}, u32[]{:S(2)}, u32[]{:S(2)}) collective-permute-start(f32[1024]{0:T(1024)S(1)} %broadcast_select_fusion.5), channel_id=1, source_target_pairs={{24,0},{28,4},{0,8},{4,12},{8,16},{12,20},{16,24},{20,28},{25,1},{... | collective-permute-start | bytes 12296 | tf_op jit(solution)/shard_map/ppermute | solution.py:10
  64.9 3.1 %collective-permute-start.6 = (f32[1024]{0:T(1024)S(1)}, f32[1024]{0:T(1024)S(1)}, u32[]{:S(2)}, u32[]{:S(2)}) collective-permute-start(f32[1024]{0:T(1024)S(1)} %subtract_multiply_fusion.1), channel_id=1, source_target_pairs={{4,0},{8,4},{12,8},{16,12},{20,16},{24,20},{28,24},{0,28},{5,1},{9... | collective-permute-start | bytes 12296 | tf_op jit(solution)/shard_map/ppermute | solution.py:10
  66.9 3.6 %collective-permute-start.11 = (f32[1024]{0:T(1024)S(1)}, f32[1024]{0:T(1024)S(1)}, u32[]{:S(2)}, u32[]{:S(2)}) collective-permute-start(f32[1024]{0:T(1024)S(1)} %broadcast_select_fusion.7), channel_id=1, source_target_pairs={{16,0},{20,4},{24,8},{28,12},{0,16},{4,20},{8,24},{12,28},{17,1},{... | collective-permute-start | bytes 12296 | tf_op jit(solution)/shard_map/ppermute | solution.py:10
  70.5 3.7 %collective-permute-start.7 = (f32[1024]{0:T(1024)S(1)}, f32[1024]{0:T(1024)S(1)}, u32[]{:S(2)}, u32[]{:S(2)}) collective-permute-start(f32[1024]{0:T(1024)S(1)} %get-tuple-element.1296), channel_id=1, source_target_pairs={{8,0},{12,4},{16,8},{20,12},{24,16},{28,20},{0,24},{4,28},{9,1},{1... | collective-permute-start | bytes 12296 | tf_op jit(solution)/shard_map/ppermute | solution.py:10
  74.2 8.5 %collective-permute-start.8 = (f32[1024]{0:T(1024)S(1)}, f32[1024]{0:T(1024)S(1)}, u32[]{:S(2)}, u32[]{:S(2)}) collective-permute-start(f32[1024]{0:T(1024)S(1)} %broadcast_select_fusion.8), channel_id=1, source_target_pairs={{16,0},{20,4},{24,8},{28,12},{0,16},{4,20},{8,24},{12,28},{17,1},{... | collective-permute-start | bytes 12296 | tf_op jit(solution)/shard_map/ppermute | solution.py:10
Sparse Core Ops, SparseCore 0:
  91.3 36.9 all-reduce.1
where the time goes:
time: 137 us
  waiting for transfers between devices  57.6 us (42%)
  blocking collectives  20.4 us (15%)
  starting transfers between devices  17 us (12%)
  matrix products  14.6 us (11%)
  between operations  14.1 us (10%)
  other arithmetic  8.1 us (6%)
  local copies, waits for them, and re-layouts  4.08 us (3%)
    ppermute x12, waiting for transfers between devices, shifted(): return lax.ppermute(block, axis, route)  29.5 us
    psum x1, waiting for transfers between devices, shards(): second, numerator = lax.psum((second_local, numer_local), 'rep')  28.1 us
    ppermute x12, starting transfers between devices, shifted(): return lax.ppermute(block, axis, route)  17 us
    psum x1, blocking collectives, shards(): first_sum = lax.psum(first_local, 'rep')  12 us
    dot_general x32, matrix products, col_step(): lax.dot_general(part_x, other_x, (((1,), (1,)), ((), ())), preferred_elem...  9.5 us
    psum x1, blocking collectives, shards(): second, numerator = lax.psum((second_local, numer_local), 'rep')  8.4 us
    dot_general x16, matrix products, col_step(): jnp.dot(row_weight.astype(jnp.bfloat16), other_x, preferred_element_type=...  5.07 us
  transfers between devices with their start and end apart: 13, of which 11 were waited for; matrix products, arithmetic and copies ran while one was open for 9% of the time, Pallas kernels for 0%

commit v1 on v0

--- a/solution.py
+++ b/solution.py
@@ -1,7 +1,247 @@
+import functools
 import jax
 import jax.numpy as jnp
 from jax import lax
+from jax.experimental import pallas as pl
+from jax.experimental.pallas import tpu as pltpu
 from jax.sharding import PartitionSpec as P
+
+F32 = jnp.float32
+BF16 = jnp.bfloat16
+NT = (((1,), (1,)), ((), ()))
+IN_VMEM = pl.BlockSpec(memory_space=pltpu.VMEM)
+IN_HBM = pl.BlockSpec(memory_space=pl.ANY)
+PARAMS = pltpu.CompilerParams(vmem_limit_bytes=8 << 20)
+
+
+def kept(array):
+    return pltpu.with_memory_space_constraint(array, pltpu.VMEM)
+
+
+def swapped(array, mask):
+    size = lax.axis_size("team")
+    return lax.ppermute(array, "team", [(i, i ^ mask) for i in range(size)])
+
+
+def norm_pieces(x):
+    wide = x.astype(F32)
+    value = jnp.sum(wide * wide, axis=1, keepdims=True) * -0.125
+    high = value.astype(BF16).astype(F32)
+    rest = value - high
+    middle = rest.astype(BF16).astype(F32)
+    return high, middle, rest - middle
+
+
+def norm_lanes(x, first):
+    high, middle, low = norm_pieces(x)
+    lane = lax.broadcasted_iota(jnp.int32, x.shape, 1)
+    out = jnp.where(lane < 6, 1.0, 0.0)
+    out = jnp.where(lane == first, high, out)
+    out = jnp.where(lane == first + 1, middle, out)
+    out = jnp.where(lane == first + 2, low, out)
+    return out.astype(BF16)
+
+
+def row_kernel(x_ref, rows_ref):
+    x = x_ref[...]
+    width = x.shape[1]
+    rows_ref[:, :width] = x * jnp.asarray(0.25, BF16)
+    rows_ref[:, width:] = norm_lanes(x, 3)
+
+
+def first_tile(rows_ref, x_ref, e_ref, cols, row_block, before, after):
+    n, width = x_ref.shape
+    cols[:, :width] = x_ref[...]
+    cols[:, width:] = norm_lanes(x_ref[...], 0)
+    col_block = min(n, 256)
+    for r in range(0, n, row_block):
+        rows = slice(r, r + row_block)
+        left = rows_ref[rows, :]
+        total = before(rows)
+        for c in range(0, n, col_block):
+            part = slice(c, c + col_block)
+            k = jnp.exp(lax.dot_general(left, cols[part, :], NT, preferred_element_type=F32))
+            for l in range(0, col_block, 128):
+                total = total + k[:, l : l + 128]
+            e_ref[rows, part] = k * k
+        after(rows, total)
+
+
+def first_kernel(count, start, *refs):
+    rows_ref, refs = refs[0], refs[1:]
+    x_refs, refs = refs[:count], refs[count:]
+    if start:
+        acc_in = None
+    else:
+        acc_in, refs = refs[0], refs[1:]
+    e_refs, refs = refs[:count], refs[count:]
+    acc_ref, cols = refs
+    row_block = min(256, rows_ref.shape[0])
+    for j in range(count):
+        if j:
+            before = lambda rows: acc_ref[rows, :]
+        elif start:
+            before = lambda rows: jnp.zeros((row_block, 128), F32)
+        else:
+            before = lambda rows: acc_in[rows, :]
+
+        def after(rows, total):
+            acc_ref[rows, :] = total
+
+        first_tile(rows_ref, x_refs[j], e_refs[j], cols, row_block, before, after)
+
+
+def across(column):
+    n = column.shape[0]
+    wide = jnp.broadcast_to(column, (n, 128))
+    row = lax.broadcasted_iota(jnp.int32, (n, 128), 0) % 128
+    lane = lax.broadcasted_iota(jnp.int32, (n, 128), 1)
+    return jnp.sum(jnp.where(row == lane, wide, 0.0).reshape(n // 128, 128, 128), axis=1)
+
+
+def sums_kernel(acc_ref, sums_ref):
+    sums_ref[...] = across(jnp.sum(acc_ref[...], axis=1, keepdims=True))
+
+
+def pack_kernel(own_ref, mate_ref, both_ref):
+    g = own_ref.shape[0]
+    both_ref[:g, :] = own_ref[...]
+    both_ref[g:, :] = mate_ref[...]
+
+
+def weighted_tile(rows, e_ref, scale, x_ref, total, numerator):
+    n = x_ref.shape[0]
+    col_block = min(n, 256)
+    for c in range(0, n, col_block):
+        weights = []
+        for l in range(c, c + col_block, 128):
+            w = e_ref[rows, l : l + 128] * scale[l // 128 : l // 128 + 1, :]
+            total = total + w
+            weights.append(w.astype(BF16))
+        weight = weights[0] if len(weights) == 1 else jnp.concatenate(weights, axis=1)
+        numerator = numerator + jnp.dot(weight, x_ref[c : c + col_block, :], preferred_element_type=F32)
+    return total, numerator
+
+
+def second_kernel(points, count, *refs):
+    e_refs, refs = refs[:count], refs[count:]
+    s_refs, refs = refs[: count // 2], refs[count // 2 :]
+    x_refs, refs = refs[:count], refs[count:]
+    num_ref, acc_ref = refs
+    n = x_refs[0].shape[0]
+    groups = n // 128
+    row_block = min(128, n)
+    scales = [float(points) / s_refs[j // 2][(j % 2) * groups : (j % 2 + 1) * groups, :] for j in range(count)]
+    for r in range(0, n, row_block):
+        rows = slice(r, r + row_block)
+        total = jnp.zeros((row_block, 128), F32)
+        numerator = jnp.zeros((row_block, x_refs[0].shape[1]), F32)
+        for j in range(count):
+            total, numerator = weighted_tile(rows, e_refs[j], scales[j], x_refs[j], total, numerator)
+        acc_ref[rows, :] = total
+        num_ref[rows, :] = numerator
+
+
+def last_kernel(points, count, *refs):
+    e_refs, refs = refs[:count], refs[count:]
+    s_refs, refs = refs[: count // 2], refs[count // 2 :]
+    x_refs, refs = refs[:count], refs[count:]
+    num_in, acc_in, own_ref, sums_ref, pot_hbm, out_hbm, pot_ref, out_ref, sems = refs
+    n = own_ref.shape[0]
+    groups = n // 128
+    row_block = min(128, n)
+    log_count = jnp.log(jnp.float32(points))
+    scales = [float(points) / s_refs[j // 2][(j % 2) * groups : (j % 2 + 1) * groups, :] for j in range(count)]
+    copies = []
+    seconds = []
+    for i, r in enumerate(range(0, n, row_block)):
+        rows = slice(r, r + row_block)
+        total, numerator = acc_in[rows, :], num_in[rows, :]
+        for j in range(count):
+            total, numerator = weighted_tile(rows, e_refs[j], scales[j], x_refs[j], total, numerator)
+        second = jnp.sum(total, axis=1, keepdims=True)
+        seconds.append(across(second))
+        out_ref[rows, :] = own_ref[rows, :].astype(F32) - numerator / second
+        copies.append(pltpu.make_async_copy(out_ref.at[rows, :], out_hbm.at[rows, :], sems.at[i]))
+        copies[-1].start()
+    second = jnp.concatenate(seconds, axis=0)
+    pot_one = -2.0 * (jnp.log(sums_ref[...]) - log_count)
+    pot_ref[...] = 0.5 * (pot_one - 2.0 * (jnp.log(second) - log_count))
+    copies.append(pltpu.make_async_copy(pot_ref, pot_hbm, sems.at[len(copies)]))
+    copies[-1].start()
+    for copy in copies:
+        copy.wait()
+
+
+def shards(points):
+    n, width = points.shape
+    team = lax.axis_size("team")
+    total_points = n * team
+    groups = n // 128
+
+    def tile(shape, dtype=F32):
+        return pltpu.VMEM(shape, dtype)
+
+    def call(kernel, out_shape, args, scratch=(), out_specs=None, name=None):
+        single = not isinstance(out_shape, tuple)
+        specs = out_specs or (IN_VMEM if single else tuple(IN_VMEM for _ in out_shape))
+        return pl.pallas_call(
+            kernel,
+            out_shape=out_shape,
+            in_specs=[IN_VMEM] * len(args),
+            out_specs=specs,
+            scratch_shapes=list(scratch),
+            compiler_params=PARAMS,
+            name=name,
+        )(*[kept(a) for a in args])
+
+    masks = list(range(2, team, 2))
+    mate = swapped(points, 1)
+    far = [swapped(points, m) for m in masks]
+    pairs = [(points, mate)] + [(f, swapped(f, 1)) for f in far]
+
+    rows = call(row_kernel, tile((n, 2 * width), BF16), [points], name="rows")
+    tiles = []
+    acc = None
+    for pair in pairs:
+        for x in pair:
+            args = [rows, x] + ([] if acc is None else [acc])
+            e, acc = call(
+                functools.partial(first_kernel, 1, acc is None),
+                (tile((n, n)), tile((n, 128))),
+                args,
+                scratch=[pltpu.VMEM((n, 2 * width), BF16)],
+                name="first",
+            )
+            tiles.append(e)
+    sums = call(sums_kernel, tile((groups, 128)), [acc], name="sums")
+    mate_sums = swapped(sums, 1)
+    both = call(pack_kernel, tile((2 * groups, 128)), [sums, mate_sums], name="pack")
+    packs = [both] + [swapped(both, m) for m in masks]
+
+    flat = [x for pair in pairs for x in pair]
+    split = 4
+    numerator, second = call(
+        functools.partial(second_kernel, total_points, split),
+        (tile((n, width)), tile((n, 128))),
+        tiles[:split] + packs[: split // 2] + flat[:split],
+        name="second",
+    )
+    count = len(flat) - split
+    chunks = n // min(128, n)
+    potential, displacement = call(
+        functools.partial(last_kernel, total_points, count),
+        (jax.ShapeDtypeStruct((groups, 128), F32), jax.ShapeDtypeStruct((n, width), F32)),
+        tiles[split:] + packs[split // 2 :] + flat[split:] + [numerator, second, points, sums],
+        scratch=[
+            pltpu.VMEM((groups, 128), F32),
+            pltpu.VMEM((n, width), F32),
+            pltpu.SemaphoreType.DMA((chunks + 1,)),
+        ],
+        out_specs=(IN_HBM, IN_HBM),
+        name="last",
+    )
+    return potential.reshape(n), displacement
 
 
 def shifted(block, axis, distance):
@@ -125,7 +365,7 @@
     return (partner_pot, mirror_pot)
 
 
-def shards(points):
+def looped_shards(points):
     block_rows = points.shape[0]
     replicas = lax.axis_size("rep")
     team_count = lax.axis_size("team")
@@ -162,9 +402,19 @@
     return (potential, displacement)
 
 
+TILE_BYTES = 36 << 20
+
+
 def solution(mesh):
+    team = mesh.shape["team"]
+
+    def body(points):
+        n = points.shape[0]
+        fits = 4 * n * n * team <= TILE_BYTES and team == 8 and n % 256 == 0
+        return shards(points) if fits else looped_shards(points)
+
     return jax.shard_map(
-        shards,
+        body,
         mesh=mesh,
         in_specs=(P("team", None),),
         out_specs=(P("team"), P("team", None)),

time: 137 us -> 40.1 us (0.29)
  waiting for transfers between devices: 57.6 us -> 13.4 us
  blocking collectives: 20.4 us -> 0 us
  Pallas kernels: 0 us -> 15.2 us
  matrix products: 14.6 us -> 0 us
  between operations: 14.1 us -> 0.78 us
  starting transfers between devices: 17 us -> 8.62 us
  other arithmetic: 8.1 us -> 0 us
  local copies, waits for them, and re-layouts: 4.08 us -> 1.9 us
    psum x1 -> x0, waiting for transfers between devices: 28.1 us -> none  [shards(): second, numerator = lax.psum((second_local, numer_local), 'rep')]
    psum x2 -> x0, blocking collectives: 20.4 us -> none  [the longest x1 12 us: shards(): first_sum = lax.psum(first_local, 'rep')]
    ppermute x12 -> x11, waiting for transfers between devices: 29.5 us -> 13.4 us  [swapped(): return lax.ppermute(array, 'team', [(i, i ^ mask) for i in range(size)])]
    pallas_call x0 -> x13, Pallas kernels: none -> 15.2 us  [call(): pl.pallas_call(kernel, out_shape=out_shape, in_specs=[IN_VMEM] * len(args...]
    dot_general x48 -> x0, matrix products: 14.6 us -> none  [the longest x32 9.5 us: col_step(): lax.dot_general(part_x, other_x, (((1,), (1,)), ((), ())), preferred_elem...]
    ppermute x12 -> x11, starting transfers between devices: 17 us -> 8.62 us  [swapped(): return lax.ppermute(array, 'team', [(i, i ^ mask) for i in range(size)])]
    mul x66 -> x0, other arithmetic: 3.15 us -> none  [the longest x32 2.44 us: col_step(): 0.5 * other_sq[None, :]]
    dynamic_update_slice x12 -> x0, local copies, waits for them, and re-layouts: 2.08 us -> none  [the longest x8 2 us: row_step(): lax.dynamic_update_slice_in_dim(row_total, block_total, row_start, 0)]
  transfers between devices with their start and end apart: 13 -> 11, of which waited for: 11 -> 5; matrix products, arithmetic and copies ran while one was open for 9% -> 0% of each run, Pallas kernels for 0% -> 25%
where the time goes in v1:
time: 40.1 us; the launch traced here: 39.9 us
  Pallas kernels  15.2 us (38%)
  waiting for transfers between devices  13.4 us (33%)
  starting transfers between devices  8.62 us (21%)
  local copies, waits for them, and re-layouts  1.9 us (5%)
  between operations  0.78 us (2%)
    pallas_call x13, Pallas kernels, call(): pl.pallas_call(kernel, out_shape=out_shape, in_specs=[IN_VMEM] * len(args...  15.2 us
    ppermute x11, waiting for transfers between devices, swapped(): return lax.ppermute(array, 'team', [(i, i ^ mask) for i in range(size)])  13.4 us
    ppermute x11, starting transfers between devices, swapped(): return lax.ppermute(array, 'team', [(i, i ^ mask) for i in range(size)])  8.62 us
    unnamed x6, local copies, waits for them, and re-layouts  1.9 us
  transfers between devices with their start and end apart: 11, of which 5 were waited for; matrix products, arithmetic and copies ran while one was open for 0% of the time, Pallas kernels for 25%

profile of v1, /device:TPU:0, one launch (start us, length us, event | category | flops | bytes accessed | tf_op | source)
XLA Modules:
  0.0 39.9 jit_solution(11165005871393070149)
XLA Ops:
  0.6 3.0 %collective-permute-start.1 = (bf16[1024,128]{1,0:T(8,128)(2,1)}, bf16[1024,128]{1,0:T(8,128)(2,1)S(1)}, u32[]{:S(2)}, u32[]{:S(2)}) collective-permute-start(bf16[1024,128]{1,0:T(8,128)(2,1)} %refs_12_.1), channel_id=1, source_target_pairs={{0,8},{4,12},{8,0},{12,4},{16,24},{20,28},{24,16},{28,20},{1,9},{5... | collective-permute-start | bytes 786440 | tf_op jit(solution)/shard_map/ppermute | solution.py:23
  3.6 1.5 %collective-permute-start = (bf16[1024,128]{1,0:T(8,128)(2,1)}, bf16[1024,128]{1,0:T(8,128)(2,1)S(1)}, u32[]{:S(2)}, u32[]{:S(2)}) collective-permute-start(bf16[1024,128]{1,0:T(8,128)(2,1)} %refs_12_.1), channel_id=1, source_target_pairs={{0,16},{4,20},{8,24},{12,28},{16,0},{20,4},{24,8},{28,12},{1,17},{... | collective-permute-start | bytes 786440 | tf_op jit(solution)/shard_map/ppermute | solution.py:23
  5.2 0.0 collective-permute-start.5
  5.2 0.0 collective-permute-start.3
  5.2 5.8 %collective-permute-done.1.refs_1_.refs_8_ = bf16[1024,128]{1,0:T(8,128)(2,1)S(1)} collective-permute-done((bf16[1024,128]{1,0:T(8,128)(2,1)}, bf16[1024,128]{1,0:T(8,128)(2,1)S(1)}, u32[]{:S(2)}, u32[]{:S(2)}) %collective-permute-start.1) | collective-permute-done | bytes 262176 | tf_op jit(solution)/shard_map/ppermute | solution.py:23
  11.0 0.0 collective-permute-start.2
  11.0 6.2 %collective-permute-done.refs_1_.refs_6_ = bf16[1024,128]{1,0:T(8,128)(2,1)S(1)} collective-permute-done((bf16[1024,128]{1,0:T(8,128)(2,1)}, bf16[1024,128]{1,0:T(8,128)(2,1)S(1)}, u32[]{:S(2)}, u32[]{:S(2)}) %collective-permute-start) | collective-permute-done | bytes 262176 | tf_op jit(solution)/shard_map/ppermute | solution.py:23
  17.2 0.0 collective-permute-start.4
  17.2 0.0 collective-permute-done.5.refs_1_.refs_8_
  17.2 0.5 %collective-permute-start.6 = (bf16[1024,128]{1,0:T(8,128)(2,1)S(1)}, bf16[1024,128]{1,0:T(8,128)(2,1)S(1)}, u32[]{:S(2)}, u32[]{:S(2)}) collective-permute-start(bf16[1024,128]{1,0:T(8,128)(2,1)S(1)} %collective-permute-done.5.refs_1_.refs_8_), channel_id=1, source_target_pairs={{0,4},{4,0},{8,12},{12,8},{16,20},{20,16},{24,28},{28,24},{1,5},{5... | collective-permute-start | bytes 786440 | tf_op jit(solution)/shard_map/ppermute | solution.py:23
  17.7 0.0 copy-start
  17.7 0.9 %copy-done = bf16[1024,128]{1,0:T(8,128)(2,1)S(1)} copy-done((bf16[1024,128]{1,0:T(8,128)(2,1)S(1)}, bf16[1024,128]{1,0:T(8,128)(2,1)}, u32[]{:S(2)}) %copy-start) | copy-done | bytes 262168
  18.7 0.3 rows.1.refs_0_
  19.0 0.0 copy-start.1
  19.0 0.9 %copy-done.1 = bf16[1024,128]{1,0:T(8,128)(2,1)S(1)} copy-done((bf16[1024,128]{1,0:T(8,128)(2,1)S(1)}, bf16[1024,128]{1,0:T(8,128)(2,1)}, u32[]{:S(2)}) %copy-start.1) | copy-done | bytes 262168
  19.9 0.9 %first.8 = (f32[1024,1024]{1,0:T(8,128)S(1)}, f32[1024,128]{1,0:T(8,128)S(1)}) custom-call(bf16[1024,256]{1,0:T(8,128)(2,1)S(1)} %rows.1.refs_0_, bf16[1024,128]{1,0:T(8,128)(2,1)S(1)} %copy-done.1), custom_call_target="tpu_custom_call" | custom-call | tf_op jit(solution)/shard_map/first/pallas_call | solution.py:188
  20.9 0.0 collective-permute-done.3.refs_1_.refs_7_
  20.9 0.9 %first.9 = (f32[1024,1024]{1,0:T(8,128)S(1)}, f32[1024,128]{1,0:T(8,128)S(1)}) custom-call(bf16[1024,256]{1,0:T(8,128)(2,1)S(1)} %rows.1.refs_0_, bf16[1024,128]{1,0:T(8,128)(2,1)S(1)} %collective-permute-done.3.refs_1_.refs_7_, f32[1024,128]{1,0:T(8,128)S(1)} %get-tuple-element.22.refs_2_), custom_call_target="tpu_custom_call" | custom-call | tf_op jit(solution)/shard_map/first/pallas_call | solution.py:188
  21.8 0.0 copy-start.2
  21.8 0.9 %first.10 = (f32[1024,1024]{1,0:T(8,128)S(1)}, f32[1024,128]{1,0:T(8,128)S(1)}) custom-call(bf16[1024,256]{1,0:T(8,128)(2,1)S(1)} %rows.1.refs_0_, bf16[1024,128]{1,0:T(8,128)(2,1)S(1)} %collective-permute-done.1.refs_1_.refs_8_, f32[1024,128]{1,0:T(8,128)S(1)} %get-tuple-element.23.refs_2_), custom_call_target="tpu_custom_call" | custom-call | tf_op jit(solution)/shard_map/first/pallas_call | solution.py:188
  22.8 0.0 collective-permute-done.2.refs_1_.refs_9_
  22.8 1.0 %first.11 = (f32[1024,1024]{1,0:T(8,128)S(1)}, f32[1024,128]{1,0:T(8,128)S(1)}) custom-call(bf16[1024,256]{1,0:T(8,128)(2,1)S(1)} %rows.1.refs_0_, bf16[1024,128]{1,0:T(8,128)(2,1)S(1)} %collective-permute-done.2.refs_1_.refs_9_, f32[1024,128]{1,0:T(8,128)S(1)} %get-tuple-element.24.refs_2_), custom_call_target="tpu_custom_call" | custom-call | tf_op jit(solution)/shard_map/first/pallas_call | solution.py:188
  23.8 0.9 %first.12 = (f32[1024,1024]{1,0:T(8,128)S(1)}, f32[1024,128]{1,0:T(8,128)S(1)}) custom-call(bf16[1024,256]{1,0:T(8,128)(2,1)S(1)} %rows.1.refs_0_, bf16[1024,128]{1,0:T(8,128)(2,1)S(1)} %collective-permute-done.refs_1_.refs_6_, f32[1024,128]{1,0:T(8,128)S(1)} %get-tuple-element.25.refs_2_), custom_call_target="tpu_custom_call" | custom-call | tf_op jit(solution)/shard_map/first/pallas_call | solution.py:188
  24.7 0.0 collective-permute-done.4.refs_1_.refs_7_
  24.7 1.0 %first.13 = (f32[1024,1024]{1,0:T(8,128)S(1)}, f32[1024,128]{1,0:T(8,128)S(1)}) custom-call(bf16[1024,256]{1,0:T(8,128)(2,1)S(1)} %rows.1.refs_0_, bf16[1024,128]{1,0:T(8,128)(2,1)S(1)} %collective-permute-done.4.refs_1_.refs_7_, f32[1024,128]{1,0:T(8,128)S(1)} %get-tuple-element.27.refs_2_), custom_call_target="tpu_custom_call" | custom-call | tf_op jit(solution)/shard_map/first/pallas_call | solution.py:188
  25.7 0.9 %first.14 = (f32[1024,1024]{1,0:T(8,128)S(1)}, f32[1024,128]{1,0:T(8,128)S(1)}) custom-call(bf16[1024,256]{1,0:T(8,128)(2,1)S(1)} %rows.1.refs_0_, bf16[1024,128]{1,0:T(8,128)(2,1)S(1)} %collective-permute-done.5.refs_1_.refs_8_, f32[1024,128]{1,0:T(8,128)S(1)} %get-tuple-element.29.refs_2_), custom_call_target="tpu_custom_call" | custom-call | tf_op jit(solution)/shard_map/first/pallas_call | solution.py:188
  26.7 0.0 collective-permute-done.6.refs_1_.refs_9_
  26.7 1.0 %first.15 = (f32[1024,1024]{1,0:T(8,128)S(1)}, f32[1024,128]{1,0:T(8,128)S(1)}) custom-call(bf16[1024,256]{1,0:T(8,128)(2,1)S(1)} %rows.1.refs_0_, bf16[1024,128]{1,0:T(8,128)(2,1)S(1)} %collective-permute-done.6.refs_1_.refs_9_, f32[1024,128]{1,0:T(8,128)S(1)} %get-tuple-element.31.refs_2_), custom_call_target="tpu_custom_call" | custom-call | tf_op jit(solution)/shard_map/first/pallas_call | solution.py:188
  27.6 0.2 sums.1.own_ref.refs_13_
  27.8 0.1 collective-permute-start.7
  27.9 1.2 %collective-permute-done.7.mate_ref = f32[8,128]{1,0:T(8,128)S(1)} collective-permute-done((f32[8,128]{1,0:T(8,128)S(1)}, f32[8,128]{1,0:T(8,128)S(1)}, u32[]{:S(2)}, u32[]{:S(2)}) %collective-permute-start.7) | collective-permute-done | bytes 4128 | tf_op jit(solution)/shard_map/ppermute | solution.py:23
  29.1 0.9 %collective-permute-start.10 = (f32[16,128]{1,0:T(8,128)S(1)}, f32[16,128]{1,0:T(8,128)S(1)}, u32[]{:S(2)}, u32[]{:S(2)}) collective-permute-start(f32[16,128]{1,0:T(8,128)S(1)} %pack.1.refs_4_), channel_id=1, source_target_pairs={{0,8},{4,12},{8,0},{12,4},{16,24},{20,28},{24,16},{28,20},{1,9},{5... | collective-permute-start | bytes 24584 | tf_op jit(solution)/shard_map/ppermute | solution.py:23
  30.0 2.1 %collective-permute-start.9 = (f32[16,128]{1,0:T(8,128)S(1)}, f32[16,128]{1,0:T(8,128)S(1)}, u32[]{:S(2)}, u32[]{:S(2)}) collective-permute-start(f32[16,128]{1,0:T(8,128)S(1)} %pack.1.refs_4_), channel_id=1, source_target_pairs={{0,24},{4,28},{8,16},{12,20},{16,8},{20,12},{24,0},{28,4},{1,25},{... | collective-permute-start | bytes 24584 | tf_op jit(solution)/shard_map/ppermute | solution.py:23
  32.1 0.5 %collective-permute-start.8 = (f32[16,128]{1,0:T(8,128)S(1)}, f32[16,128]{1,0:T(8,128)S(1)}, u32[]{:S(2)}, u32[]{:S(2)}) collective-permute-start(f32[16,128]{1,0:T(8,128)S(1)} %pack.1.refs_4_), channel_id=1, source_target_pairs={{0,16},{4,20},{8,24},{12,28},{16,0},{20,4},{24,8},{28,12},{1,17},{... | collective-permute-start | bytes 24584 | tf_op jit(solution)/shard_map/ppermute | solution.py:23
  32.6 0.2 collective-permute-done.10.refs_5_
  32.7 0.0 copy-done.2
  32.7 2.9 %second.1 = (f32[1024,128]{1,0:T(8,128)S(1)}, f32[1024,128]{1,0:T(8,128)S(1)}) custom-call(f32[1024,1024]{1,0:T(8,128)S(1)} %get-tuple-element.34.refs_0_, f32[1024,1024]{1,0:T(8,128)S(1)} %get-tuple-element.35.refs_1_, f32[1024,1024]{1,0:T(8,128)S(1)} %get-tuple-element.36.refs_2_, f32[1024,1024]{1,0:T(8,128)S(1)} %get-tuple-element.37.refs_3_, ...), custom_call_target="tpu_custom_call" | custom-call | tf_op jit(solution)/shard_map/second/pallas_call | solution.py:188
  35.6 0.0 collective-permute-done.9.refs_5_
  35.7 0.1 collective-permute-done.8.refs_4_
  35.7 4.2 %last.1 = (f32[8,128]{1,0:T(8,128)}, f32[1024,128]{1,0:T(8,128)}) custom-call(f32[1024,1024]{1,0:T(8,128)S(1)} %get-tuple-element.26.refs_0_, f32[1024,1024]{1,0:T(8,128)S(1)} %get-tuple-element.28.refs_1_, f32[1024,1024]{1,0:T(8,128)S(1)} %get-tuple-element.30.refs_2_, f32[1024,1024]{1,0:T(8,128)S(1)} %get-tuple-element.32.refs_3_, ...), custom_call_target="tpu_custom_call" | custom-call | tf_op jit(solution)/shard_map/last/pallas_call | solution.py:188
  (1 shorter events, 0.0 us)
Async XLA Ops:
  0.6 10.4 %collective-permute-start.1 = (bf16[1024,128]{1,0:T(8,128)(2,1)}, bf16[1024,128]{1,0:T(8,128)(2,1)S(1)}, u32[]{:S(2)}, u32[]{:S(2)}) collective-permute-start(bf16[1024,128]{1,0:T(8,128)(2,1)} %refs_12_.1), channel_id=1, source_target_pairs={{0,8},{4,12},{8,0},{12,4},{16,24},{20,28},{24,16},{28,20},{1,9},{5... | collective-permute-start | bytes 786440 | tf_op jit(solution)/shard_map/ppermute | solution.py:23
  3.6 13.6 %collective-permute-start = (bf16[1024,128]{1,0:T(8,128)(2,1)}, bf16[1024,128]{1,0:T(8,128)(2,1)S(1)}, u32[]{:S(2)}, u32[]{:S(2)}) collective-permute-start(bf16[1024,128]{1,0:T(8,128)(2,1)} %refs_12_.1), channel_id=1, source_target_pairs={{0,16},{4,20},{8,24},{12,28},{16,0},{20,4},{24,8},{28,12},{1,17},{... | collective-permute-start | bytes 786440 | tf_op jit(solution)/shard_map/ppermute | solution.py:23
  5.2 12.1 %collective-permute-start.5 = (bf16[1024,128]{1,0:T(8,128)(2,1)}, bf16[1024,128]{1,0:T(8,128)(2,1)S(1)}, u32[]{:S(2)}, u32[]{:S(2)}) collective-permute-start(bf16[1024,128]{1,0:T(8,128)(2,1)} %refs_12_.1), channel_id=1, source_target_pairs={{0,24},{4,28},{8,16},{12,20},{16,8},{20,12},{24,0},{28,4},{1,25},{... | collective-permute-start | bytes 786440 | tf_op jit(solution)/shard_map/ppermute | solution.py:23
  5.2 15.7 %collective-permute-start.3 = (bf16[1024,128]{1,0:T(8,128)(2,1)}, bf16[1024,128]{1,0:T(8,128)(2,1)S(1)}, u32[]{:S(2)}, u32[]{:S(2)}) collective-permute-start(bf16[1024,128]{1,0:T(8,128)(2,1)} %refs_12_.1), channel_id=1, source_target_pairs={{0,4},{4,0},{8,12},{12,8},{16,20},{20,16},{24,28},{28,24},{1,5},{5... | collective-permute-start | bytes 786440 | tf_op jit(solution)/shard_map/ppermute | solution.py:23
  11.0 11.8 %collective-permute-start.2 = (bf16[1024,128]{1,0:T(8,128)(2,1)S(1)}, bf16[1024,128]{1,0:T(8,128)(2,1)S(1)}, u32[]{:S(2)}, u32[]{:S(2)}) collective-permute-start(bf16[1024,128]{1,0:T(8,128)(2,1)S(1)} %collective-permute-done.1.refs_1_.refs_8_), channel_id=1, source_target_pairs={{0,4},{4,0},{8,12},{12,8},{16,20},{20,16},{24,28},{28,24},{1,5},{5... | collective-permute-start | bytes 786440 | tf_op jit(solution)/shard_map/ppermute | solution.py:23
  17.2 7.5 %collective-permute-start.4 = (bf16[1024,128]{1,0:T(8,128)(2,1)S(1)}, bf16[1024,128]{1,0:T(8,128)(2,1)S(1)}, u32[]{:S(2)}, u32[]{:S(2)}) collective-permute-start(bf16[1024,128]{1,0:T(8,128)(2,1)S(1)} %collective-permute-done.refs_1_.refs_6_), channel_id=1, source_target_pairs={{0,4},{4,0},{8,12},{12,8},{16,20},{20,16},{24,28},{28,24},{1,5},{5... | collective-permute-start | bytes 786440 | tf_op jit(solution)/shard_map/ppermute | solution.py:23
  17.2 9.4 %collective-permute-start.6 = (bf16[1024,128]{1,0:T(8,128)(2,1)S(1)}, bf16[1024,128]{1,0:T(8,128)(2,1)S(1)}, u32[]{:S(2)}, u32[]{:S(2)}) collective-permute-start(bf16[1024,128]{1,0:T(8,128)(2,1)S(1)} %collective-permute-done.5.refs_1_.refs_8_), channel_id=1, source_target_pairs={{0,4},{4,0},{8,12},{12,8},{16,20},{20,16},{24,28},{28,24},{1,5},{5... | collective-permute-start | bytes 786440 | tf_op jit(solution)/shard_map/ppermute | solution.py:23
  17.7 0.9 %copy-start = (bf16[1024,128]{1,0:T(8,128)(2,1)S(1)}, bf16[1024,128]{1,0:T(8,128)(2,1)}, u32[]{:S(2)}) copy-start(bf16[1024,128]{1,0:T(8,128)(2,1)} %refs_12_.1) | copy-start | bytes 786436
  19.0 1.0 %copy-start.1 = (bf16[1024,128]{1,0:T(8,128)(2,1)S(1)}, bf16[1024,128]{1,0:T(8,128)(2,1)}, u32[]{:S(2)}) copy-start(bf16[1024,128]{1,0:T(8,128)(2,1)} %refs_12_.1) | copy-start | bytes 786436
  21.8 10.9 %copy-start.2 = (bf16[1024,128]{1,0:T(8,128)(2,1)S(1)}, bf16[1024,128]{1,0:T(8,128)(2,1)}, u32[]{:S(2)}) copy-start(bf16[1024,128]{1,0:T(8,128)(2,1)} %refs_12_.1) | copy-start | bytes 786436
  27.8 1.2 %collective-permute-start.7 = (f32[8,128]{1,0:T(8,128)S(1)}, f32[8,128]{1,0:T(8,128)S(1)}, u32[]{:S(2)}, u32[]{:S(2)}) collective-permute-start(f32[8,128]{1,0:T(8,128)S(1)} %sums.1.own_ref.refs_13_), channel_id=1, source_target_pairs={{0,4},{4,0},{8,12},{12,8},{16,20},{20,16},{24,28},{28,24},{1,5},{5... | collective-permute-start | bytes 12296 | tf_op jit(solution)/shard_map/ppermute | solution.py:23
  29.1 3.7 %collective-permute-start.10 = (f32[16,128]{1,0:T(8,128)S(1)}, f32[16,128]{1,0:T(8,128)S(1)}, u32[]{:S(2)}, u32[]{:S(2)}) collective-permute-start(f32[16,128]{1,0:T(8,128)S(1)} %pack.1.refs_4_), channel_id=1, source_target_pairs={{0,8},{4,12},{8,0},{12,4},{16,24},{20,28},{24,16},{28,20},{1,9},{5... | collective-permute-start | bytes 24584 | tf_op jit(solution)/shard_map/ppermute | solution.py:23
  30.0 5.7 %collective-permute-start.9 = (f32[16,128]{1,0:T(8,128)S(1)}, f32[16,128]{1,0:T(8,128)S(1)}, u32[]{:S(2)}, u32[]{:S(2)}) collective-permute-start(f32[16,128]{1,0:T(8,128)S(1)} %pack.1.refs_4_), channel_id=1, source_target_pairs={{0,24},{4,28},{8,16},{12,20},{16,8},{20,12},{24,0},{28,4},{1,25},{... | collective-permute-start | bytes 24584 | tf_op jit(solution)/shard_map/ppermute | solution.py:23
  32.1 3.7 %collective-permute-start.8 = (f32[16,128]{1,0:T(8,128)S(1)}, f32[16,128]{1,0:T(8,128)S(1)}, u32[]{:S(2)}, u32[]{:S(2)}) collective-permute-start(f32[16,128]{1,0:T(8,128)S(1)} %pack.1.refs_4_), channel_id=1, source_target_pairs={{0,16},{4,20},{8,24},{12,28},{16,0},{20,4},{24,8},{28,12},{1,17},{... | collective-permute-start | bytes 24584 | tf_op jit(solution)/shard_map/ppermute | solution.py:23

commit v2 on v0

--- a/solution.py
+++ b/solution.py
@@ -1,7 +1,332 @@
+import functools
 import jax
 import jax.numpy as jnp
 from jax import lax
+from jax.experimental import pallas as pl
+from jax.experimental.pallas import tpu as pltpu
 from jax.sharding import PartitionSpec as P
+
+F32 = jnp.float32
+BF16 = jnp.bfloat16
+NT = (((1,), (1,)), ((), ()))
+IN_VMEM = pl.BlockSpec(memory_space=pltpu.VMEM)
+IN_HBM = pl.BlockSpec(memory_space=pl.ANY)
+PARAMS = pltpu.CompilerParams(vmem_limit_bytes=16 << 20)
+
+
+def kept(array):
+    return pltpu.with_memory_space_constraint(array, pltpu.VMEM)
+
+
+def swapped(array, mask):
+    size = lax.axis_size("team")
+    return lax.ppermute(array, "team", [(i, i ^ mask) for i in range(size)])
+
+
+def exchanged(array, even, odd):
+    size = lax.axis_size("team")
+    return lax.ppermute(array, "team", [(i, i ^ (odd if i % 2 else even)) for i in range(size)])
+
+
+def down(rows):
+    row = lax.broadcasted_iota(jnp.int32, (128, 128), 0)
+    diagonal = row == lax.broadcasted_iota(jnp.int32, (128, 128), 1)
+    wide = [jnp.where(diagonal, rows[g : g + 1, :], 0.0) for g in range(rows.shape[0])]
+    return jnp.concatenate([jnp.broadcast_to(jnp.sum(w, axis=1, keepdims=True), (128, 128)) for w in wide], axis=0)
+
+
+def across(columns):
+    row = lax.broadcasted_iota(jnp.int32, (128, 128), 0)
+    diagonal = row == lax.broadcasted_iota(jnp.int32, (128, 128), 1)
+    sums = [jnp.sum(columns[g : g + 128, :], axis=1, keepdims=True) for g in range(0, columns.shape[0], 128)]
+    return [jnp.sum(jnp.where(diagonal, s, 0.0), axis=0, keepdims=True) for s in sums]
+
+
+def pieces(x_turned):
+    wide = x_turned.astype(F32)
+    norms = jnp.sum(wide * wide, axis=0, keepdims=True)
+    high = norms.astype(BF16).astype(F32)
+    rest = norms - high
+    middle = rest.astype(BF16).astype(F32)
+    return high, middle, rest - middle
+
+
+def put_columns(cols, part, x, x_turned):
+    width = x.shape[1]
+    high, middle, low = pieces(x_turned)
+    sub = lax.broadcasted_iota(jnp.int32, (16, x.shape[0]), 0)
+    extra = jnp.where(sub == 0, high, jnp.where(sub == 1, middle, jnp.where(sub == 2, low, 1.0))).astype(BF16)
+    cols[part, :width] = x
+    cols[part, width:] = jnp.concatenate([extra] * (width // 16), axis=0).T
+
+
+def put_rows(rows, x_turned):
+    width, n = x_turned.shape
+    high, middle, low = pieces(x_turned)
+    sub = lax.broadcasted_iota(jnp.int32, (16, n), 0)
+    norm = jnp.where(sub == 3, high, jnp.where(sub == 4, middle, low))
+    extra = jnp.where(sub < 3, -0.125, jnp.where(sub < 6, norm * -0.125, 0.0))
+    rows[:width, :] = x_turned * jnp.asarray(0.25, BF16)
+    rows[width : width + 16, :] = extra.astype(BF16)
+    rows[width + 16 :, :] = jnp.zeros((width - 16, n), BF16)
+
+
+def row_kernel(x_ref, rows_ref, own_ref):
+    own_ref[...] = x_ref[...]
+    put_rows(rows_ref, x_ref[...].T)
+
+
+def first_kernel(count, start, sums, *refs):
+    rows_ref, x_refs, refs = refs[0], refs[1 : 1 + count], refs[1 + count :]
+    if sums and not start:
+        acc_in, refs = refs[0], refs[1:]
+    e_refs, turned_refs, refs = refs[:count], refs[count : 2 * count], refs[2 * count :]
+    if sums:
+        acc_ref, refs = refs[0], refs[1:]
+    n = x_refs[0].shape[0]
+    block = 256
+    for i in range(0, n, block):
+        groups = range(i // 128, (i + block) // 128)
+        if sums:
+            totals = [jnp.zeros((8, 128), F32) if start else acc_in[8 * g : 8 * g + 8, :] for g in groups]
+        for x_ref, e_ref, turned_ref, cols in zip(x_refs, e_refs, turned_refs, refs):
+            for j in range(0, n, block):
+                part = slice(j, j + block)
+                if i == 0:
+                    x_turned = x_ref[part, :].T
+                    turned_ref[:, part] = x_turned
+                    put_columns(cols, part, x_ref[part, :], x_turned)
+                p = jnp.dot(cols[part, :], rows_ref[:, i : i + block], preferred_element_type=F32)
+                for t, g in enumerate(groups):
+                    k = jnp.exp(p[:, t * 128 : (t + 1) * 128])
+                    e_ref[part, g * 128 : g * 128 + 128] = k * k
+                    if sums:
+                        totals[t] = totals[t] + jnp.sum(k.reshape(block // 8, 8, 128), axis=0)
+        if sums:
+            for t, g in enumerate(groups):
+                acc_ref[8 * g : 8 * g + 8, :] = totals[t]
+
+
+def between_kernel(near_ref, cross_ref, near_mate_ref, cross_mate_ref, near_t, cross_t, acc_in, out_ref, rows, cols, x, row_sums):
+    me = lax.axis_index("team")
+    core, side = me % 2, (me // 2) % 2
+    n, width = near_ref.shape
+    groups = n // 128
+    block = 256
+
+    @pl.when(core == 0)
+    def _():
+        rows[:width, :] = near_t[...]
+
+    @pl.when(core == 1)
+    def _():
+        rows[:width, :] = cross_t[...]
+
+    for which, (c, s) in ((cross_ref, (0, 0)), (near_ref, (1, 0)), (near_mate_ref, (0, 1)), (cross_mate_ref, (1, 1))):
+
+        @pl.when((core == c) & (side == s))
+        def _(which=which):
+            x[...] = which[...]
+
+    put_rows(rows, rows[:width, :])
+    for j in range(0, n, block):
+        part = slice(j, j + block)
+        put_columns(cols, part, x[part, :], x[part, :].T)
+        row_sums[part, :] = jnp.zeros((block, 128), F32)
+    for g in range(groups):
+        out_ref[g : g + 1, :] = jnp.sum(acc_in[8 * g : 8 * g + 8, :], axis=0, keepdims=True)
+    for i in range(0, n, block):
+        totals = [jnp.zeros((8, 128), F32) for _ in range(block // 128)]
+        for j in range(0, n, block):
+            part = slice(j, j + block)
+            p = jnp.dot(cols[part, :], rows[:, i : i + block], preferred_element_type=F32)
+            along = row_sums[part, :]
+            for t in range(block // 128):
+                k = jnp.exp(p[:, t * 128 : (t + 1) * 128])
+                along = along + k
+                totals[t] = totals[t] + jnp.sum(k.reshape(block // 8, 8, 128), axis=0)
+            row_sums[part, :] = along
+        for t, total in enumerate(totals):
+            g = groups + i // 128 + t
+            out_ref[g : g + 1, :] = jnp.sum(total, axis=0, keepdims=True)
+    other = jnp.concatenate(across(row_sums[...]), axis=0)
+    zero = jnp.zeros_like(other)
+    out_ref[2 * groups : 3 * groups, :] = jnp.where(side == 0, other, zero)
+    out_ref[3 * groups :, :] = jnp.where(side == 1, other, zero)
+
+
+def pack_kernel(own_ref, mate_ref, both_ref):
+    g = own_ref.shape[0]
+    both_ref[:g, :] = own_ref[...]
+    both_ref[g:, :] = mate_ref[...]
+
+
+def second_kernel(points, masks, *refs):
+    count = len(masks)
+    e_refs, refs = refs[:count], refs[count:]
+    x_refs, refs = refs[:count], refs[count:]
+    packs, refs = refs[: count // 2], refs[count // 2 :]
+    own_ref, pot_hbm, out_hbm, scales, pot_ref, out_ref, sems = refs
+    width, n = x_refs[0].shape
+    groups = n // 128
+    block = 256
+    core = lax.axis_index("team") % 2
+
+    def message(mask, slot):
+        first = (mask % 2 * 4 + slot) * groups
+        return packs[(0, 2, 3, 1)[mask // 2]][first : first + groups, :]
+
+    def first_sum(mask):
+        near = message(mask ^ 2, 1) + message(mask ^ 4, 2)
+        return message(mask, 0) + near + message(mask ^ 5, 3)
+
+    def put_scales(t):
+        even, odd = masks[t]
+        total = first_sum(even) if even == odd else jnp.where(core == 0, first_sum(even), first_sum(odd))
+        scales[t * n : (t + 1) * n, :] = down(float(points) / total)
+
+    copies = []
+    seconds = []
+    for i in range(0, n, block):
+        lanes = range(i, i + block, 128)
+        cols = slice(i, i + block)
+        numerator = jnp.zeros((width, block), F32)
+        totals = [jnp.zeros((8, 128), F32) for _ in lanes]
+        for t in range(count):
+            if i == 0:
+                put_scales(t)
+            for j in range(0, n, block):
+                scale = scales[t * n + j : t * n + j + block, :]
+                weights = []
+                for u, l in enumerate(lanes):
+                    w = e_refs[t][j : j + block, l : l + 128] * scale
+                    totals[u] = totals[u] + jnp.sum(w.reshape(block // 8, 8, 128), axis=0)
+                    weights.append(w.astype(BF16))
+                weight = jnp.concatenate(weights, axis=1)
+                numerator = numerator + jnp.dot(x_refs[t][:, j : j + block], weight, preferred_element_type=F32)
+        for u, l in enumerate(lanes):
+            second = jnp.sum(totals[u], axis=0, keepdims=True)
+            seconds.append(second)
+            image = (numerator[:, u * 128 : (u + 1) * 128] / second).T
+            out_ref[l : l + 128, :] = own_ref[l : l + 128, :].astype(F32) - image
+        copies.append(pltpu.make_async_copy(out_ref.at[cols, :], out_hbm.at[cols, :], sems.at[len(copies)]))
+        copies[-1].start()
+    log_count = jnp.log(jnp.float32(points))
+    second = jnp.concatenate(seconds, axis=0)
+    pot_one = -2.0 * (jnp.log(first_sum(0)) - log_count)
+    pot_ref[...] = 0.5 * (pot_one - 2.0 * (jnp.log(second) - log_count))
+    copies.append(pltpu.make_async_copy(pot_ref, pot_hbm, sems.at[len(copies)]))
+    copies[-1].start()
+    for copy in copies:
+        copy.wait()
+
+
+def shards(points):
+    n, width = points.shape
+    total_points = n * lax.axis_size("team")
+    groups = n // 128
+    chunks = n // 256
+
+    def tile(shape, dtype=F32):
+        return pltpu.VMEM(shape, dtype)
+
+    def call(kernel, out_shape, args, scratch=(), out_specs=None, name=None, tiles=0):
+        single = not isinstance(out_shape, tuple)
+        specs = out_specs or (IN_VMEM if single else tuple(IN_VMEM for _ in out_shape))
+        return pl.pallas_call(
+            kernel,
+            out_shape=out_shape,
+            in_specs=[IN_VMEM] * len(args),
+            out_specs=specs,
+            scratch_shapes=list(scratch),
+            compiler_params=PARAMS,
+            cost_estimate=pl.CostEstimate(flops=tiles * 24 * n * n * width, bytes_accessed=0, transcendentals=0),
+            name=name,
+        )(*[kept(a) for a in args])
+
+    acc = None
+    done = {}
+
+    def first(blocks, sums=True):
+        nonlocal acc
+        count = len(blocks)
+        out = call(
+            functools.partial(first_kernel, count, acc is None, sums),
+            (tile((n, n)),) * count + (tile((width, n), BF16),) * count + (tile((8 * groups, 128)),) * sums,
+            [rows, *blocks.values()] + ([acc] if sums and acc is not None else []),
+            scratch=[pltpu.VMEM((n, 2 * width), BF16)] * count,
+            name="first",
+            tiles=count,
+        )
+        for t, block in enumerate(blocks):
+            done[block] = (out[t], out[count + t])
+        if sums:
+            acc = out[-1]
+
+    def after(x):
+        nonlocal acc
+        x, acc = lax.optimization_barrier((x, acc))
+        return x
+
+    near = exchanged(points, 2, 4)
+    mate = swapped(points, 1)
+    rows, own = call(row_kernel, (tile((2 * width, n), BF16), tile((n, width), BF16)), [points], name="rows")
+    first(dict(own=own))
+    cross = exchanged(after(points), 4, 2)
+    first(dict(mate=mate))
+    near = after(near)
+    near_mate = swapped(near, 1)
+    first(dict(near=near))
+    diagonal = exchanged(after(near), 4, 2)
+    cross_mate = swapped(cross, 1)
+    first(dict(cross=cross))
+    first(dict(near_mate=near_mate, cross_mate=cross_mate))
+    sums = call(
+        between_kernel,
+        tile((4 * groups, 128)),
+        [near, cross, near_mate, cross_mate, done["near"][1], done["cross"][1], acc],
+        scratch=[
+            pltpu.VMEM((2 * width, n), BF16),
+            pltpu.VMEM((n, 2 * width), BF16),
+            pltpu.VMEM((n, width), BF16),
+            pltpu.VMEM((n, 128), F32),
+        ],
+        name="between",
+        tiles=1,
+    )
+    mate_sums = swapped(sums, 1)
+    both = call(pack_kernel, tile((8 * groups, 128)), [sums, mate_sums], name="pack")
+    far, *packs = [swapped(both, m) for m in (6, 2, 4)]
+    packs = [both, far, *packs]
+    diagonal, both = lax.optimization_barrier((diagonal, both))
+    diagonal_mate = swapped(diagonal, 1)
+    first(dict(diagonal=diagonal), sums=False)
+    first(dict(diagonal_mate=diagonal_mate), sums=False)
+    masks = dict(
+        own=(0, 0),
+        mate=(1, 1),
+        near=(2, 4),
+        cross_mate=(3, 5),
+        cross=(4, 2),
+        near_mate=(5, 3),
+        diagonal=(6, 6),
+        diagonal_mate=(7, 7),
+    )
+    potential, displacement = call(
+        functools.partial(second_kernel, total_points, list(masks.values())),
+        (jax.ShapeDtypeStruct((groups, 128), F32), jax.ShapeDtypeStruct((n, width), F32)),
+        [done[b][0] for b in masks] + [done[b][1] for b in masks] + packs + [own],
+        scratch=[
+            pltpu.VMEM((len(masks) * n, 128), F32),
+            pltpu.VMEM((groups, 128), F32),
+            pltpu.VMEM((n, width), F32),
+            pltpu.SemaphoreType.DMA((chunks + 1,)),
+        ],
+        out_specs=(IN_HBM, IN_HBM),
+        name="second",
+        tiles=len(masks),
+    )
+    return potential.reshape(n), displacement
 
 
 def shifted(block, axis, distance):
@@ -125,7 +450,7 @@
     return (partner_pot, mirror_pot)
 
 
-def shards(points):
+def looped_shards(points):
     block_rows = points.shape[0]
     replicas = lax.axis_size("rep")
     team_count = lax.axis_size("team")
@@ -162,9 +487,19 @@
     return (potential, displacement)
 
 
+TILE_BYTES = 36 << 20
+
+
 def solution(mesh):
+    team = mesh.shape["team"]
+
+    def body(points):
+        n = points.shape[0]
+        fits = 4 * n * n * team <= TILE_BYTES and team == 8 and n % 256 == 0
+        return shards(points) if fits else looped_shards(points)
+
     return jax.shard_map(
-        shards,
+        body,
         mesh=mesh,
         in_specs=(P("team", None),),
         out_specs=(P("team"), P("team", None)),

time: 137 us -> 30.4 us (0.22)
  waiting for transfers between devices: 57.6 us -> 2.79 us
  blocking collectives: 20.4 us -> 0 us
  matrix products: 14.6 us -> 0 us
  Pallas kernels: 0 us -> 13.8 us
  between operations: 14.1 us -> 0.92 us
  other arithmetic: 8.1 us -> 0 us
  starting transfers between devices: 17 us -> 11.7 us
  local copies, waits for them, and re-layouts: 4.08 us -> 0.99 us
    psum x1 -> x0, waiting for transfers between devices: 28.1 us -> none  [shards(): second, numerator = lax.psum((second_local, numer_local), 'rep')]
    ppermute x12 -> x11, waiting for transfers between devices: 29.5 us -> 2.79 us  [the longest x8 2.79 us: swapped(): return lax.ppermute(array, 'team', [(i, i ^ mask) for i in range(size)])]
    psum x2 -> x0, blocking collectives: 20.4 us -> none  [the longest x1 12 us: shards(): first_sum = lax.psum(first_local, 'rep')]
    dot_general x48 -> x0, matrix products: 14.6 us -> none  [the longest x32 9.5 us: col_step(): lax.dot_general(part_x, other_x, (((1,), (1,)), ((), ())), preferred_elem...]
    pallas_call x0 -> x11, Pallas kernels: none -> 13.8 us  [call(): pl.pallas_call(kernel, out_shape=out_shape, in_specs=[IN_VMEM] * len(args...]
    ppermute x12 -> x11, starting transfers between devices: 17 us -> 11.7 us  [the longest x3 7.43 us: exchanged(): lax.ppermute(array, 'team', [(i, i ^ (odd if i % 2 else even)) for i in r...]
    mul x66 -> x0, other arithmetic: 3.15 us -> none  [the longest x32 2.44 us: col_step(): 0.5 * other_sq[None, :]]
    dynamic_update_slice x12 -> x0, local copies, waits for them, and re-layouts: 2.08 us -> none  [the longest x8 2 us: row_step(): lax.dynamic_update_slice_in_dim(row_total, block_total, row_start, 0)]
  transfers between devices with their start and end apart: 13 -> 11, of which waited for: 11 -> 4; matrix products, arithmetic and copies ran while one was open for 9% -> 0% of each run, Pallas kernels for 0% -> 29%
where the time goes in v2:
time: 30.4 us; the launch traced here: 30.2 us
  Pallas kernels  13.8 us (45%)
  starting transfers between devices  11.7 us (38%)
  waiting for transfers between devices  2.79 us (9%)
  local copies, waits for them, and re-layouts  0.99 us (3%)
  between operations  0.92 us (3%)
    pallas_call x11, Pallas kernels, call(): pl.pallas_call(kernel, out_shape=out_shape, in_specs=[IN_VMEM] * len(args...  13.8 us
    ppermute x3, starting transfers between devices, exchanged(): lax.ppermute(array, 'team', [(i, i ^ (odd if i % 2 else even)) for i in r...  7.43 us
    ppermute x8, starting transfers between devices, swapped(): return lax.ppermute(array, 'team', [(i, i ^ mask) for i in range(size)])  4.28 us
    ppermute x8, waiting for transfers between devices, swapped(): return lax.ppermute(array, 'team', [(i, i ^ mask) for i in range(size)])  2.79 us
    unnamed x4, local copies, waits for them, and re-layouts  0.99 us
  transfers between devices with their start and end apart: 11, of which 4 were waited for; matrix products, arithmetic and copies ran while one was open for 0% of the time, Pallas kernels for 29%

profile of v2, /device:TPU:0, one launch (start us, length us, event | category | flops | bytes accessed | tf_op | source)
XLA Modules:
  0.0 30.2 jit_solution(11052632556656098830)
XLA Ops:
  0.6 0.5 %collective-permute-start = (bf16[1024,128]{1,0:T(8,128)(2,1)}, bf16[1024,128]{1,0:T(8,128)(2,1)S(1)}, u32[]{:S(2)}, u32[]{:S(2)}) collective-permute-start(bf16[1024,128]{1,0:T(8,128)(2,1)} %x_ref.1), channel_id=1, source_target_pairs={{0,4},{4,0},{8,12},{12,8},{16,20},{20,16},{24,28},{28,24},{1,5},{5... | collective-permute-start | bytes 786440 | tf_op jit(solution)/shard_map/ppermute | solution.py:23
  1.1 2.6 %collective-permute-start.1 = (bf16[1024,128]{1,0:T(8,128)(2,1)}, bf16[1024,128]{1,0:T(8,128)(2,1)S(1)}, u32[]{:S(2)}, u32[]{:S(2)}) collective-permute-start(bf16[1024,128]{1,0:T(8,128)(2,1)} %x_ref.1), channel_id=1, source_target_pairs={{0,8},{4,20},{8,0},{12,28},{16,24},{20,4},{24,16},{28,12},{1,9},{5... | collective-permute-start | bytes 786440 | tf_op jit(solution)/shard_map/ppermute | solution.py:28
  3.7 0.0 copy-start
  3.7 1.0 %copy-done = bf16[1024,128]{1,0:T(8,128)(2,1)S(1)} copy-done((bf16[1024,128]{1,0:T(8,128)(2,1)S(1)}, bf16[1024,128]{1,0:T(8,128)(2,1)}, u32[]{:S(2)}) %copy-start) | copy-done | bytes 262168
  4.7 0.2 rows.1
  4.9 0.0 copy-start.1
  4.9 0.9 %first.7 = (f32[1024,1024]{1,0:T(8,128)S(1)}, bf16[128,1024]{1,0:T(8,128)(2,1)S(1)}, f32[64,128]{1,0:T(8,128)S(1)}) custom-call(bf16[256,1024]{1,0:T(8,128)(2,1)S(1)} %get-tuple-element.34.refs_0_, bf16[1024,128]{1,0:T(8,128)(2,1)S(1)} %get-tuple-element.35.refs_1_.refs_20_), custom_call_target="tpu_custom_call" | custom-call | flops 3221225472 | tf_op jit(solution)/shard_map/first/pallas_call | solution.py:236
  5.8 0.0 copy-done.1
  5.8 1.6 %collective-permute-start.3 = (bf16[1024,128]{1,0:T(8,128)(2,1)S(1)}, bf16[1024,128]{1,0:T(8,128)(2,1)S(1)}, u32[]{:S(2)}, u32[]{:S(2)}) collective-permute-start(bf16[1024,128]{1,0:T(8,128)(2,1)S(1)} %copy-done.1), channel_id=1, source_target_pairs={{0,16},{4,12},{8,24},{12,4},{16,0},{20,28},{24,8},{28,20},{1,17},{... | collective-permute-start | bytes 786440 | tf_op jit(solution)/shard_map/ppermute | solution.py:28
  7.4 0.0 collective-permute-done.refs_1_
  7.4 0.9 %first.8 = (f32[1024,1024]{1,0:T(8,128)S(1)}, bf16[128,1024]{1,0:T(8,128)(2,1)S(1)}, f32[64,128]{1,0:T(8,128)S(1)}) custom-call(bf16[256,1024]{1,0:T(8,128)(2,1)S(1)} %get-tuple-element.34.refs_0_, bf16[1024,128]{1,0:T(8,128)(2,1)S(1)} %collective-permute-done.refs_1_, f32[64,128]{1,0:T(8,128)S(1)} %get-tuple-element.38.refs_2_), custom_call_target="tpu_custom_call" | custom-call | flops 3221225472 | tf_op jit(solution)/shard_map/first/pallas_call | solution.py:236
  8.4 0.0 collective-permute-done.1.refs_1_.near_ref
  8.4 0.1 collective-permute-start.2
  8.4 0.9 %first.9 = (f32[1024,1024]{1,0:T(8,128)S(1)}, bf16[128,1024]{1,0:T(8,128)(2,1)S(1)}, f32[64,128]{1,0:T(8,128)S(1)}) custom-call(bf16[256,1024]{1,0:T(8,128)(2,1)S(1)} %get-tuple-element.34.refs_0_, bf16[1024,128]{1,0:T(8,128)(2,1)S(1)} %collective-permute-done.1.refs_1_.near_ref, f32[64,128]{1,0:T(8,128)S(1)} %get-tuple-element.42.refs_2_), custom_call_target="tpu_custom_call" | custom-call | flops 3221225472 | tf_op jit(solution)/shard_map/first/pallas_call | solution.py:236
  9.4 3.3 %collective-permute-start.5 = (bf16[1024,128]{1,0:T(8,128)(2,1)S(1)}, bf16[1024,128]{1,0:T(8,128)(2,1)S(1)}, u32[]{:S(2)}, u32[]{:S(2)}) collective-permute-start(bf16[1024,128]{1,0:T(8,128)(2,1)S(1)} %collective-permute-done.1.refs_1_.near_ref), channel_id=1, source_target_pairs={{0,16},{4,12},{8,24},{12,4},{16,0},{20,28},{24,8},{28,20},{1,17},{... | collective-permute-start | bytes 786440 | tf_op jit(solution)/shard_map/ppermute | solution.py:28
  12.7 0.0 collective-permute-done.3.refs_1_.cross_ref
  12.7 0.0 collective-permute-start.4
  12.7 0.9 %first.10 = (f32[1024,1024]{1,0:T(8,128)S(1)}, bf16[128,1024]{1,0:T(8,128)(2,1)S(1)}, f32[64,128]{1,0:T(8,128)S(1)}) custom-call(bf16[256,1024]{1,0:T(8,128)(2,1)S(1)} %get-tuple-element.34.refs_0_, bf16[1024,128]{1,0:T(8,128)(2,1)S(1)} %collective-permute-done.3.refs_1_.cross_ref, f32[64,128]{1,0:T(8,128)S(1)} %get-tuple-element.46.refs_2_), custom_call_target="tpu_custom_call" | custom-call | flops 3221225472 | tf_op jit(solution)/shard_map/first/pallas_call | solution.py:236
  13.6 0.0 collective-permute-done.2.refs_1_.near_mate_ref
  13.6 0.6 %collective-permute-done.4.refs_2_.cross_mate_ref = bf16[1024,128]{1,0:T(8,128)(2,1)S(1)} collective-permute-done((bf16[1024,128]{1,0:T(8,128)(2,1)S(1)}, bf16[1024,128]{1,0:T(8,128)(2,1)S(1)}, u32[]{:S(2)}, u32[]{:S(2)}) %collective-permute-start.4) | collective-permute-done | bytes 262176 | tf_op jit(solution)/shard_map/ppermute | solution.py:23
  14.2 1.7 %first.11 = (f32[1024,1024]{1,0:T(8,128)S(1)}, f32[1024,1024]{1,0:T(8,128)S(1)}, bf16[128,1024]{1,0:T(8,128)(2,1)S(1)}, bf16[128,1024]{1,0:T(8,128)(2,1)S(1)}, f32[64,128]{1,0:T(8,128)S(1)}) custom-call(bf16[256,1024]{1,0:T(8,128)(2,1)S(1)} %get-tuple-element.34.refs_0_, bf16[1024,128]{1,0:T(8,128)(2,1)S(1)} %collective-permute-done.2.refs_1_.near_mate_ref, ...), custom_call_target="tpu_custom_call" | custom-call | flops 6442450944 | tf_op jit(solution)/shard_map/first/pallas_call | solution.py:236
  15.9 1.3 %between.1.own_ref = f32[32,128]{1,0:T(8,128)S(1)} custom-call(bf16[1024,128]{1,0:T(8,128)(2,1)S(1)} %collective-permute-done.1.refs_1_.near_ref, bf16[1024,128]{1,0:T(8,128)(2,1)S(1)} %collective-permute-done.3.refs_1_.cross_ref, bf16[1024,128]{1,0:T(8,128)(2,1)S(1)} %collective-permute-done.2.refs_1_.near_mate_ref, ...), custom_call_target="tpu_custom_call" | custom-call | flops 3221225472 | tf_op jit(solution)/shard_map/between/pallas_call | solution.py:236
  17.3 0.2 collective-permute-start.6
  17.5 1.0 %collective-permute-done.6.mate_ref = f32[32,128]{1,0:T(8,128)S(1)} collective-permute-done((f32[32,128]{1,0:T(8,128)S(1)}, f32[32,128]{1,0:T(8,128)S(1)}, u32[]{:S(2)}, u32[]{:S(2)}) %collective-permute-start.6) | collective-permute-done | bytes 16416 | tf_op jit(solution)/shard_map/ppermute | solution.py:23
  18.5 1.3 %collective-permute-start.8 = (f32[64,128]{1,0:T(8,128)S(1)}, f32[64,128]{1,0:T(8,128)S(1)}, u32[]{:S(2)}, u32[]{:S(2)}) collective-permute-start(f32[64,128]{1,0:T(8,128)S(1)} %pack.1.refs_16_), channel_id=1, source_target_pairs={{0,24},{4,28},{8,16},{12,20},{16,8},{20,12},{24,0},{28,4},{1,25},{... | collective-permute-start | bytes 98312 | tf_op jit(solution)/shard_map/ppermute | solution.py:23
  19.9 1.3 %collective-permute-start.9 = (f32[64,128]{1,0:T(8,128)S(1)}, f32[64,128]{1,0:T(8,128)S(1)}, u32[]{:S(2)}, u32[]{:S(2)}) collective-permute-start(f32[64,128]{1,0:T(8,128)S(1)} %pack.1.refs_16_), channel_id=1, source_target_pairs={{0,8},{4,12},{8,0},{12,4},{16,24},{20,28},{24,16},{28,20},{1,9},{5... | collective-permute-start | bytes 98312 | tf_op jit(solution)/shard_map/ppermute | solution.py:23
  21.1 0.9 %collective-permute-start.10 = (f32[64,128]{1,0:T(8,128)S(1)}, f32[64,128]{1,0:T(8,128)S(1)}, u32[]{:S(2)}, u32[]{:S(2)}) collective-permute-start(f32[64,128]{1,0:T(8,128)S(1)} %pack.1.refs_16_), channel_id=1, source_target_pairs={{0,16},{4,20},{8,24},{12,28},{16,0},{20,4},{24,8},{28,12},{1,17},{... | collective-permute-start | bytes 98312 | tf_op jit(solution)/shard_map/ppermute | solution.py:23
  22.0 0.0 collective-permute-done.5.refs_1_
  22.0 0.0 collective-permute-start.7
  22.0 0.9 %first.12 = (f32[1024,1024]{1,0:T(8,128)S(1)}, bf16[128,1024]{1,0:T(8,128)(2,1)S(1)}) custom-call(bf16[256,1024]{1,0:T(8,128)(2,1)S(1)} %get-tuple-element.34.refs_0_, bf16[1024,128]{1,0:T(8,128)(2,1)S(1)} %collective-permute-done.5.refs_1_), custom_call_target="tpu_custom_call" | custom-call | flops 3221225472 | tf_op jit(solution)/shard_map/first/pallas_call | solution.py:236
  23.0 0.6 %collective-permute-done.7.refs_1_ = bf16[1024,128]{1,0:T(8,128)(2,1)S(1)} collective-permute-done((bf16[1024,128]{1,0:T(8,128)(2,1)S(1)}, bf16[1024,128]{1,0:T(8,128)(2,1)S(1)}, u32[]{:S(2)}, u32[]{:S(2)}) %collective-permute-start.7) | collective-permute-done | bytes 262176 | tf_op jit(solution)/shard_map/ppermute | solution.py:23
  23.6 0.9 %first.13 = (f32[1024,1024]{1,0:T(8,128)S(1)}, bf16[128,1024]{1,0:T(8,128)(2,1)S(1)}) custom-call(bf16[256,1024]{1,0:T(8,128)(2,1)S(1)} %get-tuple-element.34.refs_0_, bf16[1024,128]{1,0:T(8,128)(2,1)S(1)} %collective-permute-done.7.refs_1_), custom_call_target="tpu_custom_call" | custom-call | flops 3221225472 | tf_op jit(solution)/shard_map/first/pallas_call | solution.py:236
  24.5 0.0 collective-permute-done.8.refs_17_
  24.5 0.0 collective-permute-done.9.refs_18_
  24.5 0.5 %collective-permute-done.10.refs_19_ = f32[64,128]{1,0:T(8,128)S(1)} collective-permute-done((f32[64,128]{1,0:T(8,128)S(1)}, f32[64,128]{1,0:T(8,128)S(1)}, u32[]{:S(2)}, u32[]{:S(2)}) %collective-permute-start.10) | collective-permute-done | bytes 32800 | tf_op jit(solution)/shard_map/ppermute | solution.py:23
  25.1 5.0 %second.1 = (f32[8,128]{1,0:T(8,128)}, f32[1024,128]{1,0:T(8,128)}) custom-call(f32[1024,1024]{1,0:T(8,128)S(1)} %get-tuple-element.36.refs_0_, f32[1024,1024]{1,0:T(8,128)S(1)} %get-tuple-element.39.refs_1_, f32[1024,1024]{1,0:T(8,128)S(1)} %get-tuple-element.43.refs_2_, f32[1024,1024]{1,0:T(8,128)S(1)} %get-tuple-element.48.refs_3_, ...), custom_call_target="tpu_custom_call" | custom-call | flops 25769803776 | tf_op jit(solution)/shard_map/second/pallas_call | solution.py:236
  (1 shorter events, 0.0 us)
Async XLA Ops:
  0.6 6.8 %collective-permute-start = (bf16[1024,128]{1,0:T(8,128)(2,1)}, bf16[1024,128]{1,0:T(8,128)(2,1)S(1)}, u32[]{:S(2)}, u32[]{:S(2)}) collective-permute-start(bf16[1024,128]{1,0:T(8,128)(2,1)} %x_ref.1), channel_id=1, source_target_pairs={{0,4},{4,0},{8,12},{12,8},{16,20},{20,16},{24,28},{28,24},{1,5},{5... | collective-permute-start | bytes 786440 | tf_op jit(solution)/shard_map/ppermute | solution.py:23
  1.1 7.2 %collective-permute-start.1 = (bf16[1024,128]{1,0:T(8,128)(2,1)}, bf16[1024,128]{1,0:T(8,128)(2,1)S(1)}, u32[]{:S(2)}, u32[]{:S(2)}) collective-permute-start(bf16[1024,128]{1,0:T(8,128)(2,1)} %x_ref.1), channel_id=1, source_target_pairs={{0,8},{4,20},{8,0},{12,28},{16,24},{20,4},{24,16},{28,12},{1,9},{5... | collective-permute-start | bytes 786440 | tf_op jit(solution)/shard_map/ppermute | solution.py:28
  3.7 1.0 %copy-start = (bf16[1024,128]{1,0:T(8,128)(2,1)S(1)}, bf16[1024,128]{1,0:T(8,128)(2,1)}, u32[]{:S(2)}) copy-start(bf16[1024,128]{1,0:T(8,128)(2,1)} %x_ref.1) | copy-start | bytes 786436
  4.9 1.0 %copy-start.1 = (bf16[1024,128]{1,0:T(8,128)(2,1)S(1)}, bf16[1024,128]{1,0:T(8,128)(2,1)}, u32[]{:S(2)}) copy-start(bf16[1024,128]{1,0:T(8,128)(2,1)} %x_ref.1) | copy-start | bytes 786436
  5.8 6.8 %collective-permute-start.3 = (bf16[1024,128]{1,0:T(8,128)(2,1)S(1)}, bf16[1024,128]{1,0:T(8,128)(2,1)S(1)}, u32[]{:S(2)}, u32[]{:S(2)}) collective-permute-start(bf16[1024,128]{1,0:T(8,128)(2,1)S(1)} %copy-done.1), channel_id=1, source_target_pairs={{0,16},{4,12},{8,24},{12,4},{16,0},{20,28},{24,8},{28,20},{1,17},{... | collective-permute-start | bytes 786440 | tf_op jit(solution)/shard_map/ppermute | solution.py:28
  8.4 5.3 %collective-permute-start.2 = (bf16[1024,128]{1,0:T(8,128)(2,1)S(1)}, bf16[1024,128]{1,0:T(8,128)(2,1)S(1)}, u32[]{:S(2)}, u32[]{:S(2)}) collective-permute-start(bf16[1024,128]{1,0:T(8,128)(2,1)S(1)} %collective-permute-done.1.refs_1_.near_ref), channel_id=1, source_target_pairs={{0,4},{4,0},{8,12},{12,8},{16,20},{20,16},{24,28},{28,24},{1,5},{5... | collective-permute-start | bytes 786440 | tf_op jit(solution)/shard_map/ppermute | solution.py:23
  9.4 12.6 %collective-permute-start.5 = (bf16[1024,128]{1,0:T(8,128)(2,1)S(1)}, bf16[1024,128]{1,0:T(8,128)(2,1)S(1)}, u32[]{:S(2)}, u32[]{:S(2)}) collective-permute-start(bf16[1024,128]{1,0:T(8,128)(2,1)S(1)} %collective-permute-done.1.refs_1_.near_ref), channel_id=1, source_target_pairs={{0,16},{4,12},{8,24},{12,4},{16,0},{20,28},{24,8},{28,20},{1,17},{... | collective-permute-start | bytes 786440 | tf_op jit(solution)/shard_map/ppermute | solution.py:28
  12.7 1.5 %collective-permute-start.4 = (bf16[1024,128]{1,0:T(8,128)(2,1)S(1)}, bf16[1024,128]{1,0:T(8,128)(2,1)S(1)}, u32[]{:S(2)}, u32[]{:S(2)}) collective-permute-start(bf16[1024,128]{1,0:T(8,128)(2,1)S(1)} %collective-permute-done.3.refs_1_.cross_ref), channel_id=1, source_target_pairs={{0,4},{4,0},{8,12},{12,8},{16,20},{20,16},{24,28},{28,24},{1,5},{5... | collective-permute-start | bytes 786440 | tf_op jit(solution)/shard_map/ppermute | solution.py:23
  17.3 1.2 %collective-permute-start.6 = (f32[32,128]{1,0:T(8,128)S(1)}, f32[32,128]{1,0:T(8,128)S(1)}, u32[]{:S(2)}, u32[]{:S(2)}) collective-permute-start(f32[32,128]{1,0:T(8,128)S(1)} %between.1.own_ref), channel_id=1, source_target_pairs={{0,4},{4,0},{8,12},{12,8},{16,20},{20,16},{24,28},{28,24},{1,5},{5... | collective-permute-start | bytes 49160 | tf_op jit(solution)/shard_map/ppermute | solution.py:23
  18.5 6.0 %collective-permute-start.8 = (f32[64,128]{1,0:T(8,128)S(1)}, f32[64,128]{1,0:T(8,128)S(1)}, u32[]{:S(2)}, u32[]{:S(2)}) collective-permute-start(f32[64,128]{1,0:T(8,128)S(1)} %pack.1.refs_16_), channel_id=1, source_target_pairs={{0,24},{4,28},{8,16},{12,20},{16,8},{20,12},{24,0},{28,4},{1,25},{... | collective-permute-start | bytes 98312 | tf_op jit(solution)/shard_map/ppermute | solution.py:23
  19.9 4.6 %collective-permute-start.9 = (f32[64,128]{1,0:T(8,128)S(1)}, f32[64,128]{1,0:T(8,128)S(1)}, u32[]{:S(2)}, u32[]{:S(2)}) collective-permute-start(f32[64,128]{1,0:T(8,128)S(1)} %pack.1.refs_16_), channel_id=1, source_target_pairs={{0,8},{4,12},{8,0},{12,4},{16,24},{20,28},{24,16},{28,20},{1,9},{5... | collective-permute-start | bytes 98312 | tf_op jit(solution)/shard_map/ppermute | solution.py:23
  21.1 3.9 %collective-permute-start.10 = (f32[64,128]{1,0:T(8,128)S(1)}, f32[64,128]{1,0:T(8,128)S(1)}, u32[]{:S(2)}, u32[]{:S(2)}) collective-permute-start(f32[64,128]{1,0:T(8,128)S(1)} %pack.1.refs_16_), channel_id=1, source_target_pairs={{0,16},{4,20},{8,24},{12,28},{16,0},{20,4},{24,8},{28,12},{1,17},{... | collective-permute-start | bytes 98312 | tf_op jit(solution)/shard_map/ppermute | solution.py:23
  22.0 1.5 %collective-permute-start.7 = (bf16[1024,128]{1,0:T(8,128)(2,1)S(1)}, bf16[1024,128]{1,0:T(8,128)(2,1)S(1)}, u32[]{:S(2)}, u32[]{:S(2)}) collective-permute-start(bf16[1024,128]{1,0:T(8,128)(2,1)S(1)} %collective-permute-done.5.refs_1_), channel_id=1, source_target_pairs={{0,4},{4,0},{8,12},{12,8},{16,20},{20,16},{24,28},{28,24},{1,5},{5... | collective-permute-start | bytes 786440 | tf_op jit(solution)/shard_map/ppermute | solution.py:23

commit v3 on v2

--- a/solution.py
+++ b/solution.py
@@ -26,13 +26,6 @@
 def exchanged(array, even, odd):
     size = lax.axis_size("team")
     return lax.ppermute(array, "team", [(i, i ^ (odd if i % 2 else even)) for i in range(size)])
-
-
-def down(rows):
-    row = lax.broadcasted_iota(jnp.int32, (128, 128), 0)
-    diagonal = row == lax.broadcasted_iota(jnp.int32, (128, 128), 1)
-    wide = [jnp.where(diagonal, rows[g : g + 1, :], 0.0) for g in range(rows.shape[0])]
-    return jnp.concatenate([jnp.broadcast_to(jnp.sum(w, axis=1, keepdims=True), (128, 128)) for w in wide], axis=0)
 
 
 def across(columns):
@@ -76,20 +69,14 @@
     put_rows(rows_ref, x_ref[...].T)
 
 
-def first_kernel(count, start, sums, *refs):
-    rows_ref, x_refs, refs = refs[0], refs[1 : 1 + count], refs[1 + count :]
-    if sums and not start:
-        acc_in, refs = refs[0], refs[1:]
-    e_refs, turned_refs, refs = refs[:count], refs[count : 2 * count], refs[2 * count :]
-    if sums:
-        acc_ref, refs = refs[0], refs[1:]
+def put_tiles(rows_ref, x_refs, e_refs, turned_refs, col_refs, acc_in, acc_ref):
     n = x_refs[0].shape[0]
     block = 256
     for i in range(0, n, block):
         groups = range(i // 128, (i + block) // 128)
-        if sums:
-            totals = [jnp.zeros((8, 128), F32) if start else acc_in[8 * g : 8 * g + 8, :] for g in groups]
-        for x_ref, e_ref, turned_ref, cols in zip(x_refs, e_refs, turned_refs, refs):
+        if acc_ref is not None:
+            totals = [jnp.zeros((8, 128), F32) if acc_in is None else acc_in[8 * g : 8 * g + 8, :] for g in groups]
+        for x_ref, e_ref, turned_ref, cols in zip(x_refs, e_refs, turned_refs, col_refs):
             for j in range(0, n, block):
                 part = slice(j, j + block)
                 if i == 0:
@@ -100,14 +87,27 @@
                 for t, g in enumerate(groups):
                     k = jnp.exp(p[:, t * 128 : (t + 1) * 128])
                     e_ref[part, g * 128 : g * 128 + 128] = k * k
-                    if sums:
+                    if acc_ref is not None:
                         totals[t] = totals[t] + jnp.sum(k.reshape(block // 8, 8, 128), axis=0)
-        if sums:
+        if acc_ref is not None:
             for t, g in enumerate(groups):
                 acc_ref[8 * g : 8 * g + 8, :] = totals[t]
 
 
-def between_kernel(near_ref, cross_ref, near_mate_ref, cross_mate_ref, near_t, cross_t, acc_in, out_ref, rows, cols, x, row_sums):
+def first_kernel(count, start, sums, *refs):
+    rows_ref, x_refs, refs = refs[0], refs[1 : 1 + count], refs[1 + count :]
+    acc_in = acc_ref = None
+    if sums and not start:
+        acc_in, refs = refs[0], refs[1:]
+    e_refs, turned_refs, refs = refs[:count], refs[count : 2 * count], refs[2 * count :]
+    if sums:
+        acc_ref, refs = refs[0], refs[1:]
+    put_tiles(rows_ref, x_refs, e_refs, turned_refs, refs, acc_in, acc_ref)
+
+
+def between_kernel(*refs):
+    own_rows, near_ref, cross_ref, near_mate_ref, cross_mate_ref, near_t, cross_t, acc_in, *refs = refs
+    e_ref, turned_ref, out_ref, rows, own_cols, cols, x, row_sums, acc = refs
     me = lax.axis_index("team")
     core, side = me % 2, (me // 2) % 2
     n, width = near_ref.shape
@@ -133,8 +133,9 @@
         part = slice(j, j + block)
         put_columns(cols, part, x[part, :], x[part, :].T)
         row_sums[part, :] = jnp.zeros((block, 128), F32)
+    put_tiles(own_rows, [cross_mate_ref], [e_ref], [turned_ref], [own_cols], acc_in, acc)
     for g in range(groups):
-        out_ref[g : g + 1, :] = jnp.sum(acc_in[8 * g : 8 * g + 8, :], axis=0, keepdims=True)
+        out_ref[g : g + 1, :] = jnp.sum(acc[8 * g : 8 * g + 8, :], axis=0, keepdims=True)
     for i in range(0, n, block):
         totals = [jnp.zeros((8, 128), F32) for _ in range(block // 128)]
         for j in range(0, n, block):
@@ -149,76 +150,95 @@
         for t, total in enumerate(totals):
             g = groups + i // 128 + t
             out_ref[g : g + 1, :] = jnp.sum(total, axis=0, keepdims=True)
-    other = jnp.concatenate(across(row_sums[...]), axis=0)
-    zero = jnp.zeros_like(other)
-    out_ref[2 * groups : 3 * groups, :] = jnp.where(side == 0, other, zero)
-    out_ref[3 * groups :, :] = jnp.where(side == 1, other, zero)
-
-
-def pack_kernel(own_ref, mate_ref, both_ref):
-    g = own_ref.shape[0]
-    both_ref[:g, :] = own_ref[...]
-    both_ref[g:, :] = mate_ref[...]
+    out_ref[2 * groups :, :] = jnp.concatenate(across(row_sums[...]), axis=0)
+
+
+def pack_kernel(*refs):
+    step = refs[0].shape[0]
+    for t, ref in enumerate(refs[:-1]):
+        refs[-1][t * step : (t + 1) * step, :] = ref[...]
+
+
+PARTS = (((0,), (1, 2)), ((1, 2), (3, 4, 5)), ((3, 4, 5), (6, 7)), ((6, 7), ()))
 
 
 def second_kernel(points, masks, *refs):
     count = len(masks)
     e_refs, refs = refs[:count], refs[count:]
     x_refs, refs = refs[:count], refs[count:]
-    packs, refs = refs[: count // 2], refs[count // 2 :]
-    own_ref, pot_hbm, out_hbm, scales, pot_ref, out_ref, sems = refs
+    pack_refs, refs = refs[:4], refs[4:]
+    own_ref, pot_hbm, out_hbm, shares_ref, scales, num_ref, acc_ref, pot_ref, out_ref, sems = refs
     width, n = x_refs[0].shape
     groups = n // 128
     block = 256
-    core = lax.axis_index("team") % 2
+    team = lax.axis_index("team")
+    core, side = team % 2, team // 2 % 2
 
     def message(mask, slot):
-        first = (mask % 2 * 4 + slot) * groups
-        return packs[(0, 2, 3, 1)[mask // 2]][first : first + groups, :]
+        first = (mask % 2 * 3 + slot) * groups
+        return pack_refs[(3, 1, 2, 0)[mask // 2]][first : first + groups, :]
 
     def first_sum(mask):
-        near = message(mask ^ 2, 1) + message(mask ^ 4, 2)
-        return message(mask, 0) + near + message(mask ^ 5, 3)
+        near = message(mask, 0) + message(mask ^ 2, 1)
+        return near + jnp.where(side == mask // 2 % 2, message(mask ^ 4, 2), message(mask ^ 5, 2))
+
+    sums = [first_sum(mask) for mask in range(count)]
+    order = [sums[even] if even == odd else jnp.where(core == 0, sums[even], sums[odd]) for even, odd in masks]
+    shares = float(points) / jnp.concatenate(order, axis=0)
+    shares_ref[...] = jnp.concatenate([shares, jnp.zeros((128 - count * groups, 128), F32)], axis=0).T
 
     def put_scales(t):
-        even, odd = masks[t]
-        total = first_sum(even) if even == odd else jnp.where(core == 0, first_sum(even), first_sum(odd))
-        scales[t * n : (t + 1) * n, :] = down(float(points) / total)
-
-    copies = []
+        for g in range(groups):
+            first = t * n + g * 128
+            lane = t * groups + g
+            scales[first : first + 128, :] = jnp.broadcast_to(shares_ref[:, lane : lane + 1], (128, 128))
+
+    def part(tiles, ahead):
+        start = tiles[0] == 0
+        for t in ahead:
+            put_scales(t)
+        for i in range(0, n, block):
+            cols = slice(i, i + block)
+            lanes = range(i, i + block, 128)
+            numerator = jnp.zeros((width, block), F32) if start else num_ref[:, cols]
+            totals = [jnp.zeros((8, 128), F32) if start else acc_ref[l // 16 : l // 16 + 8, :] for l in lanes]
+            for t in tiles:
+                for j in range(0, n, block):
+                    scale = scales[t * n + j : t * n + j + block, :]
+                    weights = []
+                    for u, l in enumerate(lanes):
+                        w = e_refs[t][j : j + block, l : l + 128] * scale
+                        totals[u] = totals[u] + jnp.sum(w.reshape(block // 8, 8, 128), axis=0)
+                        weights.append(w.astype(BF16))
+                    weight = jnp.concatenate(weights, axis=1)
+                    numerator = numerator + jnp.dot(x_refs[t][:, j : j + block], weight, preferred_element_type=F32)
+            for u, l in enumerate(lanes):
+                acc_ref[l // 16 : l // 16 + 8, :] = totals[u]
+            num_ref[:, cols] = numerator
+
+    def out_copy(i):
+        rows = slice(i * block, (i + 1) * block)
+        return pltpu.make_async_copy(out_ref.at[rows, :], out_hbm.at[rows, :], sems.at[i])
+
+    put_scales(0)
+    for tiles, ahead in PARTS:
+        pl.when(team >= 0)(functools.partial(part, tiles, ahead))
     seconds = []
-    for i in range(0, n, block):
-        lanes = range(i, i + block, 128)
-        cols = slice(i, i + block)
-        numerator = jnp.zeros((width, block), F32)
-        totals = [jnp.zeros((8, 128), F32) for _ in lanes]
-        for t in range(count):
-            if i == 0:
-                put_scales(t)
-            for j in range(0, n, block):
-                scale = scales[t * n + j : t * n + j + block, :]
-                weights = []
-                for u, l in enumerate(lanes):
-                    w = e_refs[t][j : j + block, l : l + 128] * scale
-                    totals[u] = totals[u] + jnp.sum(w.reshape(block // 8, 8, 128), axis=0)
-                    weights.append(w.astype(BF16))
-                weight = jnp.concatenate(weights, axis=1)
-                numerator = numerator + jnp.dot(x_refs[t][:, j : j + block], weight, preferred_element_type=F32)
-        for u, l in enumerate(lanes):
-            second = jnp.sum(totals[u], axis=0, keepdims=True)
-            seconds.append(second)
-            image = (numerator[:, u * 128 : (u + 1) * 128] / second).T
-            out_ref[l : l + 128, :] = own_ref[l : l + 128, :].astype(F32) - image
-        copies.append(pltpu.make_async_copy(out_ref.at[cols, :], out_hbm.at[cols, :], sems.at[len(copies)]))
-        copies[-1].start()
+    for g in range(groups):
+        rows = slice(g * 128, (g + 1) * 128)
+        seconds.append(jnp.sum(acc_ref[8 * g : 8 * g + 8, :], axis=0, keepdims=True))
+        out_ref[rows, :] = own_ref[rows, :].astype(F32) - (num_ref[:, rows] / seconds[-1]).T
+        if (g + 1) * 128 % block == 0:
+            out_copy(g * 128 // block).start()
     log_count = jnp.log(jnp.float32(points))
     second = jnp.concatenate(seconds, axis=0)
-    pot_one = -2.0 * (jnp.log(first_sum(0)) - log_count)
+    pot_one = -2.0 * (jnp.log(sums[0]) - log_count)
     pot_ref[...] = 0.5 * (pot_one - 2.0 * (jnp.log(second) - log_count))
-    copies.append(pltpu.make_async_copy(pot_ref, pot_hbm, sems.at[len(copies)]))
-    copies[-1].start()
-    for copy in copies:
-        copy.wait()
+    pot_copy = pltpu.make_async_copy(pot_ref, pot_hbm, sems.at[n // block])
+    pot_copy.start()
+    for i in range(n // block):
+        out_copy(i).wait()
+    pot_copy.wait()
 
 
 def shards(points):
@@ -279,26 +299,28 @@
     first(dict(near=near))
     diagonal = exchanged(after(near), 4, 2)
     cross_mate = swapped(cross, 1)
-    first(dict(cross=cross))
-    first(dict(near_mate=near_mate, cross_mate=cross_mate))
-    sums = call(
+    first(dict(cross=cross, near_mate=near_mate))
+    e, turned, sums = call(
         between_kernel,
-        tile((4 * groups, 128)),
-        [near, cross, near_mate, cross_mate, done["near"][1], done["cross"][1], acc],
+        (tile((n, n)), tile((width, n), BF16), tile((3 * groups, 128))),
+        [rows, near, cross, near_mate, cross_mate, done["near"][1], done["cross"][1], acc],
         scratch=[
             pltpu.VMEM((2 * width, n), BF16),
             pltpu.VMEM((n, 2 * width), BF16),
+            pltpu.VMEM((n, 2 * width), BF16),
             pltpu.VMEM((n, width), BF16),
             pltpu.VMEM((n, 128), F32),
+            pltpu.VMEM((8 * groups, 128), F32),
         ],
         name="between",
-        tiles=1,
-    )
+        tiles=2,
+    )
+    done["cross_mate"] = (e, turned)
     mate_sums = swapped(sums, 1)
-    both = call(pack_kernel, tile((8 * groups, 128)), [sums, mate_sums], name="pack")
-    far, *packs = [swapped(both, m) for m in (6, 2, 4)]
-    packs = [both, far, *packs]
-    diagonal, both = lax.optimization_barrier((diagonal, both))
+    pack = call(pack_kernel, tile((6 * groups, 128)), [sums, mate_sums], name="pack")
+    x, y, far = [swapped(pack, m) for m in (2, 4, 6)]
+    packs = [far, x, y, pack]
+    diagonal, pack = lax.optimization_barrier((diagonal, pack))
     diagonal_mate = swapped(diagonal, 1)
     first(dict(diagonal=diagonal), sums=False)
     first(dict(diagonal_mate=diagonal_mate), sums=False)
@@ -317,7 +339,10 @@
         (jax.ShapeDtypeStruct((groups, 128), F32), jax.ShapeDtypeStruct((n, width), F32)),
         [done[b][0] for b in masks] + [done[b][1] for b in masks] + packs + [own],
         scratch=[
+            pltpu.VMEM((128, 128), F32),
             pltpu.VMEM((len(masks) * n, 128), F32),
+            pltpu.VMEM((width, n), F32),
+            pltpu.VMEM((8 * groups, 128), F32),
             pltpu.VMEM((groups, 128), F32),
             pltpu.VMEM((n, width), F32),
             pltpu.SemaphoreType.DMA((chunks + 1,)),

time: 30.4 us -> 29.7 us (0.977)
  waiting for transfers between devices: 2.79 us -> 2.02 us
  starting transfers between devices: 11.7 us -> 12.1 us
    ppermute x8, waiting for transfers between devices: 2.79 us -> 2.02 us  [swapped(): return lax.ppermute(array, 'team', [(i, i ^ mask) for i in range(size)])]
    ppermute x8, starting transfers between devices: 4.28 us -> 4.66 us  [swapped(): return lax.ppermute(array, 'team', [(i, i ^ mask) for i in range(size)])]
    pallas_call x11 -> x10, Pallas kernels: 13.8 us -> 13.5 us  [call(): pl.pallas_call(kernel, out_shape=out_shape, in_specs=[IN_VMEM] * len(args...]
where the time goes in v3:
time: 29.7 us; the launch traced here: 29.5 us
  Pallas kernels  13.5 us (45%)
  starting transfers between devices  12.1 us (41%)
  waiting for transfers between devices  2.02 us (7%)
  local copies, waits for them, and re-layouts  0.99 us (3%)
  between operations  0.91 us (3%)
    pallas_call x10, Pallas kernels, call(): pl.pallas_call(kernel, out_shape=out_shape, in_specs=[IN_VMEM] * len(args...  13.5 us
    ppermute x3, starting transfers between devices, exchanged(): lax.ppermute(array, 'team', [(i, i ^ (odd if i % 2 else even)) for i in r...  7.42 us
    ppermute x8, starting transfers between devices, swapped(): return lax.ppermute(array, 'team', [(i, i ^ mask) for i in range(size)])  4.66 us
    ppermute x8, waiting for transfers between devices, swapped(): return lax.ppermute(array, 'team', [(i, i ^ mask) for i in range(size)])  2.02 us
    unnamed x4, local copies, waits for them, and re-layouts  0.99 us
  transfers between devices with their start and end apart: 11, of which 4 were waited for; matrix products, arithmetic and copies ran while one was open for 0% of the time, Pallas kernels for 29%

profile of v3, /device:TPU:0, one launch (start us, length us, event | category | flops | bytes accessed | tf_op | source)
XLA Modules:
  0.0 29.5 jit_solution(17734822029166104970)
XLA Ops:
  0.6 0.5 %collective-permute-start = (bf16[1024,128]{1,0:T(8,128)(2,1)}, bf16[1024,128]{1,0:T(8,128)(2,1)S(1)}, u32[]{:S(2)}, u32[]{:S(2)}) collective-permute-start(bf16[1024,128]{1,0:T(8,128)(2,1)} %x_ref.1), channel_id=1, source_target_pairs={{0,4},{4,0},{8,12},{12,8},{16,20},{20,16},{24,28},{28,24},{1,5},{5... | collective-permute-start | bytes 786440 | tf_op jit(solution)/shard_map/ppermute | solution.py:23
  1.1 2.6 %collective-permute-start.1 = (bf16[1024,128]{1,0:T(8,128)(2,1)}, bf16[1024,128]{1,0:T(8,128)(2,1)S(1)}, u32[]{:S(2)}, u32[]{:S(2)}) collective-permute-start(bf16[1024,128]{1,0:T(8,128)(2,1)} %x_ref.1), channel_id=1, source_target_pairs={{0,8},{4,20},{8,0},{12,28},{16,24},{20,4},{24,16},{28,12},{1,9},{5... | collective-permute-start | bytes 786440 | tf_op jit(solution)/shard_map/ppermute | solution.py:28
  3.7 0.0 copy-start
  3.7 1.0 %copy-done = bf16[1024,128]{1,0:T(8,128)(2,1)S(1)} copy-done((bf16[1024,128]{1,0:T(8,128)(2,1)S(1)}, bf16[1024,128]{1,0:T(8,128)(2,1)}, u32[]{:S(2)}) %copy-start) | copy-done | bytes 262168
  4.7 0.2 rows.1
  4.9 0.0 copy-start.1
  4.9 0.9 %first.6 = (f32[1024,1024]{1,0:T(8,128)S(1)}, bf16[128,1024]{1,0:T(8,128)(2,1)S(1)}, f32[64,128]{1,0:T(8,128)S(1)}) custom-call(bf16[256,1024]{1,0:T(8,128)(2,1)S(1)} %get-tuple-element.34.refs_0_, bf16[1024,128]{1,0:T(8,128)(2,1)S(1)} %get-tuple-element.35.refs_1_.refs_20_), custom_call_target="tpu_custom_call" | custom-call | flops 3221225472 | tf_op jit(solution)/shard_map/first/pallas_call | solution.py:256
  5.8 0.0 copy-done.1
  5.8 1.6 %collective-permute-start.2 = (bf16[1024,128]{1,0:T(8,128)(2,1)S(1)}, bf16[1024,128]{1,0:T(8,128)(2,1)S(1)}, u32[]{:S(2)}, u32[]{:S(2)}) collective-permute-start(bf16[1024,128]{1,0:T(8,128)(2,1)S(1)} %copy-done.1), channel_id=1, source_target_pairs={{0,16},{4,12},{8,24},{12,4},{16,0},{20,28},{24,8},{28,20},{1,17},{... | collective-permute-start | bytes 786440 | tf_op jit(solution)/shard_map/ppermute | solution.py:28
  7.4 0.0 collective-permute-done.refs_1_
  7.4 0.9 %first.7 = (f32[1024,1024]{1,0:T(8,128)S(1)}, bf16[128,1024]{1,0:T(8,128)(2,1)S(1)}, f32[64,128]{1,0:T(8,128)S(1)}) custom-call(bf16[256,1024]{1,0:T(8,128)(2,1)S(1)} %get-tuple-element.34.refs_0_, bf16[1024,128]{1,0:T(8,128)(2,1)S(1)} %collective-permute-done.refs_1_, f32[64,128]{1,0:T(8,128)S(1)} %get-tuple-element.38.refs_2_), custom_call_target="tpu_custom_call" | custom-call | flops 3221225472 | tf_op jit(solution)/shard_map/first/pallas_call | solution.py:256
  8.4 0.0 collective-permute-done.1.refs_1_
  8.4 0.1 collective-permute-start.3
  8.4 0.9 %first.8 = (f32[1024,1024]{1,0:T(8,128)S(1)}, bf16[128,1024]{1,0:T(8,128)(2,1)S(1)}, f32[64,128]{1,0:T(8,128)S(1)}) custom-call(bf16[256,1024]{1,0:T(8,128)(2,1)S(1)} %get-tuple-element.34.refs_0_, bf16[1024,128]{1,0:T(8,128)(2,1)S(1)} %collective-permute-done.1.refs_1_, f32[64,128]{1,0:T(8,128)S(1)} %get-tuple-element.42.refs_2_), custom_call_target="tpu_custom_call" | custom-call | flops 3221225472 | tf_op jit(solution)/shard_map/first/pallas_call | solution.py:256
  9.4 3.3 %collective-permute-start.5 = (bf16[1024,128]{1,0:T(8,128)(2,1)S(1)}, bf16[1024,128]{1,0:T(8,128)(2,1)S(1)}, u32[]{:S(2)}, u32[]{:S(2)}) collective-permute-start(bf16[1024,128]{1,0:T(8,128)(2,1)S(1)} %collective-permute-done.1.refs_1_), channel_id=1, source_target_pairs={{0,16},{4,12},{8,24},{12,4},{16,0},{20,28},{24,8},{28,20},{1,17},{... | collective-permute-start | bytes 786440 | tf_op jit(solution)/shard_map/ppermute | solution.py:28
  12.7 0.0 collective-permute-done.2.refs_1_.refs_2_
  12.7 0.0 collective-permute-start.4
  12.7 0.0 collective-permute-done.3.refs_2_.refs_3_
  12.7 1.7 %first.9 = (f32[1024,1024]{1,0:T(8,128)S(1)}, f32[1024,1024]{1,0:T(8,128)S(1)}, bf16[128,1024]{1,0:T(8,128)(2,1)S(1)}, bf16[128,1024]{1,0:T(8,128)(2,1)S(1)}, f32[64,128]{1,0:T(8,128)S(1)}) custom-call(bf16[256,1024]{1,0:T(8,128)(2,1)S(1)} %get-tuple-element.34.refs_0_, bf16[1024,128]{1,0:T(8,128)(2,1)S(1)} %collective-permute-done.2.refs_1_.refs_2_, ...), custom_call_target="tpu_custom_call" | custom-call | flops 6442450944 | tf_op jit(solution)/shard_map/first/pallas_call | solution.py:256
  14.4 0.0 collective-permute-done.4.refs_4_
  14.4 2.0 %between.1 = (f32[1024,1024]{1,0:T(8,128)S(1)}, bf16[128,1024]{1,0:T(8,128)(2,1)S(1)}, f32[24,128]{1,0:T(8,128)S(1)}) custom-call(bf16[256,1024]{1,0:T(8,128)(2,1)S(1)} %get-tuple-element.34.refs_0_, bf16[1024,128]{1,0:T(8,128)(2,1)S(1)} %collective-permute-done.1.refs_1_, bf16[1024,128]{1,0:T(8,128)(2,1)S(1)} %collective-permute-done.2.refs_1_.refs_2_, ...), custom_call_target="tpu_custom_call" | custom-call | flops 6442450944 | tf_op jit(solution)/shard_map/between/pallas_call | solution.py:256
  16.4 0.6 %collective-permute-start.6 = (f32[24,128]{1,0:T(8,128)S(1)}, f32[24,128]{1,0:T(8,128)S(1)}, u32[]{:S(2)}, u32[]{:S(2)}) collective-permute-start(f32[24,128]{1,0:T(8,128)S(1)} %get-tuple-element.54.refs_0_), channel_id=1, source_target_pairs={{0,4},{4,0},{8,12},{12,8},{16,20},{20,16},{24,28},{28,24},{1,5},{5... | collective-permute-start | bytes 36872 | tf_op jit(solution)/shard_map/ppermute | solution.py:23
  17.0 0.8 %collective-permute-done.6.refs_1_ = f32[24,128]{1,0:T(8,128)S(1)} collective-permute-done((f32[24,128]{1,0:T(8,128)S(1)}, f32[24,128]{1,0:T(8,128)S(1)}, u32[]{:S(2)}, u32[]{:S(2)}) %collective-permute-start.6) | collective-permute-done | bytes 12320 | tf_op jit(solution)/shard_map/ppermute | solution.py:23
  17.8 1.3 %collective-permute-start.10 = (f32[48,128]{1,0:T(8,128)S(1)}, f32[48,128]{1,0:T(8,128)S(1)}, u32[]{:S(2)}, u32[]{:S(2)}) collective-permute-start(f32[48,128]{1,0:T(8,128)S(1)} %pack.1.refs_19_), channel_id=1, source_target_pairs={{0,16},{4,20},{8,24},{12,28},{16,0},{20,4},{24,8},{28,12},{1,17},{... | collective-permute-start | bytes 73736 | tf_op jit(solution)/shard_map/ppermute | solution.py:23
  19.1 1.4 %collective-permute-start.8 = (f32[48,128]{1,0:T(8,128)S(1)}, f32[48,128]{1,0:T(8,128)S(1)}, u32[]{:S(2)}, u32[]{:S(2)}) collective-permute-start(f32[48,128]{1,0:T(8,128)S(1)} %pack.1.refs_19_), channel_id=1, source_target_pairs={{0,24},{4,28},{8,16},{12,20},{16,8},{20,12},{24,0},{28,4},{1,25},{... | collective-permute-start | bytes 73736 | tf_op jit(solution)/shard_map/ppermute | solution.py:23
  20.5 0.8 %collective-permute-start.9 = (f32[48,128]{1,0:T(8,128)S(1)}, f32[48,128]{1,0:T(8,128)S(1)}, u32[]{:S(2)}, u32[]{:S(2)}) collective-permute-start(f32[48,128]{1,0:T(8,128)S(1)} %pack.1.refs_19_), channel_id=1, source_target_pairs={{0,8},{4,12},{8,0},{12,4},{16,24},{20,28},{24,16},{28,20},{1,9},{5... | collective-permute-start | bytes 73736 | tf_op jit(solution)/shard_map/ppermute | solution.py:23
  21.3 0.0 collective-permute-done.5.refs_1_
  21.3 0.0 collective-permute-start.7
  21.3 0.9 %first.10 = (f32[1024,1024]{1,0:T(8,128)S(1)}, bf16[128,1024]{1,0:T(8,128)(2,1)S(1)}) custom-call(bf16[256,1024]{1,0:T(8,128)(2,1)S(1)} %get-tuple-element.34.refs_0_, bf16[1024,128]{1,0:T(8,128)(2,1)S(1)} %collective-permute-done.5.refs_1_), custom_call_target="tpu_custom_call" | custom-call | flops 3221225472 | tf_op jit(solution)/shard_map/first/pallas_call | solution.py:256
  22.3 0.6 %collective-permute-done.7.refs_1_ = bf16[1024,128]{1,0:T(8,128)(2,1)S(1)} collective-permute-done((bf16[1024,128]{1,0:T(8,128)(2,1)S(1)}, bf16[1024,128]{1,0:T(8,128)(2,1)S(1)}, u32[]{:S(2)}, u32[]{:S(2)}) %collective-permute-start.7) | collective-permute-done | bytes 262176 | tf_op jit(solution)/shard_map/ppermute | solution.py:23
  22.9 0.9 %first.11 = (f32[1024,1024]{1,0:T(8,128)S(1)}, bf16[128,1024]{1,0:T(8,128)(2,1)S(1)}) custom-call(bf16[256,1024]{1,0:T(8,128)(2,1)S(1)} %get-tuple-element.34.refs_0_, bf16[1024,128]{1,0:T(8,128)(2,1)S(1)} %collective-permute-done.7.refs_1_), custom_call_target="tpu_custom_call" | custom-call | flops 3221225472 | tf_op jit(solution)/shard_map/first/pallas_call | solution.py:256
  23.8 0.0 collective-permute-done.10.refs_18_
  23.8 0.1 collective-permute-done.8.refs_16_
  23.9 0.5 %collective-permute-done.9.refs_17_ = f32[48,128]{1,0:T(8,128)S(1)} collective-permute-done((f32[48,128]{1,0:T(8,128)S(1)}, f32[48,128]{1,0:T(8,128)S(1)}, u32[]{:S(2)}, u32[]{:S(2)}) %collective-permute-start.9) | collective-permute-done | bytes 24608 | tf_op jit(solution)/shard_map/ppermute | solution.py:23
  24.4 5.0 %second.1 = (f32[8,128]{1,0:T(8,128)}, f32[1024,128]{1,0:T(8,128)}) custom-call(f32[1024,1024]{1,0:T(8,128)S(1)} %get-tuple-element.36.refs_0_, f32[1024,1024]{1,0:T(8,128)S(1)} %get-tuple-element.39.refs_1_, f32[1024,1024]{1,0:T(8,128)S(1)} %get-tuple-element.43.refs_2_, f32[1024,1024]{1,0:T(8,128)S(1)} %get-tuple-element.50.refs_3_, ...), custom_call_target="tpu_custom_call" | custom-call | flops 25769803776 | tf_op jit(solution)/shard_map/second/pallas_call | solution.py:256
  (1 shorter events, 0.0 us)
Async XLA Ops:
  0.6 6.8 %collective-permute-start = (bf16[1024,128]{1,0:T(8,128)(2,1)}, bf16[1024,128]{1,0:T(8,128)(2,1)S(1)}, u32[]{:S(2)}, u32[]{:S(2)}) collective-permute-start(bf16[1024,128]{1,0:T(8,128)(2,1)} %x_ref.1), channel_id=1, source_target_pairs={{0,4},{4,0},{8,12},{12,8},{16,20},{20,16},{24,28},{28,24},{1,5},{5... | collective-permute-start | bytes 786440 | tf_op jit(solution)/shard_map/ppermute | solution.py:23
  1.1 7.2 %collective-permute-start.1 = (bf16[1024,128]{1,0:T(8,128)(2,1)}, bf16[1024,128]{1,0:T(8,128)(2,1)S(1)}, u32[]{:S(2)}, u32[]{:S(2)}) collective-permute-start(bf16[1024,128]{1,0:T(8,128)(2,1)} %x_ref.1), channel_id=1, source_target_pairs={{0,8},{4,20},{8,0},{12,28},{16,24},{20,4},{24,16},{28,12},{1,9},{5... | collective-permute-start | bytes 786440 | tf_op jit(solution)/shard_map/ppermute | solution.py:28
  3.7 1.0 %copy-start = (bf16[1024,128]{1,0:T(8,128)(2,1)S(1)}, bf16[1024,128]{1,0:T(8,128)(2,1)}, u32[]{:S(2)}) copy-start(bf16[1024,128]{1,0:T(8,128)(2,1)} %x_ref.1) | copy-start | bytes 786436
  4.9 1.0 %copy-start.1 = (bf16[1024,128]{1,0:T(8,128)(2,1)S(1)}, bf16[1024,128]{1,0:T(8,128)(2,1)}, u32[]{:S(2)}) copy-start(bf16[1024,128]{1,0:T(8,128)(2,1)} %x_ref.1) | copy-start | bytes 786436
  5.8 6.8 %collective-permute-start.2 = (bf16[1024,128]{1,0:T(8,128)(2,1)S(1)}, bf16[1024,128]{1,0:T(8,128)(2,1)S(1)}, u32[]{:S(2)}, u32[]{:S(2)}) collective-permute-start(bf16[1024,128]{1,0:T(8,128)(2,1)S(1)} %copy-done.1), channel_id=1, source_target_pairs={{0,16},{4,12},{8,24},{12,4},{16,0},{20,28},{24,8},{28,20},{1,17},{... | collective-permute-start | bytes 786440 | tf_op jit(solution)/shard_map/ppermute | solution.py:28
  8.4 4.3 %collective-permute-start.3 = (bf16[1024,128]{1,0:T(8,128)(2,1)S(1)}, bf16[1024,128]{1,0:T(8,128)(2,1)S(1)}, u32[]{:S(2)}, u32[]{:S(2)}) collective-permute-start(bf16[1024,128]{1,0:T(8,128)(2,1)S(1)} %collective-permute-done.1.refs_1_), channel_id=1, source_target_pairs={{0,4},{4,0},{8,12},{12,8},{16,20},{20,16},{24,28},{28,24},{1,5},{5... | collective-permute-start | bytes 786440 | tf_op jit(solution)/shard_map/ppermute | solution.py:23
  9.4 11.9 %collective-permute-start.5 = (bf16[1024,128]{1,0:T(8,128)(2,1)S(1)}, bf16[1024,128]{1,0:T(8,128)(2,1)S(1)}, u32[]{:S(2)}, u32[]{:S(2)}) collective-permute-start(bf16[1024,128]{1,0:T(8,128)(2,1)S(1)} %collective-permute-done.1.refs_1_), channel_id=1, source_target_pairs={{0,16},{4,12},{8,24},{12,4},{16,0},{20,28},{24,8},{28,20},{1,17},{... | collective-permute-start | bytes 786440 | tf_op jit(solution)/shard_map/ppermute | solution.py:28
  12.7 1.7 %collective-permute-start.4 = (bf16[1024,128]{1,0:T(8,128)(2,1)S(1)}, bf16[1024,128]{1,0:T(8,128)(2,1)S(1)}, u32[]{:S(2)}, u32[]{:S(2)}) collective-permute-start(bf16[1024,128]{1,0:T(8,128)(2,1)S(1)} %collective-permute-done.2.refs_1_.refs_2_), channel_id=1, source_target_pairs={{0,4},{4,0},{8,12},{12,8},{16,20},{20,16},{24,28},{28,24},{1,5},{5... | collective-permute-start | bytes 786440 | tf_op jit(solution)/shard_map/ppermute | solution.py:23
  16.4 1.4 %collective-permute-start.6 = (f32[24,128]{1,0:T(8,128)S(1)}, f32[24,128]{1,0:T(8,128)S(1)}, u32[]{:S(2)}, u32[]{:S(2)}) collective-permute-start(f32[24,128]{1,0:T(8,128)S(1)} %get-tuple-element.54.refs_0_), channel_id=1, source_target_pairs={{0,4},{4,0},{8,12},{12,8},{16,20},{20,16},{24,28},{28,24},{1,5},{5... | collective-permute-start | bytes 36872 | tf_op jit(solution)/shard_map/ppermute | solution.py:23
  17.8 6.0 %collective-permute-start.10 = (f32[48,128]{1,0:T(8,128)S(1)}, f32[48,128]{1,0:T(8,128)S(1)}, u32[]{:S(2)}, u32[]{:S(2)}) collective-permute-start(f32[48,128]{1,0:T(8,128)S(1)} %pack.1.refs_19_), channel_id=1, source_target_pairs={{0,16},{4,20},{8,24},{12,28},{16,0},{20,4},{24,8},{28,12},{1,17},{... | collective-permute-start | bytes 73736 | tf_op jit(solution)/shard_map/ppermute | solution.py:23
  19.1 4.7 %collective-permute-start.8 = (f32[48,128]{1,0:T(8,128)S(1)}, f32[48,128]{1,0:T(8,128)S(1)}, u32[]{:S(2)}, u32[]{:S(2)}) collective-permute-start(f32[48,128]{1,0:T(8,128)S(1)} %pack.1.refs_19_), channel_id=1, source_target_pairs={{0,24},{4,28},{8,16},{12,20},{16,8},{20,12},{24,0},{28,4},{1,25},{... | collective-permute-start | bytes 73736 | tf_op jit(solution)/shard_map/ppermute | solution.py:23
  20.5 3.8 %collective-permute-start.9 = (f32[48,128]{1,0:T(8,128)S(1)}, f32[48,128]{1,0:T(8,128)S(1)}, u32[]{:S(2)}, u32[]{:S(2)}) collective-permute-start(f32[48,128]{1,0:T(8,128)S(1)} %pack.1.refs_19_), channel_id=1, source_target_pairs={{0,8},{4,12},{8,0},{12,4},{16,24},{20,28},{24,16},{28,20},{1,9},{5... | collective-permute-start | bytes 73736 | tf_op jit(solution)/shard_map/ppermute | solution.py:23
  21.3 1.5 %collective-permute-start.7 = (bf16[1024,128]{1,0:T(8,128)(2,1)S(1)}, bf16[1024,128]{1,0:T(8,128)(2,1)S(1)}, u32[]{:S(2)}, u32[]{:S(2)}) collective-permute-start(bf16[1024,128]{1,0:T(8,128)(2,1)S(1)} %collective-permute-done.5.refs_1_), channel_id=1, source_target_pairs={{0,4},{4,0},{8,12},{12,8},{16,20},{20,16},{24,28},{28,24},{1,5},{5... | collective-permute-start | bytes 786440 | tf_op jit(solution)/shard_map/ppermute | solution.py:23

commit v4 on v3

--- a/solution.py
+++ b/solution.py
@@ -69,7 +69,7 @@
     put_rows(rows_ref, x_ref[...].T)
 
 
-def put_tiles(rows_ref, x_refs, e_refs, turned_refs, col_refs, acc_in, acc_ref):
+def put_tiles(rows_ref, x_refs, e_refs, turned_refs, col_refs, acc_in, acc_ref, along_ref):
     n = x_refs[0].shape[0]
     block = 256
     for i in range(0, n, block):
@@ -84,30 +84,40 @@
                     turned_ref[:, part] = x_turned
                     put_columns(cols, part, x_ref[part, :], x_turned)
                 p = jnp.dot(cols[part, :], rows_ref[:, i : i + block], preferred_element_type=F32)
+                sideways = along_ref is not None and x_ref is x_refs[-1]
+                along = along_ref[part, :] if sideways and i else jnp.zeros((block, 128), F32)
                 for t, g in enumerate(groups):
                     k = jnp.exp(p[:, t * 128 : (t + 1) * 128])
                     e_ref[part, g * 128 : g * 128 + 128] = k * k
                     if acc_ref is not None:
                         totals[t] = totals[t] + jnp.sum(k.reshape(block // 8, 8, 128), axis=0)
+                    if sideways:
+                        along = along + k
+                if sideways:
+                    along_ref[part, :] = along
         if acc_ref is not None:
             for t, g in enumerate(groups):
                 acc_ref[8 * g : 8 * g + 8, :] = totals[t]
 
 
-def first_kernel(count, start, sums, *refs):
+def first_kernel(count, start, sums, sideways, *refs):
     rows_ref, x_refs, refs = refs[0], refs[1 : 1 + count], refs[1 + count :]
-    acc_in = acc_ref = None
+    acc_in = acc_ref = along_ref = None
     if sums and not start:
         acc_in, refs = refs[0], refs[1:]
     e_refs, turned_refs, refs = refs[:count], refs[count : 2 * count], refs[2 * count :]
     if sums:
         acc_ref, refs = refs[0], refs[1:]
-    put_tiles(rows_ref, x_refs, e_refs, turned_refs, refs, acc_in, acc_ref)
+    if sideways:
+        side_ref, along_ref, refs = refs[0], refs[-1], refs[1:-1]
+    put_tiles(rows_ref, x_refs, e_refs, turned_refs, refs, acc_in, acc_ref, along_ref)
+    if sideways:
+        side_ref[...] = jnp.concatenate(across(along_ref[...]), axis=0)
 
 
 def between_kernel(*refs):
-    own_rows, near_ref, cross_ref, near_mate_ref, cross_mate_ref, near_t, cross_t, acc_in, *refs = refs
-    e_ref, turned_ref, out_ref, rows, own_cols, cols, x, row_sums, acc = refs
+    near_ref, cross_ref, near_mate_ref, cross_mate_ref, near_t, cross_t, acc_in, side_ref, *refs = refs
+    out_ref, rows, cols, x, row_sums = refs
     me = lax.axis_index("team")
     core, side = me % 2, (me // 2) % 2
     n, width = near_ref.shape
@@ -133,9 +143,6 @@
         part = slice(j, j + block)
         put_columns(cols, part, x[part, :], x[part, :].T)
         row_sums[part, :] = jnp.zeros((block, 128), F32)
-    put_tiles(own_rows, [cross_mate_ref], [e_ref], [turned_ref], [own_cols], acc_in, acc)
-    for g in range(groups):
-        out_ref[g : g + 1, :] = jnp.sum(acc[8 * g : 8 * g + 8, :], axis=0, keepdims=True)
     for i in range(0, n, block):
         totals = [jnp.zeros((8, 128), F32) for _ in range(block // 128)]
         for j in range(0, n, block):
@@ -150,7 +157,10 @@
         for t, total in enumerate(totals):
             g = groups + i // 128 + t
             out_ref[g : g + 1, :] = jnp.sum(total, axis=0, keepdims=True)
-    out_ref[2 * groups :, :] = jnp.concatenate(across(row_sums[...]), axis=0)
+    out_ref[2 * groups : 3 * groups, :] = jnp.concatenate(across(row_sums[...]), axis=0)
+    out_ref[3 * groups :, :] = side_ref[...]
+    for g in range(groups):
+        out_ref[g : g + 1, :] = jnp.sum(acc_in[8 * g : 8 * g + 8, :], axis=0, keepdims=True)
 
 
 def pack_kernel(*refs):
@@ -166,7 +176,7 @@
     count = len(masks)
     e_refs, refs = refs[:count], refs[count:]
     x_refs, refs = refs[:count], refs[count:]
-    pack_refs, refs = refs[:4], refs[4:]
+    pack_refs, refs = refs[:5], refs[5:]
     own_ref, pot_hbm, out_hbm, shares_ref, scales, num_ref, acc_ref, pot_ref, out_ref, sems = refs
     width, n = x_refs[0].shape
     groups = n // 128
@@ -175,12 +185,15 @@
     core, side = team % 2, team // 2 % 2
 
     def message(mask, slot):
-        first = (mask % 2 * 3 + slot) * groups
-        return pack_refs[(3, 1, 2, 0)[mask // 2]][first : first + groups, :]
+        if mask >= 6:
+            return pack_refs[mask - 6][slot * groups : (slot + 1) * groups, :]
+        first = (mask % 2 * 4 + slot) * groups
+        return pack_refs[(4, 2, 3)[mask // 2]][first : first + groups, :]
 
     def first_sum(mask):
         near = message(mask, 0) + message(mask ^ 2, 1)
-        return near + jnp.where(side == mask // 2 % 2, message(mask ^ 4, 2), message(mask ^ 5, 2))
+        near = near + jnp.where(side == mask // 2 % 2, message(mask ^ 4, 2), message(mask ^ 5, 2))
+        return near + jnp.where(core == mask % 2, message(mask ^ 3, 3), message(mask ^ 5, 3))
 
     sums = [first_sum(mask) for mask in range(count)]
     order = [sums[even] if even == odd else jnp.where(core == 0, sums[even], sums[odd]) for even, odd in masks]
@@ -267,21 +280,25 @@
     acc = None
     done = {}
 
-    def first(blocks, sums=True):
+    def first(blocks, sums=True, sideways=False):
         nonlocal acc
         count = len(blocks)
         out = call(
-            functools.partial(first_kernel, count, acc is None, sums),
-            (tile((n, n)),) * count + (tile((width, n), BF16),) * count + (tile((8 * groups, 128)),) * sums,
+            functools.partial(first_kernel, count, acc is None, sums, sideways),
+            (tile((n, n)),) * count
+            + (tile((width, n), BF16),) * count
+            + (tile((8 * groups, 128)),) * sums
+            + (tile((groups, 128)),) * sideways,
             [rows, *blocks.values()] + ([acc] if sums and acc is not None else []),
-            scratch=[pltpu.VMEM((n, 2 * width), BF16)] * count,
+            scratch=[pltpu.VMEM((n, 2 * width), BF16)] * count + [pltpu.VMEM((n, 128), F32)] * sideways,
             name="first",
             tiles=count,
         )
         for t, block in enumerate(blocks):
             done[block] = (out[t], out[count + t])
         if sums:
-            acc = out[-1]
+            acc = out[2 * count]
+        return out[-1]
 
     def after(x):
         nonlocal acc
@@ -299,31 +316,32 @@
     first(dict(near=near))
     diagonal = exchanged(after(near), 4, 2)
     cross_mate = swapped(cross, 1)
-    first(dict(cross=cross, near_mate=near_mate))
-    e, turned, sums = call(
+    side = first(dict(cross=cross, near_mate=near_mate), sideways=True)
+    sums = call(
         between_kernel,
-        (tile((n, n)), tile((width, n), BF16), tile((3 * groups, 128))),
-        [rows, near, cross, near_mate, cross_mate, done["near"][1], done["cross"][1], acc],
+        tile((4 * groups, 128)),
+        [near, cross, near_mate, cross_mate, done["near"][1], done["cross"][1], acc, side],
         scratch=[
             pltpu.VMEM((2 * width, n), BF16),
             pltpu.VMEM((n, 2 * width), BF16),
-            pltpu.VMEM((n, 2 * width), BF16),
             pltpu.VMEM((n, width), BF16),
             pltpu.VMEM((n, 128), F32),
-            pltpu.VMEM((8 * groups, 128), F32),
         ],
         name="between",
-        tiles=2,
-    )
-    done["cross_mate"] = (e, turned)
+        tiles=1,
+    )
+    far = swapped(sums, 6)
     mate_sums = swapped(sums, 1)
-    pack = call(pack_kernel, tile((6 * groups, 128)), [sums, mate_sums], name="pack")
-    x, y, far = [swapped(pack, m) for m in (2, 4, 6)]
-    packs = [far, x, y, pack]
-    diagonal, pack = lax.optimization_barrier((diagonal, pack))
+    pack = call(pack_kernel, tile((8 * groups, 128)), [sums, mate_sums], name="pack")
+    x, y = [swapped(pack, m) for m in (2, 4)]
+    cross_mate, diagonal, pack = lax.optimization_barrier((cross_mate, diagonal, pack))
     diagonal_mate = swapped(diagonal, 1)
-    first(dict(diagonal=diagonal), sums=False)
+    first(dict(cross_mate=cross_mate, diagonal=diagonal), sums=False)
+    e, far = lax.optimization_barrier((done["diagonal"][0], far))
+    done["diagonal"] = (e, done["diagonal"][1])
+    far_mate = swapped(far, 1)
     first(dict(diagonal_mate=diagonal_mate), sums=False)
+    packs = [far, far_mate, x, y, pack]
     masks = dict(
         own=(0, 0),
         mate=(1, 1),

time: 29.7 us -> 28.4 us (0.956)
  waiting for transfers between devices: 2.02 us -> 0.03 us
  starting transfers between devices: 12.1 us -> 12.6 us
    ppermute x8 -> x9, waiting for transfers between devices: 2.02 us -> 0.02 us  [swapped(): return lax.ppermute(array, 'team', [(i, i ^ mask) for i in range(size)])]
    ppermute x8 -> x9, starting transfers between devices: 4.66 us -> 5.22 us  [swapped(): return lax.ppermute(array, 'team', [(i, i ^ mask) for i in range(size)])]
  transfers between devices with their start and end apart: 11 -> 12, of which waited for: 4 -> 0; matrix products, arithmetic and copies ran while one was open for 0% -> 0% of each run, Pallas kernels for 29% -> 31%
where the time goes in v4:
time: 28.4 us; the launch traced here: 28.2 us
  Pallas kernels  13.7 us (48%)
  starting transfers between devices  12.6 us (44%)
  local copies, waits for them, and re-layouts  0.99 us (3%)
  between operations  0.93 us (3%)
    pallas_call x10, Pallas kernels, call(): pl.pallas_call(kernel, out_shape=out_shape, in_specs=[IN_VMEM] * len(args...  13.7 us
    ppermute x3, starting transfers between devices, exchanged(): lax.ppermute(array, 'team', [(i, i ^ (odd if i % 2 else even)) for i in r...  7.38 us
    ppermute x9, starting transfers between devices, swapped(): return lax.ppermute(array, 'team', [(i, i ^ mask) for i in range(size)])  5.22 us
    unnamed x4, local copies, waits for them, and re-layouts  0.99 us
  transfers between devices with their start and end apart: 12, of which 0 were waited for; matrix products, arithmetic and copies ran while one was open for 0% of the time, Pallas kernels for 31%

profile of v4, /device:TPU:0, one launch (start us, length us, event | category | flops | bytes accessed | tf_op | source)
XLA Modules:
  0.0 28.2 jit_solution(11879764937962274084)
XLA Ops:
  0.6 0.5 %collective-permute-start = (bf16[1024,128]{1,0:T(8,128)(2,1)}, bf16[1024,128]{1,0:T(8,128)(2,1)S(1)}, u32[]{:S(2)}, u32[]{:S(2)}) collective-permute-start(bf16[1024,128]{1,0:T(8,128)(2,1)} %x_ref.1), channel_id=1, source_target_pairs={{0,4},{4,0},{8,12},{12,8},{16,20},{20,16},{24,28},{28,24},{1,5},{5... | collective-permute-start | bytes 786440 | tf_op jit(solution)/shard_map/ppermute | solution.py:23
  1.1 2.6 %collective-permute-start.1 = (bf16[1024,128]{1,0:T(8,128)(2,1)}, bf16[1024,128]{1,0:T(8,128)(2,1)S(1)}, u32[]{:S(2)}, u32[]{:S(2)}) collective-permute-start(bf16[1024,128]{1,0:T(8,128)(2,1)} %x_ref.1), channel_id=1, source_target_pairs={{0,8},{4,20},{8,0},{12,28},{16,24},{20,4},{24,16},{28,12},{1,9},{5... | collective-permute-start | bytes 786440 | tf_op jit(solution)/shard_map/ppermute | solution.py:28
  3.7 0.0 copy-start
  3.7 1.0 %copy-done = bf16[1024,128]{1,0:T(8,128)(2,1)S(1)} copy-done((bf16[1024,128]{1,0:T(8,128)(2,1)S(1)}, bf16[1024,128]{1,0:T(8,128)(2,1)}, u32[]{:S(2)}) %copy-start) | copy-done | bytes 262168
  4.7 0.2 rows.1
  4.9 0.0 copy-start.1
  4.9 1.0 %first.6 = (f32[1024,1024]{1,0:T(8,128)S(1)}, bf16[128,1024]{1,0:T(8,128)(2,1)S(1)}, f32[64,128]{1,0:T(8,128)S(1)}) custom-call(bf16[256,1024]{1,0:T(8,128)(2,1)S(1)} %get-tuple-element.38.refs_0_, bf16[1024,128]{1,0:T(8,128)(2,1)S(1)} %get-tuple-element.39.refs_1_.refs_21_), custom_call_target="tpu_custom_call" | custom-call | flops 3221225472 | tf_op jit(solution)/shard_map/first/pallas_call | solution.py:269
  5.8 0.0 copy-done.1
  5.8 1.6 %collective-permute-start.2 = (bf16[1024,128]{1,0:T(8,128)(2,1)S(1)}, bf16[1024,128]{1,0:T(8,128)(2,1)S(1)}, u32[]{:S(2)}, u32[]{:S(2)}) collective-permute-start(bf16[1024,128]{1,0:T(8,128)(2,1)S(1)} %copy-done.1), channel_id=1, source_target_pairs={{0,16},{4,12},{8,24},{12,4},{16,0},{20,28},{24,8},{28,20},{1,17},{... | collective-permute-start | bytes 786440 | tf_op jit(solution)/shard_map/ppermute | solution.py:28
  7.4 0.0 collective-permute-done.refs_1_
  7.4 0.9 %first.7 = (f32[1024,1024]{1,0:T(8,128)S(1)}, bf16[128,1024]{1,0:T(8,128)(2,1)S(1)}, f32[64,128]{1,0:T(8,128)S(1)}) custom-call(bf16[256,1024]{1,0:T(8,128)(2,1)S(1)} %get-tuple-element.38.refs_0_, bf16[1024,128]{1,0:T(8,128)(2,1)S(1)} %collective-permute-done.refs_1_, f32[64,128]{1,0:T(8,128)S(1)} %get-tuple-element.42.refs_2_), custom_call_target="tpu_custom_call" | custom-call | flops 3221225472 | tf_op jit(solution)/shard_map/first/pallas_call | solution.py:269
  8.4 0.0 collective-permute-done.1.refs_1_.refs_0_
  8.4 0.1 collective-permute-start.5
  8.5 1.0 %first.8 = (f32[1024,1024]{1,0:T(8,128)S(1)}, bf16[128,1024]{1,0:T(8,128)(2,1)S(1)}, f32[64,128]{1,0:T(8,128)S(1)}) custom-call(bf16[256,1024]{1,0:T(8,128)(2,1)S(1)} %get-tuple-element.38.refs_0_, bf16[1024,128]{1,0:T(8,128)(2,1)S(1)} %collective-permute-done.1.refs_1_.refs_0_, f32[64,128]{1,0:T(8,128)S(1)} %get-tuple-element.46.refs_2_), custom_call_target="tpu_custom_call" | custom-call | flops 3221225472 | tf_op jit(solution)/shard_map/first/pallas_call | solution.py:269
  9.4 3.2 %collective-permute-start.4 = (bf16[1024,128]{1,0:T(8,128)(2,1)S(1)}, bf16[1024,128]{1,0:T(8,128)(2,1)S(1)}, u32[]{:S(2)}, u32[]{:S(2)}) collective-permute-start(bf16[1024,128]{1,0:T(8,128)(2,1)S(1)} %collective-permute-done.1.refs_1_.refs_0_), channel_id=1, source_target_pairs={{0,16},{4,12},{8,24},{12,4},{16,0},{20,28},{24,8},{28,20},{1,17},{... | collective-permute-start | bytes 786440 | tf_op jit(solution)/shard_map/ppermute | solution.py:28
  12.7 0.0 collective-permute-done.2.refs_1_
  12.7 0.0 collective-permute-start.3
  12.7 0.0 collective-permute-done.5.refs_2_
  12.7 2.0 %first.9 = (f32[1024,1024]{1,0:T(8,128)S(1)}, f32[1024,1024]{1,0:T(8,128)S(1)}, bf16[128,1024]{1,0:T(8,128)(2,1)S(1)}, bf16[128,1024]{1,0:T(8,128)(2,1)S(1)}, f3...) custom-call(bf16[256,1024]{1,0:T(8,128)(2,1)S(1)} %get-tuple-element.38.refs_0_, ...), custom_call_target="tpu_custom_call" | custom-call | flops 6442450944 | tf_op jit(solution)/shard_map/first/pallas_call | solution.py:269
  14.7 0.0 collective-permute-done.3.refs_3_.refs_1_
  14.7 1.2 %between.1.refs_0_ = f32[32,128]{1,0:T(8,128)S(1)} custom-call(bf16[1024,128]{1,0:T(8,128)(2,1)S(1)} %collective-permute-done.1.refs_1_.refs_0_, bf16[1024,128]{1,0:T(8,128)(2,1)S(1)} %collective-permute-done.2.refs_1_, bf16[1024,128]{1,0:T(8,128)(2,1)S(1)} %collective-permute-done.5.refs_2_, bf16[1024,128]{1,0:T(8,128)(2,1)S(1)} %collective-permute-done.3.refs_3_.refs_1_, ...), custom_call_target="tpu_custom_call" | custom-call | flops 3221225472 | tf_op jit(solution)/shard_map/between/pallas_call | solution.py:269
  15.9 0.6 %collective-permute-start.6 = (f32[32,128]{1,0:T(8,128)S(1)}, f32[32,128]{1,0:T(8,128)S(1)}, u32[]{:S(2)}, u32[]{:S(2)}) collective-permute-start(f32[32,128]{1,0:T(8,128)S(1)} %between.1.refs_0_), channel_id=1, source_target_pairs={{0,4},{4,0},{8,12},{12,8},{16,20},{20,16},{24,28},{28,24},{1,5},{5... | collective-permute-start | bytes 49160 | tf_op jit(solution)/shard_map/ppermute | solution.py:23
  16.4 1.3 %collective-permute-start.7 = (f32[32,128]{1,0:T(8,128)S(1)}, f32[32,128]{1,0:T(8,128)S(1)}, u32[]{:S(2)}, u32[]{:S(2)}) collective-permute-start(f32[32,128]{1,0:T(8,128)S(1)} %between.1.refs_0_), channel_id=1, source_target_pairs={{0,24},{4,28},{8,16},{12,20},{16,8},{20,12},{24,0},{28,4},{1,25},{... | collective-permute-start | bytes 49160 | tf_op jit(solution)/shard_map/ppermute | solution.py:23
  17.7 0.0 collective-permute-done.6.refs_1_
  17.7 1.4 %collective-permute-start.10 = (f32[64,128]{1,0:T(8,128)S(1)}, f32[64,128]{1,0:T(8,128)S(1)}, u32[]{:S(2)}, u32[]{:S(2)}) collective-permute-start(f32[64,128]{1,0:T(8,128)S(1)} %pack.1.refs_20_), channel_id=1, source_target_pairs={{0,8},{4,12},{8,0},{12,4},{16,24},{20,28},{24,16},{28,20},{1,9},{5... | collective-permute-start | bytes 98312 | tf_op jit(solution)/shard_map/ppermute | solution.py:23
  19.0 0.9 %collective-permute-start.11 = (f32[64,128]{1,0:T(8,128)S(1)}, f32[64,128]{1,0:T(8,128)S(1)}, u32[]{:S(2)}, u32[]{:S(2)}) collective-permute-start(f32[64,128]{1,0:T(8,128)S(1)} %pack.1.refs_20_), channel_id=1, source_target_pairs={{0,16},{4,20},{8,24},{12,28},{16,0},{20,4},{24,8},{28,12},{1,17},{... | collective-permute-start | bytes 98312 | tf_op jit(solution)/shard_map/ppermute | solution.py:23
  19.9 0.0 collective-permute-done.4.refs_2_
  19.9 0.0 collective-permute-start.8
  19.9 1.7 %first.10 = (f32[1024,1024]{1,0:T(8,128)S(1)}, f32[1024,1024]{1,0:T(8,128)S(1)}, bf16[128,1024]{1,0:T(8,128)(2,1)S(1)}, bf16[128,1024]{1,0:T(8,128)(2,1)S(1)}) custom-call(bf16[256,1024]{1,0:T(8,128)(2,1)S(1)} %get-tuple-element.38.refs_0_, bf16[1024,128]{1,0:T(8,128)(2,1)S(1)} %collective-permute-done.3.refs_3_.refs_1_, ...), custom_call_target="tpu_custom_call" | custom-call | flops 6442450944 | tf_op jit(solution)/shard_map/first/pallas_call | solution.py:269
  21.6 0.0 collective-permute-done.7.refs_16_
  21.6 0.6 %collective-permute-start.9 = (f32[32,128]{1,0:T(8,128)S(1)}, f32[32,128]{1,0:T(8,128)S(1)}, u32[]{:S(2)}, u32[]{:S(2)}) collective-permute-start(f32[32,128]{1,0:T(8,128)S(1)} %collective-permute-done.7.refs_16_), channel_id=1, source_target_pairs={{0,4},{4,0},{8,12},{12,8},{16,20},{20,16},{24,28},{28,24},{1,5},{5... | collective-permute-start | bytes 49160 | tf_op jit(solution)/shard_map/ppermute | solution.py:23
  22.2 0.0 collective-permute-done.8.refs_1_
  22.2 0.9 %first.11 = (f32[1024,1024]{1,0:T(8,128)S(1)}, bf16[128,1024]{1,0:T(8,128)(2,1)S(1)}) custom-call(bf16[256,1024]{1,0:T(8,128)(2,1)S(1)} %get-tuple-element.38.refs_0_, bf16[1024,128]{1,0:T(8,128)(2,1)S(1)} %collective-permute-done.8.refs_1_), custom_call_target="tpu_custom_call" | custom-call | flops 3221225472 | tf_op jit(solution)/shard_map/first/pallas_call | solution.py:269
  23.1 0.0 collective-permute-done.9.refs_17_
  23.1 0.0 collective-permute-done.10.refs_18_
  23.2 0.0 collective-permute-done.11.refs_19_
  23.2 4.9 %second.1 = (f32[8,128]{1,0:T(8,128)}, f32[1024,128]{1,0:T(8,128)}) custom-call(f32[1024,1024]{1,0:T(8,128)S(1)} %get-tuple-element.40.refs_0_, f32[1024,1024]{1,0:T(8,128)S(1)} %get-tuple-element.43.refs_1_, f32[1024,1024]{1,0:T(8,128)S(1)} %get-tuple-element.47.refs_2_, f32[1024,1024]{1,0:T(8,128)S(1)} %get-tuple-element.58.refs_3_, ...), custom_call_target="tpu_custom_call" | custom-call | flops 25769803776 | tf_op jit(solution)/shard_map/second/pallas_call | solution.py:269
  (1 shorter events, 0.0 us)
Async XLA Ops:
  0.6 6.8 %collective-permute-start = (bf16[1024,128]{1,0:T(8,128)(2,1)}, bf16[1024,128]{1,0:T(8,128)(2,1)S(1)}, u32[]{:S(2)}, u32[]{:S(2)}) collective-permute-start(bf16[1024,128]{1,0:T(8,128)(2,1)} %x_ref.1), channel_id=1, source_target_pairs={{0,4},{4,0},{8,12},{12,8},{16,20},{20,16},{24,28},{28,24},{1,5},{5... | collective-permute-start | bytes 786440 | tf_op jit(solution)/shard_map/ppermute | solution.py:23
  1.1 7.2 %collective-permute-start.1 = (bf16[1024,128]{1,0:T(8,128)(2,1)}, bf16[1024,128]{1,0:T(8,128)(2,1)S(1)}, u32[]{:S(2)}, u32[]{:S(2)}) collective-permute-start(bf16[1024,128]{1,0:T(8,128)(2,1)} %x_ref.1), channel_id=1, source_target_pairs={{0,8},{4,20},{8,0},{12,28},{16,24},{20,4},{24,16},{28,12},{1,9},{5... | collective-permute-start | bytes 786440 | tf_op jit(solution)/shard_map/ppermute | solution.py:28
  3.7 1.0 %copy-start = (bf16[1024,128]{1,0:T(8,128)(2,1)S(1)}, bf16[1024,128]{1,0:T(8,128)(2,1)}, u32[]{:S(2)}) copy-start(bf16[1024,128]{1,0:T(8,128)(2,1)} %x_ref.1) | copy-start | bytes 786436
  4.9 1.0 %copy-start.1 = (bf16[1024,128]{1,0:T(8,128)(2,1)S(1)}, bf16[1024,128]{1,0:T(8,128)(2,1)}, u32[]{:S(2)}) copy-start(bf16[1024,128]{1,0:T(8,128)(2,1)} %x_ref.1) | copy-start | bytes 786436
  5.8 6.8 %collective-permute-start.2 = (bf16[1024,128]{1,0:T(8,128)(2,1)S(1)}, bf16[1024,128]{1,0:T(8,128)(2,1)S(1)}, u32[]{:S(2)}, u32[]{:S(2)}) collective-permute-start(bf16[1024,128]{1,0:T(8,128)(2,1)S(1)} %copy-done.1), channel_id=1, source_target_pairs={{0,16},{4,12},{8,24},{12,4},{16,0},{20,28},{24,8},{28,20},{1,17},{... | collective-permute-start | bytes 786440 | tf_op jit(solution)/shard_map/ppermute | solution.py:28
  8.4 4.3 %collective-permute-start.5 = (bf16[1024,128]{1,0:T(8,128)(2,1)S(1)}, bf16[1024,128]{1,0:T(8,128)(2,1)S(1)}, u32[]{:S(2)}, u32[]{:S(2)}) collective-permute-start(bf16[1024,128]{1,0:T(8,128)(2,1)S(1)} %collective-permute-done.1.refs_1_.refs_0_), channel_id=1, source_target_pairs={{0,4},{4,0},{8,12},{12,8},{16,20},{20,16},{24,28},{28,24},{1,5},{5... | collective-permute-start | bytes 786440 | tf_op jit(solution)/shard_map/ppermute | solution.py:23
  9.4 10.5 %collective-permute-start.4 = (bf16[1024,128]{1,0:T(8,128)(2,1)S(1)}, bf16[1024,128]{1,0:T(8,128)(2,1)S(1)}, u32[]{:S(2)}, u32[]{:S(2)}) collective-permute-start(bf16[1024,128]{1,0:T(8,128)(2,1)S(1)} %collective-permute-done.1.refs_1_.refs_0_), channel_id=1, source_target_pairs={{0,16},{4,12},{8,24},{12,4},{16,0},{20,28},{24,8},{28,20},{1,17},{... | collective-permute-start | bytes 786440 | tf_op jit(solution)/shard_map/ppermute | solution.py:28
  12.7 2.0 %collective-permute-start.3 = (bf16[1024,128]{1,0:T(8,128)(2,1)S(1)}, bf16[1024,128]{1,0:T(8,128)(2,1)S(1)}, u32[]{:S(2)}, u32[]{:S(2)}) collective-permute-start(bf16[1024,128]{1,0:T(8,128)(2,1)S(1)} %collective-permute-done.2.refs_1_), channel_id=1, source_target_pairs={{0,4},{4,0},{8,12},{12,8},{16,20},{20,16},{24,28},{28,24},{1,5},{5... | collective-permute-start | bytes 786440 | tf_op jit(solution)/shard_map/ppermute | solution.py:23
  15.9 1.8 %collective-permute-start.6 = (f32[32,128]{1,0:T(8,128)S(1)}, f32[32,128]{1,0:T(8,128)S(1)}, u32[]{:S(2)}, u32[]{:S(2)}) collective-permute-start(f32[32,128]{1,0:T(8,128)S(1)} %between.1.refs_0_), channel_id=1, source_target_pairs={{0,4},{4,0},{8,12},{12,8},{16,20},{20,16},{24,28},{28,24},{1,5},{5... | collective-permute-start | bytes 49160 | tf_op jit(solution)/shard_map/ppermute | solution.py:23
  16.4 5.2 %collective-permute-start.7 = (f32[32,128]{1,0:T(8,128)S(1)}, f32[32,128]{1,0:T(8,128)S(1)}, u32[]{:S(2)}, u32[]{:S(2)}) collective-permute-start(f32[32,128]{1,0:T(8,128)S(1)} %between.1.refs_0_), channel_id=1, source_target_pairs={{0,24},{4,28},{8,16},{12,20},{16,8},{20,12},{24,0},{28,4},{1,25},{... | collective-permute-start | bytes 49160 | tf_op jit(solution)/shard_map/ppermute | solution.py:23
  17.7 5.5 %collective-permute-start.10 = (f32[64,128]{1,0:T(8,128)S(1)}, f32[64,128]{1,0:T(8,128)S(1)}, u32[]{:S(2)}, u32[]{:S(2)}) collective-permute-start(f32[64,128]{1,0:T(8,128)S(1)} %pack.1.refs_20_), channel_id=1, source_target_pairs={{0,8},{4,12},{8,0},{12,4},{16,24},{20,28},{24,16},{28,20},{1,9},{5... | collective-permute-start | bytes 98312 | tf_op jit(solution)/shard_map/ppermute | solution.py:23
  19.0 4.1 %collective-permute-start.11 = (f32[64,128]{1,0:T(8,128)S(1)}, f32[64,128]{1,0:T(8,128)S(1)}, u32[]{:S(2)}, u32[]{:S(2)}) collective-permute-start(f32[64,128]{1,0:T(8,128)S(1)} %pack.1.refs_20_), channel_id=1, source_target_pairs={{0,16},{4,20},{8,24},{12,28},{16,0},{20,4},{24,8},{28,12},{1,17},{... | collective-permute-start | bytes 98312 | tf_op jit(solution)/shard_map/ppermute | solution.py:23
  19.9 2.3 %collective-permute-start.8 = (bf16[1024,128]{1,0:T(8,128)(2,1)S(1)}, bf16[1024,128]{1,0:T(8,128)(2,1)S(1)}, u32[]{:S(2)}, u32[]{:S(2)}) collective-permute-start(bf16[1024,128]{1,0:T(8,128)(2,1)S(1)} %collective-permute-done.4.refs_2_), channel_id=1, source_target_pairs={{0,4},{4,0},{8,12},{12,8},{16,20},{20,16},{24,28},{28,24},{1,5},{5... | collective-permute-start | bytes 786440 | tf_op jit(solution)/shard_map/ppermute | solution.py:23
  21.6 1.5 %collective-permute-start.9 = (f32[32,128]{1,0:T(8,128)S(1)}, f32[32,128]{1,0:T(8,128)S(1)}, u32[]{:S(2)}, u32[]{:S(2)}) collective-permute-start(f32[32,128]{1,0:T(8,128)S(1)} %collective-permute-done.7.refs_16_), channel_id=1, source_target_pairs={{0,4},{4,0},{8,12},{12,8},{16,20},{20,16},{24,28},{28,24},{1,5},{5... | collective-permute-start | bytes 49160 | tf_op jit(solution)/shard_map/ppermute | solution.py:23

commit v5 on v4

--- a/solution.py
+++ b/solution.py
@@ -100,67 +100,57 @@
                 acc_ref[8 * g : 8 * g + 8, :] = totals[t]
 
 
-def first_kernel(count, start, sums, sideways, *refs):
+def first_kernel(count, start, sums, as_rows, *refs):
     rows_ref, x_refs, refs = refs[0], refs[1 : 1 + count], refs[1 + count :]
-    acc_in = acc_ref = along_ref = None
+    acc_in = acc_ref = None
     if sums and not start:
         acc_in, refs = refs[0], refs[1:]
     e_refs, turned_refs, refs = refs[:count], refs[count : 2 * count], refs[2 * count :]
     if sums:
         acc_ref, refs = refs[0], refs[1:]
-    if sideways:
-        side_ref, along_ref, refs = refs[0], refs[-1], refs[1:-1]
-    put_tiles(rows_ref, x_refs, e_refs, turned_refs, refs, acc_in, acc_ref, along_ref)
-    if sideways:
-        side_ref[...] = jnp.concatenate(across(along_ref[...]), axis=0)
-
-
-def between_kernel(*refs):
-    near_ref, cross_ref, near_mate_ref, cross_mate_ref, near_t, cross_t, acc_in, side_ref, *refs = refs
-    out_ref, rows, cols, x, row_sums = refs
-    me = lax.axis_index("team")
-    core, side = me % 2, (me // 2) % 2
-    n, width = near_ref.shape
+    if as_rows:
+        put_rows(refs[0], x_refs[0][...].T)
+        refs = refs[1:]
+    put_tiles(rows_ref, x_refs, e_refs, turned_refs, refs, acc_in, acc_ref, None)
+
+
+def third_kernel(*refs):
+    rows_ref, near_rows, cross_ref, near_mate_ref, acc_in, *refs = refs
+    e_cross, e_mate, cross_t, mate_t, out_ref, cross_cols, mate_cols, along, between, acc = refs
+    team = lax.axis_index("team")
+    with_mate = team % 2 == team // 2 % 2
+    n = cross_ref.shape[0]
     groups = n // 128
     block = 256
-
-    @pl.when(core == 0)
-    def _():
-        rows[:width, :] = near_t[...]
-
-    @pl.when(core == 1)
-    def _():
-        rows[:width, :] = cross_t[...]
-
-    for which, (c, s) in ((cross_ref, (0, 0)), (near_ref, (1, 0)), (near_mate_ref, (0, 1)), (cross_mate_ref, (1, 1))):
-
-        @pl.when((core == c) & (side == s))
-        def _(which=which):
-            x[...] = which[...]
-
-    put_rows(rows, rows[:width, :])
-    for j in range(0, n, block):
-        part = slice(j, j + block)
-        put_columns(cols, part, x[part, :], x[part, :].T)
-        row_sums[part, :] = jnp.zeros((block, 128), F32)
+    put_tiles(
+        rows_ref,
+        [cross_ref, near_mate_ref],
+        [e_cross, e_mate],
+        [cross_t, mate_t],
+        [cross_cols, mate_cols],
+        acc_in,
+        acc,
+        along,
+    )
     for i in range(0, n, block):
         totals = [jnp.zeros((8, 128), F32) for _ in range(block // 128)]
         for j in range(0, n, block):
             part = slice(j, j + block)
-            p = jnp.dot(cols[part, :], rows[:, i : i + block], preferred_element_type=F32)
-            along = row_sums[part, :]
+            cols = jnp.where(with_mate, mate_cols[part, :], cross_cols[part, :])
+            p = jnp.dot(cols, near_rows[:, i : i + block], preferred_element_type=F32)
+            over = between[part, :] if i else jnp.zeros((block, 128), F32)
             for t in range(block // 128):
                 k = jnp.exp(p[:, t * 128 : (t + 1) * 128])
-                along = along + k
+                over = over + k
                 totals[t] = totals[t] + jnp.sum(k.reshape(block // 8, 8, 128), axis=0)
-            row_sums[part, :] = along
+            between[part, :] = over
         for t, total in enumerate(totals):
             g = groups + i // 128 + t
             out_ref[g : g + 1, :] = jnp.sum(total, axis=0, keepdims=True)
-    out_ref[2 * groups : 3 * groups, :] = jnp.concatenate(across(row_sums[...]), axis=0)
-    out_ref[3 * groups :, :] = side_ref[...]
+    out_ref[2 * groups : 3 * groups, :] = jnp.concatenate(across(between[...]), axis=0)
+    out_ref[3 * groups :, :] = jnp.concatenate(across(along[...]), axis=0)
     for g in range(groups):
-        out_ref[g : g + 1, :] = jnp.sum(acc_in[8 * g : 8 * g + 8, :], axis=0, keepdims=True)
+        out_ref[g : g + 1, :] = jnp.sum(acc[8 * g : 8 * g + 8, :], axis=0, keepdims=True)
 
 
 def pack_kernel(*refs):
@@ -191,9 +181,12 @@
         return pack_refs[(4, 2, 3)[mask // 2]][first : first + groups, :]
 
     def first_sum(mask):
-        near = message(mask, 0) + message(mask ^ 2, 1)
-        near = near + jnp.where(side == mask // 2 % 2, message(mask ^ 4, 2), message(mask ^ 5, 2))
-        return near + jnp.where(core == mask % 2, message(mask ^ 3, 3), message(mask ^ 5, 3))
+        even, low = core == mask % 2, side == mask // 2 % 2
+        two, three, four, five = mask ^ 2, mask ^ 3, mask ^ 4, mask ^ 5
+        total = message(mask, 0) + jnp.where(even, message(two, 1), message(four, 1))
+        at_low = jnp.where(even, message(three, 2), message(five, 2))
+        at_high = jnp.where(even, message(four, 2), message(two, 2))
+        return total + jnp.where(low, at_low, at_high) + jnp.where(even, message(three, 3), message(five, 3))
 
     sums = [first_sum(mask) for mask in range(count)]
     order = [sums[even] if even == odd else jnp.where(core == 0, sums[even], sums[odd]) for even, odd in masks]
@@ -280,17 +273,17 @@
     acc = None
     done = {}
 
-    def first(blocks, sums=True, sideways=False):
+    def first(blocks, sums=True, as_rows=False):
         nonlocal acc
         count = len(blocks)
         out = call(
-            functools.partial(first_kernel, count, acc is None, sums, sideways),
+            functools.partial(first_kernel, count, acc is None, sums, as_rows),
             (tile((n, n)),) * count
             + (tile((width, n), BF16),) * count
             + (tile((8 * groups, 128)),) * sums
-            + (tile((groups, 128)),) * sideways,
+            + (tile((2 * width, n), BF16),) * as_rows,
             [rows, *blocks.values()] + ([acc] if sums and acc is not None else []),
-            scratch=[pltpu.VMEM((n, 2 * width), BF16)] * count + [pltpu.VMEM((n, 128), F32)] * sideways,
+            scratch=[pltpu.VMEM((n, 2 * width), BF16)] * count,
             name="first",
             tiles=count,
         )
@@ -313,23 +306,24 @@
     first(dict(mate=mate))
     near = after(near)
     near_mate = swapped(near, 1)
-    first(dict(near=near))
+    near_rows = first(dict(near=near), as_rows=True)
     diagonal = exchanged(after(near), 4, 2)
     cross_mate = swapped(cross, 1)
-    side = first(dict(cross=cross, near_mate=near_mate), sideways=True)
-    sums = call(
-        between_kernel,
-        tile((4 * groups, 128)),
-        [near, cross, near_mate, cross_mate, done["near"][1], done["cross"][1], acc, side],
+    *out, sums = call(
+        third_kernel,
+        (tile((n, n)),) * 2 + (tile((width, n), BF16),) * 2 + (tile((4 * groups, 128)),),
+        [rows, near_rows, cross, near_mate, acc],
         scratch=[
-            pltpu.VMEM((2 * width, n), BF16),
             pltpu.VMEM((n, 2 * width), BF16),
-            pltpu.VMEM((n, width), BF16),
+            pltpu.VMEM((n, 2 * width), BF16),
             pltpu.VMEM((n, 128), F32),
+            pltpu.VMEM((n, 128), F32),
+            pltpu.VMEM((8 * groups, 128), F32),
         ],
         name="between",
-        tiles=1,
-    )
+        tiles=3,
+    )
+    done["cross"], done["near_mate"] = (out[0], out[2]), (out[1], out[3])
     far = swapped(sums, 6)
     mate_sums = swapped(sums, 1)
     pack = call(pack_kernel, tile((8 * groups, 128)), [sums, mate_sums], name="pack")

time: 28.4 us -> 28 us (0.986)
  Pallas kernels: 13.7 us -> 13.3 us
    pallas_call x10 -> x9, Pallas kernels: 13.7 us -> 13.3 us  [call(): pl.pallas_call(kernel, out_shape=out_shape, in_specs=[IN_VMEM] * len(args...]
  transfers between devices with their start and end apart: 12 -> 12, of which waited for: 0 -> 0; matrix products, arithmetic and copies ran while one was open for 0% -> 0% of each run, Pallas kernels for 31% -> 30%
where the time goes in v5:
time: 28 us; the launch traced here: 27.8 us
  Pallas kernels  13.3 us (48%)
  starting transfers between devices  12.6 us (45%)
  local copies, waits for them, and re-layouts  0.99 us (4%)
  between operations  0.92 us (3%)
    pallas_call x9, Pallas kernels, call(): pl.pallas_call(kernel, out_shape=out_shape, in_specs=[IN_VMEM] * len(args...  13.3 us
    ppermute x3, starting transfers between devices, exchanged(): lax.ppermute(array, 'team', [(i, i ^ (odd if i % 2 else even)) for i in r...  7.43 us
    ppermute x9, starting transfers between devices, swapped(): return lax.ppermute(array, 'team', [(i, i ^ mask) for i in range(size)])  5.22 us
    unnamed x4, local copies, waits for them, and re-layouts  0.99 us
  transfers between devices with their start and end apart: 12, of which 0 were waited for; matrix products, arithmetic and copies ran while one was open for 0% of the time, Pallas kernels for 30%

profile of v5, /device:TPU:0, one launch (start us, length us, event | category | flops | bytes accessed | tf_op | source)
XLA Modules:
  0.0 27.8 jit_solution(8195998904064657644)
XLA Ops:
  0.6 0.5 %collective-permute-start = (bf16[1024,128]{1,0:T(8,128)(2,1)}, bf16[1024,128]{1,0:T(8,128)(2,1)S(1)}, u32[]{:S(2)}, u32[]{:S(2)}) collective-permute-start(bf16[1024,128]{1,0:T(8,128)(2,1)} %x_ref.1), channel_id=1, source_target_pairs={{0,4},{4,0},{8,12},{12,8},{16,20},{20,16},{24,28},{28,24},{1,5},{5... | collective-permute-start | bytes 786440 | tf_op jit(solution)/shard_map/ppermute | solution.py:23
  1.1 2.6 %collective-permute-start.1 = (bf16[1024,128]{1,0:T(8,128)(2,1)}, bf16[1024,128]{1,0:T(8,128)(2,1)S(1)}, u32[]{:S(2)}, u32[]{:S(2)}) collective-permute-start(bf16[1024,128]{1,0:T(8,128)(2,1)} %x_ref.1), channel_id=1, source_target_pairs={{0,8},{4,20},{8,0},{12,28},{16,24},{20,4},{24,16},{28,12},{1,9},{5... | collective-permute-start | bytes 786440 | tf_op jit(solution)/shard_map/ppermute | solution.py:28
  3.7 0.0 copy-start
  3.7 1.0 %copy-done = bf16[1024,128]{1,0:T(8,128)(2,1)S(1)} copy-done((bf16[1024,128]{1,0:T(8,128)(2,1)S(1)}, bf16[1024,128]{1,0:T(8,128)(2,1)}, u32[]{:S(2)}) %copy-start) | copy-done | bytes 262168
  4.7 0.2 rows.1
  4.9 0.0 copy-start.1
  4.9 0.9 %first.5 = (f32[1024,1024]{1,0:T(8,128)S(1)}, bf16[128,1024]{1,0:T(8,128)(2,1)S(1)}, f32[64,128]{1,0:T(8,128)S(1)}) custom-call(bf16[256,1024]{1,0:T(8,128)(2,1)S(1)} %get-tuple-element.38.refs_0_, bf16[1024,128]{1,0:T(8,128)(2,1)S(1)} %get-tuple-element.39.refs_1_.refs_21_), custom_call_target="tpu_custom_call" | custom-call | flops 3221225472 | tf_op jit(solution)/shard_map/first/pallas_call | solution.py:262
  5.8 0.0 copy-done.1
  5.8 1.6 %collective-permute-start.2 = (bf16[1024,128]{1,0:T(8,128)(2,1)S(1)}, bf16[1024,128]{1,0:T(8,128)(2,1)S(1)}, u32[]{:S(2)}, u32[]{:S(2)}) collective-permute-start(bf16[1024,128]{1,0:T(8,128)(2,1)S(1)} %copy-done.1), channel_id=1, source_target_pairs={{0,16},{4,12},{8,24},{12,4},{16,0},{20,28},{24,8},{28,20},{1,17},{... | collective-permute-start | bytes 786440 | tf_op jit(solution)/shard_map/ppermute | solution.py:28
  7.4 0.0 collective-permute-done.refs_1_
  7.4 0.9 %first.6 = (f32[1024,1024]{1,0:T(8,128)S(1)}, bf16[128,1024]{1,0:T(8,128)(2,1)S(1)}, f32[64,128]{1,0:T(8,128)S(1)}) custom-call(bf16[256,1024]{1,0:T(8,128)(2,1)S(1)} %get-tuple-element.38.refs_0_, bf16[1024,128]{1,0:T(8,128)(2,1)S(1)} %collective-permute-done.refs_1_, f32[64,128]{1,0:T(8,128)S(1)} %get-tuple-element.42.refs_2_), custom_call_target="tpu_custom_call" | custom-call | flops 3221225472 | tf_op jit(solution)/shard_map/first/pallas_call | solution.py:262
  8.4 0.0 collective-permute-done.1.refs_1_
  8.4 0.1 collective-permute-start.5
  8.4 1.0 %first.7 = (f32[1024,1024]{1,0:T(8,128)S(1)}, bf16[128,1024]{1,0:T(8,128)(2,1)S(1)}, f32[64,128]{1,0:T(8,128)S(1)}, bf16[256,1024]{1,0:T(8,128)(2,1)S(1)}) custom-call(bf16[256,1024]{1,0:T(8,128)(2,1)S(1)} %get-tuple-element.38.refs_0_, bf16[1024,128]{1,0:T(8,128)(2,1)S(1)} %collective-permute-done.1.refs_1_, f32[64,128]{1,0:T(8,128)S(1)} %get-tuple-element.46.refs_2_), custom_call_target="tpu_custom_call" | custom-call | flops 3221225472 | tf_op jit(solution)/shard_map/first/pallas_call | solution.py:262
  9.5 3.3 %collective-permute-start.4 = (bf16[1024,128]{1,0:T(8,128)(2,1)S(1)}, bf16[1024,128]{1,0:T(8,128)(2,1)S(1)}, u32[]{:S(2)}, u32[]{:S(2)}) collective-permute-start(bf16[1024,128]{1,0:T(8,128)(2,1)S(1)} %collective-permute-done.1.refs_1_), channel_id=1, source_target_pairs={{0,16},{4,12},{8,24},{12,4},{16,0},{20,28},{24,8},{28,20},{1,17},{... | collective-permute-start | bytes 786440 | tf_op jit(solution)/shard_map/ppermute | solution.py:28
  12.8 0.0 collective-permute-done.2.refs_2_
  12.8 0.0 collective-permute-start.3
  12.8 0.0 collective-permute-done.5.refs_3_
  12.8 2.8 %between.1 = (f32[1024,1024]{1,0:T(8,128)S(1)}, f32[1024,1024]{1,0:T(8,128)S(1)}, bf16[128,1024]{1,0:T(8,128)(2,1)S(1)}, bf16[128,1024]{1,0:T(8,128)(2,1)S(1)}, f32[32,128]{1,0:T(8,128)S(1)}) custom-call(bf16[256,1024]{1,0:T(8,128)(2,1)S(1)} %get-tuple-element.38.refs_0_, bf16[256,1024]{1,0:T(8,128)(2,1)S(1)} %get-tuple-element.51.refs_1_, ...), custom_call_target="tpu_custom_call" | custom-call | flops 9663676416 | tf_op jit(solution)/shard_map/between/pallas_call | solution.py:262
  15.6 0.6 %collective-permute-start.6 = (f32[32,128]{1,0:T(8,128)S(1)}, f32[32,128]{1,0:T(8,128)S(1)}, u32[]{:S(2)}, u32[]{:S(2)}) collective-permute-start(f32[32,128]{1,0:T(8,128)S(1)} %get-tuple-element.53.refs_0_), channel_id=1, source_target_pairs={{0,4},{4,0},{8,12},{12,8},{16,20},{20,16},{24,28},{28,24},{1,5},{5... | collective-permute-start | bytes 49160 | tf_op jit(solution)/shard_map/ppermute | solution.py:23
  16.1 1.3 %collective-permute-start.7 = (f32[32,128]{1,0:T(8,128)S(1)}, f32[32,128]{1,0:T(8,128)S(1)}, u32[]{:S(2)}, u32[]{:S(2)}) collective-permute-start(f32[32,128]{1,0:T(8,128)S(1)} %get-tuple-element.53.refs_0_), channel_id=1, source_target_pairs={{0,24},{4,28},{8,16},{12,20},{16,8},{20,12},{24,0},{28,4},{1,25},{... | collective-permute-start | bytes 49160 | tf_op jit(solution)/shard_map/ppermute | solution.py:23
  17.4 0.0 collective-permute-done.6.refs_1_
  17.4 1.3 %collective-permute-start.10 = (f32[64,128]{1,0:T(8,128)S(1)}, f32[64,128]{1,0:T(8,128)S(1)}, u32[]{:S(2)}, u32[]{:S(2)}) collective-permute-start(f32[64,128]{1,0:T(8,128)S(1)} %pack.1.refs_20_), channel_id=1, source_target_pairs={{0,8},{4,12},{8,0},{12,4},{16,24},{20,28},{24,16},{28,20},{1,9},{5... | collective-permute-start | bytes 98312 | tf_op jit(solution)/shard_map/ppermute | solution.py:23
  18.6 1.0 %collective-permute-start.11 = (f32[64,128]{1,0:T(8,128)S(1)}, f32[64,128]{1,0:T(8,128)S(1)}, u32[]{:S(2)}, u32[]{:S(2)}) collective-permute-start(f32[64,128]{1,0:T(8,128)S(1)} %pack.1.refs_20_), channel_id=1, source_target_pairs={{0,16},{4,20},{8,24},{12,28},{16,0},{20,4},{24,8},{28,12},{1,17},{... | collective-permute-start | bytes 98312 | tf_op jit(solution)/shard_map/ppermute | solution.py:23
  19.6 0.0 collective-permute-done.3.refs_1_
  19.6 0.0 collective-permute-done.4.refs_2_
  19.6 0.0 collective-permute-start.8
  19.6 1.7 %first.8 = (f32[1024,1024]{1,0:T(8,128)S(1)}, f32[1024,1024]{1,0:T(8,128)S(1)}, bf16[128,1024]{1,0:T(8,128)(2,1)S(1)}, bf16[128,1024]{1,0:T(8,128)(2,1)S(1)}) custom-call(bf16[256,1024]{1,0:T(8,128)(2,1)S(1)} %get-tuple-element.38.refs_0_, bf16[1024,128]{1,0:T(8,128)(2,1)S(1)} %collective-permute-done.3.refs_1_, ...), custom_call_target="tpu_custom_call" | custom-call | flops 6442450944 | tf_op jit(solution)/shard_map/first/pallas_call | solution.py:262
  21.3 0.0 collective-permute-done.7.refs_16_
  21.3 0.6 %collective-permute-start.9 = (f32[32,128]{1,0:T(8,128)S(1)}, f32[32,128]{1,0:T(8,128)S(1)}, u32[]{:S(2)}, u32[]{:S(2)}) collective-permute-start(f32[32,128]{1,0:T(8,128)S(1)} %collective-permute-done.7.refs_16_), channel_id=1, source_target_pairs={{0,4},{4,0},{8,12},{12,8},{16,20},{20,16},{24,28},{28,24},{1,5},{5... | collective-permute-start | bytes 49160 | tf_op jit(solution)/shard_map/ppermute | solution.py:23
  21.9 0.0 collective-permute-done.8.refs_1_
  21.9 0.9 %first.9 = (f32[1024,1024]{1,0:T(8,128)S(1)}, bf16[128,1024]{1,0:T(8,128)(2,1)S(1)}) custom-call(bf16[256,1024]{1,0:T(8,128)(2,1)S(1)} %get-tuple-element.38.refs_0_, bf16[1024,128]{1,0:T(8,128)(2,1)S(1)} %collective-permute-done.8.refs_1_), custom_call_target="tpu_custom_call" | custom-call | flops 3221225472 | tf_op jit(solution)/shard_map/first/pallas_call | solution.py:262
  22.8 0.0 collective-permute-done.9.refs_17_
  22.8 0.0 collective-permute-done.10.refs_18_
  22.8 0.0 collective-permute-done.11.refs_19_
  22.9 4.8 %second.1 = (f32[8,128]{1,0:T(8,128)}, f32[1024,128]{1,0:T(8,128)}) custom-call(f32[1024,1024]{1,0:T(8,128)S(1)} %get-tuple-element.40.refs_0_, f32[1024,1024]{1,0:T(8,128)S(1)} %get-tuple-element.43.refs_1_, f32[1024,1024]{1,0:T(8,128)S(1)} %get-tuple-element.47.refs_2_, f32[1024,1024]{1,0:T(8,128)S(1)} %get-tuple-element.56.refs_3_, ...), custom_call_target="tpu_custom_call" | custom-call | flops 25769803776 | tf_op jit(solution)/shard_map/second/pallas_call | solution.py:262
  (1 shorter events, 0.0 us)
Async XLA Ops:
  0.6 6.8 %collective-permute-start = (bf16[1024,128]{1,0:T(8,128)(2,1)}, bf16[1024,128]{1,0:T(8,128)(2,1)S(1)}, u32[]{:S(2)}, u32[]{:S(2)}) collective-permute-start(bf16[1024,128]{1,0:T(8,128)(2,1)} %x_ref.1), channel_id=1, source_target_pairs={{0,4},{4,0},{8,12},{12,8},{16,20},{20,16},{24,28},{28,24},{1,5},{5... | collective-permute-start | bytes 786440 | tf_op jit(solution)/shard_map/ppermute | solution.py:23
  1.1 7.2 %collective-permute-start.1 = (bf16[1024,128]{1,0:T(8,128)(2,1)}, bf16[1024,128]{1,0:T(8,128)(2,1)S(1)}, u32[]{:S(2)}, u32[]{:S(2)}) collective-permute-start(bf16[1024,128]{1,0:T(8,128)(2,1)} %x_ref.1), channel_id=1, source_target_pairs={{0,8},{4,20},{8,0},{12,28},{16,24},{20,4},{24,16},{28,12},{1,9},{5... | collective-permute-start | bytes 786440 | tf_op jit(solution)/shard_map/ppermute | solution.py:28
  3.7 1.0 %copy-start = (bf16[1024,128]{1,0:T(8,128)(2,1)S(1)}, bf16[1024,128]{1,0:T(8,128)(2,1)}, u32[]{:S(2)}) copy-start(bf16[1024,128]{1,0:T(8,128)(2,1)} %x_ref.1) | copy-start | bytes 786436
  4.9 1.0 %copy-start.1 = (bf16[1024,128]{1,0:T(8,128)(2,1)S(1)}, bf16[1024,128]{1,0:T(8,128)(2,1)}, u32[]{:S(2)}) copy-start(bf16[1024,128]{1,0:T(8,128)(2,1)} %x_ref.1) | copy-start | bytes 786436
  5.8 6.9 %collective-permute-start.2 = (bf16[1024,128]{1,0:T(8,128)(2,1)S(1)}, bf16[1024,128]{1,0:T(8,128)(2,1)S(1)}, u32[]{:S(2)}, u32[]{:S(2)}) collective-permute-start(bf16[1024,128]{1,0:T(8,128)(2,1)S(1)} %copy-done.1), channel_id=1, source_target_pairs={{0,16},{4,12},{8,24},{12,4},{16,0},{20,28},{24,8},{28,20},{1,17},{... | collective-permute-start | bytes 786440 | tf_op jit(solution)/shard_map/ppermute | solution.py:28
  8.4 4.4 %collective-permute-start.5 = (bf16[1024,128]{1,0:T(8,128)(2,1)S(1)}, bf16[1024,128]{1,0:T(8,128)(2,1)S(1)}, u32[]{:S(2)}, u32[]{:S(2)}) collective-permute-start(bf16[1024,128]{1,0:T(8,128)(2,1)S(1)} %collective-permute-done.1.refs_1_), channel_id=1, source_target_pairs={{0,4},{4,0},{8,12},{12,8},{16,20},{20,16},{24,28},{28,24},{1,5},{5... | collective-permute-start | bytes 786440 | tf_op jit(solution)/shard_map/ppermute | solution.py:23
  9.5 10.1 %collective-permute-start.4 = (bf16[1024,128]{1,0:T(8,128)(2,1)S(1)}, bf16[1024,128]{1,0:T(8,128)(2,1)S(1)}, u32[]{:S(2)}, u32[]{:S(2)}) collective-permute-start(bf16[1024,128]{1,0:T(8,128)(2,1)S(1)} %collective-permute-done.1.refs_1_), channel_id=1, source_target_pairs={{0,16},{4,12},{8,24},{12,4},{16,0},{20,28},{24,8},{28,20},{1,17},{... | collective-permute-start | bytes 786440 | tf_op jit(solution)/shard_map/ppermute | solution.py:28
  12.8 6.9 %collective-permute-start.3 = (bf16[1024,128]{1,0:T(8,128)(2,1)S(1)}, bf16[1024,128]{1,0:T(8,128)(2,1)S(1)}, u32[]{:S(2)}, u32[]{:S(2)}) collective-permute-start(bf16[1024,128]{1,0:T(8,128)(2,1)S(1)} %collective-permute-done.2.refs_2_), channel_id=1, source_target_pairs={{0,4},{4,0},{8,12},{12,8},{16,20},{20,16},{24,28},{28,24},{1,5},{5... | collective-permute-start | bytes 786440 | tf_op jit(solution)/shard_map/ppermute | solution.py:23
  15.6 1.8 %collective-permute-start.6 = (f32[32,128]{1,0:T(8,128)S(1)}, f32[32,128]{1,0:T(8,128)S(1)}, u32[]{:S(2)}, u32[]{:S(2)}) collective-permute-start(f32[32,128]{1,0:T(8,128)S(1)} %get-tuple-element.53.refs_0_), channel_id=1, source_target_pairs={{0,4},{4,0},{8,12},{12,8},{16,20},{20,16},{24,28},{28,24},{1,5},{5... | collective-permute-start | bytes 49160 | tf_op jit(solution)/shard_map/ppermute | solution.py:23
  16.1 5.2 %collective-permute-start.7 = (f32[32,128]{1,0:T(8,128)S(1)}, f32[32,128]{1,0:T(8,128)S(1)}, u32[]{:S(2)}, u32[]{:S(2)}) collective-permute-start(f32[32,128]{1,0:T(8,128)S(1)} %get-tuple-element.53.refs_0_), channel_id=1, source_target_pairs={{0,24},{4,28},{8,16},{12,20},{16,8},{20,12},{24,0},{28,4},{1,25},{... | collective-permute-start | bytes 49160 | tf_op jit(solution)/shard_map/ppermute | solution.py:23
  17.4 5.5 %collective-permute-start.10 = (f32[64,128]{1,0:T(8,128)S(1)}, f32[64,128]{1,0:T(8,128)S(1)}, u32[]{:S(2)}, u32[]{:S(2)}) collective-permute-start(f32[64,128]{1,0:T(8,128)S(1)} %pack.1.refs_20_), channel_id=1, source_target_pairs={{0,8},{4,12},{8,0},{12,4},{16,24},{20,28},{24,16},{28,20},{1,9},{5... | collective-permute-start | bytes 98312 | tf_op jit(solution)/shard_map/ppermute | solution.py:23
  18.6 4.2 %collective-permute-start.11 = (f32[64,128]{1,0:T(8,128)S(1)}, f32[64,128]{1,0:T(8,128)S(1)}, u32[]{:S(2)}, u32[]{:S(2)}) collective-permute-start(f32[64,128]{1,0:T(8,128)S(1)} %pack.1.refs_20_), channel_id=1, source_target_pairs={{0,16},{4,20},{8,24},{12,28},{16,0},{20,4},{24,8},{28,12},{1,17},{... | collective-permute-start | bytes 98312 | tf_op jit(solution)/shard_map/ppermute | solution.py:23
  19.6 2.3 %collective-permute-start.8 = (bf16[1024,128]{1,0:T(8,128)(2,1)S(1)}, bf16[1024,128]{1,0:T(8,128)(2,1)S(1)}, u32[]{:S(2)}, u32[]{:S(2)}) collective-permute-start(bf16[1024,128]{1,0:T(8,128)(2,1)S(1)} %collective-permute-done.4.refs_2_), channel_id=1, source_target_pairs={{0,4},{4,0},{8,12},{12,8},{16,20},{20,16},{24,28},{28,24},{1,5},{5... | collective-permute-start | bytes 786440 | tf_op jit(solution)/shard_map/ppermute | solution.py:23
  21.3 1.5 %collective-permute-start.9 = (f32[32,128]{1,0:T(8,128)S(1)}, f32[32,128]{1,0:T(8,128)S(1)}, u32[]{:S(2)}, u32[]{:S(2)}) collective-permute-start(f32[32,128]{1,0:T(8,128)S(1)} %collective-permute-done.7.refs_16_), channel_id=1, source_target_pairs={{0,4},{4,0},{8,12},{12,8},{16,20},{20,16},{24,28},{28,24},{1,5},{5... | collective-permute-start | bytes 49160 | tf_op jit(solution)/shard_map/ppermute | solution.py:23

commit v6 on v5

--- a/solution.py
+++ b/solution.py
@@ -116,7 +116,7 @@
 
 def third_kernel(*refs):
     rows_ref, near_rows, cross_ref, near_mate_ref, acc_in, *refs = refs
-    e_cross, e_mate, cross_t, mate_t, out_ref, cross_cols, mate_cols, along, between, acc = refs
+    e_cross, e_mate, cross_t, mate_t, out_ref, cross_cols, mate_cols, chosen, along, between, acc = refs
     team = lax.axis_index("team")
     with_mate = team % 2 == team // 2 % 2
     n = cross_ref.shape[0]
@@ -136,8 +136,9 @@
         totals = [jnp.zeros((8, 128), F32) for _ in range(block // 128)]
         for j in range(0, n, block):
             part = slice(j, j + block)
-            cols = jnp.where(with_mate, mate_cols[part, :], cross_cols[part, :])
-            p = jnp.dot(cols, near_rows[:, i : i + block], preferred_element_type=F32)
+            if i == 0:
+                chosen[part, :] = jnp.where(with_mate, mate_cols[part, :], cross_cols[part, :])
+            p = jnp.dot(chosen[part, :], near_rows[:, i : i + block], preferred_element_type=F32)
             over = between[part, :] if i else jnp.zeros((block, 128), F32)
             for t in range(block // 128):
                 k = jnp.exp(p[:, t * 128 : (t + 1) * 128])
@@ -316,6 +317,7 @@
         scratch=[
             pltpu.VMEM((n, 2 * width), BF16),
             pltpu.VMEM((n, 2 * width), BF16),
+            pltpu.VMEM((n, 2 * width), BF16),
             pltpu.VMEM((n, 128), F32),
             pltpu.VMEM((n, 128), F32),
             pltpu.VMEM((8 * groups, 128), F32),

time: 28 us -> 28 us (level)
  no operation moved by 1% of the time
where the time goes in v6:
time: 28 us; the launch traced here: 27.8 us
  Pallas kernels  13.2 us (47%)
  starting transfers between devices  12.7 us (45%)
  local copies, waits for them, and re-layouts  0.99 us (4%)
  between operations  0.92 us (3%)
    pallas_call x9, Pallas kernels, call(): pl.pallas_call(kernel, out_shape=out_shape, in_specs=[IN_VMEM] * len(args...  13.2 us
    ppermute x3, starting transfers between devices, exchanged(): lax.ppermute(array, 'team', [(i, i ^ (odd if i % 2 else even)) for i in r...  7.43 us
    ppermute x9, starting transfers between devices, swapped(): return lax.ppermute(array, 'team', [(i, i ^ mask) for i in range(size)])  5.23 us
    unnamed x4, local copies, waits for them, and re-layouts  0.99 us
  transfers between devices with their start and end apart: 12, of which 0 were waited for; matrix products, arithmetic and copies ran while one was open for 0% of the time, Pallas kernels for 30%

profile of v6, /device:TPU:0, one launch (start us, length us, event | category | flops | bytes accessed | tf_op | source)
XLA Modules:
  0.0 27.8 jit_solution(5866635621736121505)
XLA Ops:
  0.6 0.5 %collective-permute-start = (bf16[1024,128]{1,0:T(8,128)(2,1)}, bf16[1024,128]{1,0:T(8,128)(2,1)S(1)}, u32[]{:S(2)}, u32[]{:S(2)}) collective-permute-start(bf16[1024,128]{1,0:T(8,128)(2,1)} %x_ref.1), channel_id=1, source_target_pairs={{0,4},{4,0},{8,12},{12,8},{16,20},{20,16},{24,28},{28,24},{1,5},{5... | collective-permute-start | bytes 786440 | tf_op jit(solution)/shard_map/ppermute | solution.py:23
  1.1 2.6 %collective-permute-start.1 = (bf16[1024,128]{1,0:T(8,128)(2,1)}, bf16[1024,128]{1,0:T(8,128)(2,1)S(1)}, u32[]{:S(2)}, u32[]{:S(2)}) collective-permute-start(bf16[1024,128]{1,0:T(8,128)(2,1)} %x_ref.1), channel_id=1, source_target_pairs={{0,8},{4,20},{8,0},{12,28},{16,24},{20,4},{24,16},{28,12},{1,9},{5... | collective-permute-start | bytes 786440 | tf_op jit(solution)/shard_map/ppermute | solution.py:28
  3.7 0.0 copy-start
  3.7 1.0 %copy-done = bf16[1024,128]{1,0:T(8,128)(2,1)S(1)} copy-done((bf16[1024,128]{1,0:T(8,128)(2,1)S(1)}, bf16[1024,128]{1,0:T(8,128)(2,1)}, u32[]{:S(2)}) %copy-start) | copy-done | bytes 262168
  4.7 0.2 rows.1
  4.9 0.0 copy-start.1
  4.9 0.9 %first.5 = (f32[1024,1024]{1,0:T(8,128)S(1)}, bf16[128,1024]{1,0:T(8,128)(2,1)S(1)}, f32[64,128]{1,0:T(8,128)S(1)}) custom-call(bf16[256,1024]{1,0:T(8,128)(2,1)S(1)} %get-tuple-element.38.refs_0_, bf16[1024,128]{1,0:T(8,128)(2,1)S(1)} %get-tuple-element.39.refs_1_.refs_21_), custom_call_target="tpu_custom_call" | custom-call | flops 3221225472 | tf_op jit(solution)/shard_map/first/pallas_call | solution.py:263
  5.8 0.0 copy-done.1
  5.8 1.6 %collective-permute-start.2 = (bf16[1024,128]{1,0:T(8,128)(2,1)S(1)}, bf16[1024,128]{1,0:T(8,128)(2,1)S(1)}, u32[]{:S(2)}, u32[]{:S(2)}) collective-permute-start(bf16[1024,128]{1,0:T(8,128)(2,1)S(1)} %copy-done.1), channel_id=1, source_target_pairs={{0,16},{4,12},{8,24},{12,4},{16,0},{20,28},{24,8},{28,20},{1,17},{... | collective-permute-start | bytes 786440 | tf_op jit(solution)/shard_map/ppermute | solution.py:28
  7.4 0.0 collective-permute-done.refs_1_
  7.4 0.9 %first.6 = (f32[1024,1024]{1,0:T(8,128)S(1)}, bf16[128,1024]{1,0:T(8,128)(2,1)S(1)}, f32[64,128]{1,0:T(8,128)S(1)}) custom-call(bf16[256,1024]{1,0:T(8,128)(2,1)S(1)} %get-tuple-element.38.refs_0_, bf16[1024,128]{1,0:T(8,128)(2,1)S(1)} %collective-permute-done.refs_1_, f32[64,128]{1,0:T(8,128)S(1)} %get-tuple-element.42.refs_2_), custom_call_target="tpu_custom_call" | custom-call | flops 3221225472 | tf_op jit(solution)/shard_map/first/pallas_call | solution.py:263
  8.4 0.0 collective-permute-done.1.refs_1_
  8.4 0.1 collective-permute-start.5
  8.4 1.0 %first.7 = (f32[1024,1024]{1,0:T(8,128)S(1)}, bf16[128,1024]{1,0:T(8,128)(2,1)S(1)}, f32[64,128]{1,0:T(8,128)S(1)}, bf16[256,1024]{1,0:T(8,128)(2,1)S(1)}) custom-call(bf16[256,1024]{1,0:T(8,128)(2,1)S(1)} %get-tuple-element.38.refs_0_, bf16[1024,128]{1,0:T(8,128)(2,1)S(1)} %collective-permute-done.1.refs_1_, f32[64,128]{1,0:T(8,128)S(1)} %get-tuple-element.46.refs_2_), custom_call_target="tpu_custom_call" | custom-call | flops 3221225472 | tf_op jit(solution)/shard_map/first/pallas_call | solution.py:263
  9.5 3.3 %collective-permute-start.4 = (bf16[1024,128]{1,0:T(8,128)(2,1)S(1)}, bf16[1024,128]{1,0:T(8,128)(2,1)S(1)}, u32[]{:S(2)}, u32[]{:S(2)}) collective-permute-start(bf16[1024,128]{1,0:T(8,128)(2,1)S(1)} %collective-permute-done.1.refs_1_), channel_id=1, source_target_pairs={{0,16},{4,12},{8,24},{12,4},{16,0},{20,28},{24,8},{28,20},{1,17},{... | collective-permute-start | bytes 786440 | tf_op jit(solution)/shard_map/ppermute | solution.py:28
  12.8 0.0 collective-permute-done.2.refs_2_
  12.8 0.0 collective-permute-start.3
  12.8 0.0 collective-permute-done.5.refs_3_
  12.8 2.7 %between.1 = (f32[1024,1024]{1,0:T(8,128)S(1)}, f32[1024,1024]{1,0:T(8,128)S(1)}, bf16[128,1024]{1,0:T(8,128)(2,1)S(1)}, bf16[128,1024]{1,0:T(8,128)(2,1)S(1)}, f32[32,128]{1,0:T(8,128)S(1)}) custom-call(bf16[256,1024]{1,0:T(8,128)(2,1)S(1)} %get-tuple-element.38.refs_0_, bf16[256,1024]{1,0:T(8,128)(2,1)S(1)} %get-tuple-element.51.refs_1_, ...), custom_call_target="tpu_custom_call" | custom-call | flops 9663676416 | tf_op jit(solution)/shard_map/between/pallas_call | solution.py:263
  15.5 0.6 %collective-permute-start.6 = (f32[32,128]{1,0:T(8,128)S(1)}, f32[32,128]{1,0:T(8,128)S(1)}, u32[]{:S(2)}, u32[]{:S(2)}) collective-permute-start(f32[32,128]{1,0:T(8,128)S(1)} %get-tuple-element.53.refs_0_), channel_id=1, source_target_pairs={{0,4},{4,0},{8,12},{12,8},{16,20},{20,16},{24,28},{28,24},{1,5},{5... | collective-permute-start | bytes 49160 | tf_op jit(solution)/shard_map/ppermute | solution.py:23
  16.1 1.3 %collective-permute-start.7 = (f32[32,128]{1,0:T(8,128)S(1)}, f32[32,128]{1,0:T(8,128)S(1)}, u32[]{:S(2)}, u32[]{:S(2)}) collective-permute-start(f32[32,128]{1,0:T(8,128)S(1)} %get-tuple-element.53.refs_0_), channel_id=1, source_target_pairs={{0,24},{4,28},{8,16},{12,20},{16,8},{20,12},{24,0},{28,4},{1,25},{... | collective-permute-start | bytes 49160 | tf_op jit(solution)/shard_map/ppermute | solution.py:23
  17.4 0.0 collective-permute-done.6.refs_1_
  17.4 1.3 %collective-permute-start.10 = (f32[64,128]{1,0:T(8,128)S(1)}, f32[64,128]{1,0:T(8,128)S(1)}, u32[]{:S(2)}, u32[]{:S(2)}) collective-permute-start(f32[64,128]{1,0:T(8,128)S(1)} %pack.1.refs_20_), channel_id=1, source_target_pairs={{0,8},{4,12},{8,0},{12,4},{16,24},{20,28},{24,16},{28,20},{1,9},{5... | collective-permute-start | bytes 98312 | tf_op jit(solution)/shard_map/ppermute | solution.py:23
  18.6 1.0 %collective-permute-start.11 = (f32[64,128]{1,0:T(8,128)S(1)}, f32[64,128]{1,0:T(8,128)S(1)}, u32[]{:S(2)}, u32[]{:S(2)}) collective-permute-start(f32[64,128]{1,0:T(8,128)S(1)} %pack.1.refs_20_), channel_id=1, source_target_pairs={{0,16},{4,20},{8,24},{12,28},{16,0},{20,4},{24,8},{28,12},{1,17},{... | collective-permute-start | bytes 98312 | tf_op jit(solution)/shard_map/ppermute | solution.py:23
  19.6 0.0 collective-permute-done.3.refs_1_
  19.6 0.0 collective-permute-done.4.refs_2_
  19.6 0.0 collective-permute-start.8
  19.6 1.7 %first.8 = (f32[1024,1024]{1,0:T(8,128)S(1)}, f32[1024,1024]{1,0:T(8,128)S(1)}, bf16[128,1024]{1,0:T(8,128)(2,1)S(1)}, bf16[128,1024]{1,0:T(8,128)(2,1)S(1)}) custom-call(bf16[256,1024]{1,0:T(8,128)(2,1)S(1)} %get-tuple-element.38.refs_0_, bf16[1024,128]{1,0:T(8,128)(2,1)S(1)} %collective-permute-done.3.refs_1_, ...), custom_call_target="tpu_custom_call" | custom-call | flops 6442450944 | tf_op jit(solution)/shard_map/first/pallas_call | solution.py:263
  21.3 0.0 collective-permute-done.7.refs_16_
  21.3 0.6 %collective-permute-start.9 = (f32[32,128]{1,0:T(8,128)S(1)}, f32[32,128]{1,0:T(8,128)S(1)}, u32[]{:S(2)}, u32[]{:S(2)}) collective-permute-start(f32[32,128]{1,0:T(8,128)S(1)} %collective-permute-done.7.refs_16_), channel_id=1, source_target_pairs={{0,4},{4,0},{8,12},{12,8},{16,20},{20,16},{24,28},{28,24},{1,5},{5... | collective-permute-start | bytes 49160 | tf_op jit(solution)/shard_map/ppermute | solution.py:23
  21.9 0.0 collective-permute-done.8.refs_1_
  21.9 0.9 %first.9 = (f32[1024,1024]{1,0:T(8,128)S(1)}, bf16[128,1024]{1,0:T(8,128)(2,1)S(1)}) custom-call(bf16[256,1024]{1,0:T(8,128)(2,1)S(1)} %get-tuple-element.38.refs_0_, bf16[1024,128]{1,0:T(8,128)(2,1)S(1)} %collective-permute-done.8.refs_1_), custom_call_target="tpu_custom_call" | custom-call | flops 3221225472 | tf_op jit(solution)/shard_map/first/pallas_call | solution.py:263
  22.8 0.0 collective-permute-done.9.refs_17_
  22.8 0.0 collective-permute-done.10.refs_18_
  22.8 0.0 collective-permute-done.11.refs_19_
  22.8 4.8 %second.1 = (f32[8,128]{1,0:T(8,128)}, f32[1024,128]{1,0:T(8,128)}) custom-call(f32[1024,1024]{1,0:T(8,128)S(1)} %get-tuple-element.40.refs_0_, f32[1024,1024]{1,0:T(8,128)S(1)} %get-tuple-element.43.refs_1_, f32[1024,1024]{1,0:T(8,128)S(1)} %get-tuple-element.47.refs_2_, f32[1024,1024]{1,0:T(8,128)S(1)} %get-tuple-element.56.refs_3_, ...), custom_call_target="tpu_custom_call" | custom-call | flops 25769803776 | tf_op jit(solution)/shard_map/second/pallas_call | solution.py:263
  (1 shorter events, 0.0 us)
Async XLA Ops:
  0.6 6.8 %collective-permute-start = (bf16[1024,128]{1,0:T(8,128)(2,1)}, bf16[1024,128]{1,0:T(8,128)(2,1)S(1)}, u32[]{:S(2)}, u32[]{:S(2)}) collective-permute-start(bf16[1024,128]{1,0:T(8,128)(2,1)} %x_ref.1), channel_id=1, source_target_pairs={{0,4},{4,0},{8,12},{12,8},{16,20},{20,16},{24,28},{28,24},{1,5},{5... | collective-permute-start | bytes 786440 | tf_op jit(solution)/shard_map/ppermute | solution.py:23
  1.1 7.2 %collective-permute-start.1 = (bf16[1024,128]{1,0:T(8,128)(2,1)}, bf16[1024,128]{1,0:T(8,128)(2,1)S(1)}, u32[]{:S(2)}, u32[]{:S(2)}) collective-permute-start(bf16[1024,128]{1,0:T(8,128)(2,1)} %x_ref.1), channel_id=1, source_target_pairs={{0,8},{4,20},{8,0},{12,28},{16,24},{20,4},{24,16},{28,12},{1,9},{5... | collective-permute-start | bytes 786440 | tf_op jit(solution)/shard_map/ppermute | solution.py:28
  3.7 1.0 %copy-start = (bf16[1024,128]{1,0:T(8,128)(2,1)S(1)}, bf16[1024,128]{1,0:T(8,128)(2,1)}, u32[]{:S(2)}) copy-start(bf16[1024,128]{1,0:T(8,128)(2,1)} %x_ref.1) | copy-start | bytes 786436
  4.9 1.0 %copy-start.1 = (bf16[1024,128]{1,0:T(8,128)(2,1)S(1)}, bf16[1024,128]{1,0:T(8,128)(2,1)}, u32[]{:S(2)}) copy-start(bf16[1024,128]{1,0:T(8,128)(2,1)} %x_ref.1) | copy-start | bytes 786436
  5.8 6.9 %collective-permute-start.2 = (bf16[1024,128]{1,0:T(8,128)(2,1)S(1)}, bf16[1024,128]{1,0:T(8,128)(2,1)S(1)}, u32[]{:S(2)}, u32[]{:S(2)}) collective-permute-start(bf16[1024,128]{1,0:T(8,128)(2,1)S(1)} %copy-done.1), channel_id=1, source_target_pairs={{0,16},{4,12},{8,24},{12,4},{16,0},{20,28},{24,8},{28,20},{1,17},{... | collective-permute-start | bytes 786440 | tf_op jit(solution)/shard_map/ppermute | solution.py:28
  8.4 4.4 %collective-permute-start.5 = (bf16[1024,128]{1,0:T(8,128)(2,1)S(1)}, bf16[1024,128]{1,0:T(8,128)(2,1)S(1)}, u32[]{:S(2)}, u32[]{:S(2)}) collective-permute-start(bf16[1024,128]{1,0:T(8,128)(2,1)S(1)} %collective-permute-done.1.refs_1_), channel_id=1, source_target_pairs={{0,4},{4,0},{8,12},{12,8},{16,20},{20,16},{24,28},{28,24},{1,5},{5... | collective-permute-start | bytes 786440 | tf_op jit(solution)/shard_map/ppermute | solution.py:23
  9.5 10.1 %collective-permute-start.4 = (bf16[1024,128]{1,0:T(8,128)(2,1)S(1)}, bf16[1024,128]{1,0:T(8,128)(2,1)S(1)}, u32[]{:S(2)}, u32[]{:S(2)}) collective-permute-start(bf16[1024,128]{1,0:T(8,128)(2,1)S(1)} %collective-permute-done.1.refs_1_), channel_id=1, source_target_pairs={{0,16},{4,12},{8,24},{12,4},{16,0},{20,28},{24,8},{28,20},{1,17},{... | collective-permute-start | bytes 786440 | tf_op jit(solution)/shard_map/ppermute | solution.py:28
  12.8 6.8 %collective-permute-start.3 = (bf16[1024,128]{1,0:T(8,128)(2,1)S(1)}, bf16[1024,128]{1,0:T(8,128)(2,1)S(1)}, u32[]{:S(2)}, u32[]{:S(2)}) collective-permute-start(bf16[1024,128]{1,0:T(8,128)(2,1)S(1)} %collective-permute-done.2.refs_2_), channel_id=1, source_target_pairs={{0,4},{4,0},{8,12},{12,8},{16,20},{20,16},{24,28},{28,24},{1,5},{5... | collective-permute-start | bytes 786440 | tf_op jit(solution)/shard_map/ppermute | solution.py:23
  15.5 1.8 %collective-permute-start.6 = (f32[32,128]{1,0:T(8,128)S(1)}, f32[32,128]{1,0:T(8,128)S(1)}, u32[]{:S(2)}, u32[]{:S(2)}) collective-permute-start(f32[32,128]{1,0:T(8,128)S(1)} %get-tuple-element.53.refs_0_), channel_id=1, source_target_pairs={{0,4},{4,0},{8,12},{12,8},{16,20},{20,16},{24,28},{28,24},{1,5},{5... | collective-permute-start | bytes 49160 | tf_op jit(solution)/shard_map/ppermute | solution.py:23
  16.1 5.2 %collective-permute-start.7 = (f32[32,128]{1,0:T(8,128)S(1)}, f32[32,128]{1,0:T(8,128)S(1)}, u32[]{:S(2)}, u32[]{:S(2)}) collective-permute-start(f32[32,128]{1,0:T(8,128)S(1)} %get-tuple-element.53.refs_0_), channel_id=1, source_target_pairs={{0,24},{4,28},{8,16},{12,20},{16,8},{20,12},{24,0},{28,4},{1,25},{... | collective-permute-start | bytes 49160 | tf_op jit(solution)/shard_map/ppermute | solution.py:23
  17.4 5.4 %collective-permute-start.10 = (f32[64,128]{1,0:T(8,128)S(1)}, f32[64,128]{1,0:T(8,128)S(1)}, u32[]{:S(2)}, u32[]{:S(2)}) collective-permute-start(f32[64,128]{1,0:T(8,128)S(1)} %pack.1.refs_20_), channel_id=1, source_target_pairs={{0,8},{4,12},{8,0},{12,4},{16,24},{20,28},{24,16},{28,20},{1,9},{5... | collective-permute-start | bytes 98312 | tf_op jit(solution)/shard_map/ppermute | solution.py:23
  18.6 4.2 %collective-permute-start.11 = (f32[64,128]{1,0:T(8,128)S(1)}, f32[64,128]{1,0:T(8,128)S(1)}, u32[]{:S(2)}, u32[]{:S(2)}) collective-permute-start(f32[64,128]{1,0:T(8,128)S(1)} %pack.1.refs_20_), channel_id=1, source_target_pairs={{0,16},{4,20},{8,24},{12,28},{16,0},{20,4},{24,8},{28,12},{1,17},{... | collective-permute-start | bytes 98312 | tf_op jit(solution)/shard_map/ppermute | solution.py:23
  19.6 2.3 %collective-permute-start.8 = (bf16[1024,128]{1,0:T(8,128)(2,1)S(1)}, bf16[1024,128]{1,0:T(8,128)(2,1)S(1)}, u32[]{:S(2)}, u32[]{:S(2)}) collective-permute-start(bf16[1024,128]{1,0:T(8,128)(2,1)S(1)} %collective-permute-done.4.refs_2_), channel_id=1, source_target_pairs={{0,4},{4,0},{8,12},{12,8},{16,20},{20,16},{24,28},{28,24},{1,5},{5... | collective-permute-start | bytes 786440 | tf_op jit(solution)/shard_map/ppermute | solution.py:23
  21.3 1.5 %collective-permute-start.9 = (f32[32,128]{1,0:T(8,128)S(1)}, f32[32,128]{1,0:T(8,128)S(1)}, u32[]{:S(2)}, u32[]{:S(2)}) collective-permute-start(f32[32,128]{1,0:T(8,128)S(1)} %collective-permute-done.7.refs_16_), channel_id=1, source_target_pairs={{0,4},{4,0},{8,12},{12,8},{16,20},{20,16},{24,28},{28,24},{1,5},{5... | collective-permute-start | bytes 49160 | tf_op jit(solution)/shard_map/ppermute | solution.py:23

commit v7 on v6

--- a/solution.py
+++ b/solution.py
@@ -230,19 +230,18 @@
     put_scales(0)
     for tiles, ahead in PARTS:
         pl.when(team >= 0)(functools.partial(part, tiles, ahead))
-    seconds = []
-    for g in range(groups):
-        rows = slice(g * 128, (g + 1) * 128)
-        seconds.append(jnp.sum(acc_ref[8 * g : 8 * g + 8, :], axis=0, keepdims=True))
-        out_ref[rows, :] = own_ref[rows, :].astype(F32) - (num_ref[:, rows] / seconds[-1]).T
-        if (g + 1) * 128 % block == 0:
-            out_copy(g * 128 // block).start()
+    seconds = [jnp.sum(acc_ref[8 * g : 8 * g + 8, :], axis=0, keepdims=True) for g in range(groups)]
+    second = jnp.concatenate(seconds, axis=0)
     log_count = jnp.log(jnp.float32(points))
-    second = jnp.concatenate(seconds, axis=0)
     pot_one = -2.0 * (jnp.log(sums[0]) - log_count)
     pot_ref[...] = 0.5 * (pot_one - 2.0 * (jnp.log(second) - log_count))
     pot_copy = pltpu.make_async_copy(pot_ref, pot_hbm, sems.at[n // block])
     pot_copy.start()
+    for g in range(groups):
+        rows = slice(g * 128, (g + 1) * 128)
+        out_ref[rows, :] = own_ref[rows, :].astype(F32) - (num_ref[:, rows] / seconds[g]).T
+        if (g + 1) * 128 % block == 0:
+            out_copy(g * 128 // block).start()
     for i in range(n // block):
         out_copy(i).wait()
     pot_copy.wait()

time: 28 us -> 28 us (level)
  no operation moved by 1% of the time
where the time goes in v7:
time: 28 us; the launch traced here: 27.8 us
  Pallas kernels  13.2 us (47%)
  starting transfers between devices  12.7 us (45%)
  local copies, waits for them, and re-layouts  0.99 us (4%)
  between operations  0.92 us (3%)
    pallas_call x9, Pallas kernels, call(): pl.pallas_call(kernel, out_shape=out_shape, in_specs=[IN_VMEM] * len(args...  13.2 us
    ppermute x3, starting transfers between devices, exchanged(): lax.ppermute(array, 'team', [(i, i ^ (odd if i % 2 else even)) for i in r...  7.43 us
    ppermute x9, starting transfers between devices, swapped(): return lax.ppermute(array, 'team', [(i, i ^ mask) for i in range(size)])  5.23 us
    unnamed x4, local copies, waits for them, and re-layouts  0.99 us
  transfers between devices with their start and end apart: 12, of which 0 were waited for; matrix products, arithmetic and copies ran while one was open for 0% of the time, Pallas kernels for 30%

profile of v7, /device:TPU:0, one launch (start us, length us, event | category | flops | bytes accessed | tf_op | source)
XLA Modules:
  0.0 27.8 jit_solution(14672164609659287768)
XLA Ops:
  0.6 0.5 %collective-permute-start = (bf16[1024,128]{1,0:T(8,128)(2,1)}, bf16[1024,128]{1,0:T(8,128)(2,1)S(1)}, u32[]{:S(2)}, u32[]{:S(2)}) collective-permute-start(bf16[1024,128]{1,0:T(8,128)(2,1)} %x_ref.1), channel_id=1, source_target_pairs={{0,4},{4,0},{8,12},{12,8},{16,20},{20,16},{24,28},{28,24},{1,5},{5... | collective-permute-start | bytes 786440 | tf_op jit(solution)/shard_map/ppermute | solution.py:23
  1.1 2.6 %collective-permute-start.1 = (bf16[1024,128]{1,0:T(8,128)(2,1)}, bf16[1024,128]{1,0:T(8,128)(2,1)S(1)}, u32[]{:S(2)}, u32[]{:S(2)}) collective-permute-start(bf16[1024,128]{1,0:T(8,128)(2,1)} %x_ref.1), channel_id=1, source_target_pairs={{0,8},{4,20},{8,0},{12,28},{16,24},{20,4},{24,16},{28,12},{1,9},{5... | collective-permute-start | bytes 786440 | tf_op jit(solution)/shard_map/ppermute | solution.py:28
  3.7 0.0 copy-start
  3.7 1.0 %copy-done = bf16[1024,128]{1,0:T(8,128)(2,1)S(1)} copy-done((bf16[1024,128]{1,0:T(8,128)(2,1)S(1)}, bf16[1024,128]{1,0:T(8,128)(2,1)}, u32[]{:S(2)}) %copy-start) | copy-done | bytes 262168
  4.7 0.2 rows.1
  4.9 0.0 copy-start.1
  4.9 0.9 %first.5 = (f32[1024,1024]{1,0:T(8,128)S(1)}, bf16[128,1024]{1,0:T(8,128)(2,1)S(1)}, f32[64,128]{1,0:T(8,128)S(1)}) custom-call(bf16[256,1024]{1,0:T(8,128)(2,1)S(1)} %get-tuple-element.38.refs_0_, bf16[1024,128]{1,0:T(8,128)(2,1)S(1)} %get-tuple-element.39.refs_1_.refs_21_), custom_call_target="tpu_custom_call" | custom-call | flops 3221225472 | tf_op jit(solution)/shard_map/first/pallas_call | solution.py:262
  5.8 0.0 copy-done.1
  5.8 1.6 %collective-permute-start.2 = (bf16[1024,128]{1,0:T(8,128)(2,1)S(1)}, bf16[1024,128]{1,0:T(8,128)(2,1)S(1)}, u32[]{:S(2)}, u32[]{:S(2)}) collective-permute-start(bf16[1024,128]{1,0:T(8,128)(2,1)S(1)} %copy-done.1), channel_id=1, source_target_pairs={{0,16},{4,12},{8,24},{12,4},{16,0},{20,28},{24,8},{28,20},{1,17},{... | collective-permute-start | bytes 786440 | tf_op jit(solution)/shard_map/ppermute | solution.py:28
  7.4 0.0 collective-permute-done.refs_1_
  7.4 0.9 %first.6 = (f32[1024,1024]{1,0:T(8,128)S(1)}, bf16[128,1024]{1,0:T(8,128)(2,1)S(1)}, f32[64,128]{1,0:T(8,128)S(1)}) custom-call(bf16[256,1024]{1,0:T(8,128)(2,1)S(1)} %get-tuple-element.38.refs_0_, bf16[1024,128]{1,0:T(8,128)(2,1)S(1)} %collective-permute-done.refs_1_, f32[64,128]{1,0:T(8,128)S(1)} %get-tuple-element.42.refs_2_), custom_call_target="tpu_custom_call" | custom-call | flops 3221225472 | tf_op jit(solution)/shard_map/first/pallas_call | solution.py:262
  8.4 0.0 collective-permute-done.1.refs_1_
  8.4 0.1 collective-permute-start.5
  8.4 1.0 %first.7 = (f32[1024,1024]{1,0:T(8,128)S(1)}, bf16[128,1024]{1,0:T(8,128)(2,1)S(1)}, f32[64,128]{1,0:T(8,128)S(1)}, bf16[256,1024]{1,0:T(8,128)(2,1)S(1)}) custom-call(bf16[256,1024]{1,0:T(8,128)(2,1)S(1)} %get-tuple-element.38.refs_0_, bf16[1024,128]{1,0:T(8,128)(2,1)S(1)} %collective-permute-done.1.refs_1_, f32[64,128]{1,0:T(8,128)S(1)} %get-tuple-element.46.refs_2_), custom_call_target="tpu_custom_call" | custom-call | flops 3221225472 | tf_op jit(solution)/shard_map/first/pallas_call | solution.py:262
  9.5 3.3 %collective-permute-start.4 = (bf16[1024,128]{1,0:T(8,128)(2,1)S(1)}, bf16[1024,128]{1,0:T(8,128)(2,1)S(1)}, u32[]{:S(2)}, u32[]{:S(2)}) collective-permute-start(bf16[1024,128]{1,0:T(8,128)(2,1)S(1)} %collective-permute-done.1.refs_1_), channel_id=1, source_target_pairs={{0,16},{4,12},{8,24},{12,4},{16,0},{20,28},{24,8},{28,20},{1,17},{... | collective-permute-start | bytes 786440 | tf_op jit(solution)/shard_map/ppermute | solution.py:28
  12.8 0.0 collective-permute-done.2.refs_2_
  12.8 0.0 collective-permute-start.3
  12.8 0.0 collective-permute-done.5.refs_3_
  12.8 2.7 %between.1 = (f32[1024,1024]{1,0:T(8,128)S(1)}, f32[1024,1024]{1,0:T(8,128)S(1)}, bf16[128,1024]{1,0:T(8,128)(2,1)S(1)}, bf16[128,1024]{1,0:T(8,128)(2,1)S(1)}, f32[32,128]{1,0:T(8,128)S(1)}) custom-call(bf16[256,1024]{1,0:T(8,128)(2,1)S(1)} %get-tuple-element.38.refs_0_, bf16[256,1024]{1,0:T(8,128)(2,1)S(1)} %get-tuple-element.51.refs_1_, ...), custom_call_target="tpu_custom_call" | custom-call | flops 9663676416 | tf_op jit(solution)/shard_map/between/pallas_call | solution.py:262
  15.5 0.6 %collective-permute-start.6 = (f32[32,128]{1,0:T(8,128)S(1)}, f32[32,128]{1,0:T(8,128)S(1)}, u32[]{:S(2)}, u32[]{:S(2)}) collective-permute-start(f32[32,128]{1,0:T(8,128)S(1)} %get-tuple-element.53.refs_0_), channel_id=1, source_target_pairs={{0,4},{4,0},{8,12},{12,8},{16,20},{20,16},{24,28},{28,24},{1,5},{5... | collective-permute-start | bytes 49160 | tf_op jit(solution)/shard_map/ppermute | solution.py:23
  16.1 1.3 %collective-permute-start.7 = (f32[32,128]{1,0:T(8,128)S(1)}, f32[32,128]{1,0:T(8,128)S(1)}, u32[]{:S(2)}, u32[]{:S(2)}) collective-permute-start(f32[32,128]{1,0:T(8,128)S(1)} %get-tuple-element.53.refs_0_), channel_id=1, source_target_pairs={{0,24},{4,28},{8,16},{12,20},{16,8},{20,12},{24,0},{28,4},{1,25},{... | collective-permute-start | bytes 49160 | tf_op jit(solution)/shard_map/ppermute | solution.py:23
  17.4 0.0 collective-permute-done.6.refs_1_
  17.4 1.3 %collective-permute-start.10 = (f32[64,128]{1,0:T(8,128)S(1)}, f32[64,128]{1,0:T(8,128)S(1)}, u32[]{:S(2)}, u32[]{:S(2)}) collective-permute-start(f32[64,128]{1,0:T(8,128)S(1)} %pack.1.refs_20_), channel_id=1, source_target_pairs={{0,8},{4,12},{8,0},{12,4},{16,24},{20,28},{24,16},{28,20},{1,9},{5... | collective-permute-start | bytes 98312 | tf_op jit(solution)/shard_map/ppermute | solution.py:23
  18.6 1.0 %collective-permute-start.11 = (f32[64,128]{1,0:T(8,128)S(1)}, f32[64,128]{1,0:T(8,128)S(1)}, u32[]{:S(2)}, u32[]{:S(2)}) collective-permute-start(f32[64,128]{1,0:T(8,128)S(1)} %pack.1.refs_20_), channel_id=1, source_target_pairs={{0,16},{4,20},{8,24},{12,28},{16,0},{20,4},{24,8},{28,12},{1,17},{... | collective-permute-start | bytes 98312 | tf_op jit(solution)/shard_map/ppermute | solution.py:23
  19.6 0.0 collective-permute-done.3.refs_1_
  19.6 0.0 collective-permute-done.4.refs_2_
  19.6 0.0 collective-permute-start.8
  19.6 1.7 %first.8 = (f32[1024,1024]{1,0:T(8,128)S(1)}, f32[1024,1024]{1,0:T(8,128)S(1)}, bf16[128,1024]{1,0:T(8,128)(2,1)S(1)}, bf16[128,1024]{1,0:T(8,128)(2,1)S(1)}) custom-call(bf16[256,1024]{1,0:T(8,128)(2,1)S(1)} %get-tuple-element.38.refs_0_, bf16[1024,128]{1,0:T(8,128)(2,1)S(1)} %collective-permute-done.3.refs_1_, ...), custom_call_target="tpu_custom_call" | custom-call | flops 6442450944 | tf_op jit(solution)/shard_map/first/pallas_call | solution.py:262
  21.3 0.0 collective-permute-done.7.refs_16_
  21.3 0.6 %collective-permute-start.9 = (f32[32,128]{1,0:T(8,128)S(1)}, f32[32,128]{1,0:T(8,128)S(1)}, u32[]{:S(2)}, u32[]{:S(2)}) collective-permute-start(f32[32,128]{1,0:T(8,128)S(1)} %collective-permute-done.7.refs_16_), channel_id=1, source_target_pairs={{0,4},{4,0},{8,12},{12,8},{16,20},{20,16},{24,28},{28,24},{1,5},{5... | collective-permute-start | bytes 49160 | tf_op jit(solution)/shard_map/ppermute | solution.py:23
  21.9 0.0 collective-permute-done.8.refs_1_
  21.9 0.9 %first.9 = (f32[1024,1024]{1,0:T(8,128)S(1)}, bf16[128,1024]{1,0:T(8,128)(2,1)S(1)}) custom-call(bf16[256,1024]{1,0:T(8,128)(2,1)S(1)} %get-tuple-element.38.refs_0_, bf16[1024,128]{1,0:T(8,128)(2,1)S(1)} %collective-permute-done.8.refs_1_), custom_call_target="tpu_custom_call" | custom-call | flops 3221225472 | tf_op jit(solution)/shard_map/first/pallas_call | solution.py:262
  22.8 0.0 collective-permute-done.9.refs_17_
  22.8 0.0 collective-permute-done.10.refs_18_
  22.8 0.0 collective-permute-done.11.refs_19_
  22.8 4.8 %second.1 = (f32[8,128]{1,0:T(8,128)}, f32[1024,128]{1,0:T(8,128)}) custom-call(f32[1024,1024]{1,0:T(8,128)S(1)} %get-tuple-element.40.refs_0_, f32[1024,1024]{1,0:T(8,128)S(1)} %get-tuple-element.43.refs_1_, f32[1024,1024]{1,0:T(8,128)S(1)} %get-tuple-element.47.refs_2_, f32[1024,1024]{1,0:T(8,128)S(1)} %get-tuple-element.56.refs_3_, ...), custom_call_target="tpu_custom_call" | custom-call | flops 25769803776 | tf_op jit(solution)/shard_map/second/pallas_call | solution.py:262
  (1 shorter events, 0.0 us)
Async XLA Ops:
  0.6 6.8 %collective-permute-start = (bf16[1024,128]{1,0:T(8,128)(2,1)}, bf16[1024,128]{1,0:T(8,128)(2,1)S(1)}, u32[]{:S(2)}, u32[]{:S(2)}) collective-permute-start(bf16[1024,128]{1,0:T(8,128)(2,1)} %x_ref.1), channel_id=1, source_target_pairs={{0,4},{4,0},{8,12},{12,8},{16,20},{20,16},{24,28},{28,24},{1,5},{5... | collective-permute-start | bytes 786440 | tf_op jit(solution)/shard_map/ppermute | solution.py:23
  1.1 7.2 %collective-permute-start.1 = (bf16[1024,128]{1,0:T(8,128)(2,1)}, bf16[1024,128]{1,0:T(8,128)(2,1)S(1)}, u32[]{:S(2)}, u32[]{:S(2)}) collective-permute-start(bf16[1024,128]{1,0:T(8,128)(2,1)} %x_ref.1), channel_id=1, source_target_pairs={{0,8},{4,20},{8,0},{12,28},{16,24},{20,4},{24,16},{28,12},{1,9},{5... | collective-permute-start | bytes 786440 | tf_op jit(solution)/shard_map/ppermute | solution.py:28
  3.7 1.0 %copy-start = (bf16[1024,128]{1,0:T(8,128)(2,1)S(1)}, bf16[1024,128]{1,0:T(8,128)(2,1)}, u32[]{:S(2)}) copy-start(bf16[1024,128]{1,0:T(8,128)(2,1)} %x_ref.1) | copy-start | bytes 786436
  4.9 1.0 %copy-start.1 = (bf16[1024,128]{1,0:T(8,128)(2,1)S(1)}, bf16[1024,128]{1,0:T(8,128)(2,1)}, u32[]{:S(2)}) copy-start(bf16[1024,128]{1,0:T(8,128)(2,1)} %x_ref.1) | copy-start | bytes 786436
  5.8 6.9 %collective-permute-start.2 = (bf16[1024,128]{1,0:T(8,128)(2,1)S(1)}, bf16[1024,128]{1,0:T(8,128)(2,1)S(1)}, u32[]{:S(2)}, u32[]{:S(2)}) collective-permute-start(bf16[1024,128]{1,0:T(8,128)(2,1)S(1)} %copy-done.1), channel_id=1, source_target_pairs={{0,16},{4,12},{8,24},{12,4},{16,0},{20,28},{24,8},{28,20},{1,17},{... | collective-permute-start | bytes 786440 | tf_op jit(solution)/shard_map/ppermute | solution.py:28
  8.4 4.4 %collective-permute-start.5 = (bf16[1024,128]{1,0:T(8,128)(2,1)S(1)}, bf16[1024,128]{1,0:T(8,128)(2,1)S(1)}, u32[]{:S(2)}, u32[]{:S(2)}) collective-permute-start(bf16[1024,128]{1,0:T(8,128)(2,1)S(1)} %collective-permute-done.1.refs_1_), channel_id=1, source_target_pairs={{0,4},{4,0},{8,12},{12,8},{16,20},{20,16},{24,28},{28,24},{1,5},{5... | collective-permute-start | bytes 786440 | tf_op jit(solution)/shard_map/ppermute | solution.py:23
  9.5 10.1 %collective-permute-start.4 = (bf16[1024,128]{1,0:T(8,128)(2,1)S(1)}, bf16[1024,128]{1,0:T(8,128)(2,1)S(1)}, u32[]{:S(2)}, u32[]{:S(2)}) collective-permute-start(bf16[1024,128]{1,0:T(8,128)(2,1)S(1)} %collective-permute-done.1.refs_1_), channel_id=1, source_target_pairs={{0,16},{4,12},{8,24},{12,4},{16,0},{20,28},{24,8},{28,20},{1,17},{... | collective-permute-start | bytes 786440 | tf_op jit(solution)/shard_map/ppermute | solution.py:28
  12.8 6.8 %collective-permute-start.3 = (bf16[1024,128]{1,0:T(8,128)(2,1)S(1)}, bf16[1024,128]{1,0:T(8,128)(2,1)S(1)}, u32[]{:S(2)}, u32[]{:S(2)}) collective-permute-start(bf16[1024,128]{1,0:T(8,128)(2,1)S(1)} %collective-permute-done.2.refs_2_), channel_id=1, source_target_pairs={{0,4},{4,0},{8,12},{12,8},{16,20},{20,16},{24,28},{28,24},{1,5},{5... | collective-permute-start | bytes 786440 | tf_op jit(solution)/shard_map/ppermute | solution.py:23
  15.5 1.8 %collective-permute-start.6 = (f32[32,128]{1,0:T(8,128)S(1)}, f32[32,128]{1,0:T(8,128)S(1)}, u32[]{:S(2)}, u32[]{:S(2)}) collective-permute-start(f32[32,128]{1,0:T(8,128)S(1)} %get-tuple-element.53.refs_0_), channel_id=1, source_target_pairs={{0,4},{4,0},{8,12},{12,8},{16,20},{20,16},{24,28},{28,24},{1,5},{5... | collective-permute-start | bytes 49160 | tf_op jit(solution)/shard_map/ppermute | solution.py:23
  16.1 5.2 %collective-permute-start.7 = (f32[32,128]{1,0:T(8,128)S(1)}, f32[32,128]{1,0:T(8,128)S(1)}, u32[]{:S(2)}, u32[]{:S(2)}) collective-permute-start(f32[32,128]{1,0:T(8,128)S(1)} %get-tuple-element.53.refs_0_), channel_id=1, source_target_pairs={{0,24},{4,28},{8,16},{12,20},{16,8},{20,12},{24,0},{28,4},{1,25},{... | collective-permute-start | bytes 49160 | tf_op jit(solution)/shard_map/ppermute | solution.py:23
  17.4 5.4 %collective-permute-start.10 = (f32[64,128]{1,0:T(8,128)S(1)}, f32[64,128]{1,0:T(8,128)S(1)}, u32[]{:S(2)}, u32[]{:S(2)}) collective-permute-start(f32[64,128]{1,0:T(8,128)S(1)} %pack.1.refs_20_), channel_id=1, source_target_pairs={{0,8},{4,12},{8,0},{12,4},{16,24},{20,28},{24,16},{28,20},{1,9},{5... | collective-permute-start | bytes 98312 | tf_op jit(solution)/shard_map/ppermute | solution.py:23
  18.6 4.2 %collective-permute-start.11 = (f32[64,128]{1,0:T(8,128)S(1)}, f32[64,128]{1,0:T(8,128)S(1)}, u32[]{:S(2)}, u32[]{:S(2)}) collective-permute-start(f32[64,128]{1,0:T(8,128)S(1)} %pack.1.refs_20_), channel_id=1, source_target_pairs={{0,16},{4,20},{8,24},{12,28},{16,0},{20,4},{24,8},{28,12},{1,17},{... | collective-permute-start | bytes 98312 | tf_op jit(solution)/shard_map/ppermute | solution.py:23
  19.6 2.3 %collective-permute-start.8 = (bf16[1024,128]{1,0:T(8,128)(2,1)S(1)}, bf16[1024,128]{1,0:T(8,128)(2,1)S(1)}, u32[]{:S(2)}, u32[]{:S(2)}) collective-permute-start(bf16[1024,128]{1,0:T(8,128)(2,1)S(1)} %collective-permute-done.4.refs_2_), channel_id=1, source_target_pairs={{0,4},{4,0},{8,12},{12,8},{16,20},{20,16},{24,28},{28,24},{1,5},{5... | collective-permute-start | bytes 786440 | tf_op jit(solution)/shard_map/ppermute | solution.py:23
  21.3 1.5 %collective-permute-start.9 = (f32[32,128]{1,0:T(8,128)S(1)}, f32[32,128]{1,0:T(8,128)S(1)}, u32[]{:S(2)}, u32[]{:S(2)}) collective-permute-start(f32[32,128]{1,0:T(8,128)S(1)} %collective-permute-done.7.refs_16_), channel_id=1, source_target_pairs={{0,4},{4,0},{8,12},{12,8},{16,20},{20,16},{24,28},{28,24},{1,5},{5... | collective-permute-start | bytes 49160 | tf_op jit(solution)/shard_map/ppermute | solution.py:23
